TPU v7x, 32 devices: a whole 2x2x4 slice. The times are simulated.
32 devices in a mesh: seq: 4 (over y, core), ctx: 8 (over z, x).
Axes of the slice: x: 2, y: 2, z: 4, core: 2. Of those that a mesh axis runs over, the one named last changes fastest.
Arguments:
- tokens: bfloat16 [4, 1024, 1536], P('seq', 'ctx'), may hold values from -6 to 6
- lengths: int32 [4], P('seq'), may hold values from 640 to 1024, as said below
- attn_gain: bfloat16 [1536], P(('seq', 'ctx')), may hold values from 0.099609375 to 1.8984375
- qkv_weight: bfloat16 [1536, 2048], P(('seq', 'ctx')), may hold values from -0.15625 to 0.15625
- qkv_bias: bfloat16 [2048], P(('seq', 'ctx')), may hold values from -3 to 3
- out_weight: bfloat16 [1536, 1536], P(('seq', 'ctx')), may hold values from -3.390625 to 3.390625
- mlp_gain: bfloat16 [1536], P(('seq', 'ctx')), may hold values from 0.099609375 to 1.8984375
- gate_weight: bfloat16 [1536, 8960], P(('seq', 'ctx')), may hold values from -0.15625 to 0.15625
- up_weight: bfloat16 [1536, 8960], P(('seq', 'ctx')), may hold values from -0.15625 to 0.15625
- down_weight: bfloat16 [8960, 1536], P(('seq', 'ctx')), may hold values from -0.0625 to 0.0625
- out_grad: bfloat16 [4, 1024, 1536], P('seq', 'ctx'), may hold values from -6 to 6
Outputs:
- output: bfloat16 [4, 1024, 1536], P('seq', 'ctx')
- input_grad: bfloat16 [4, 1024, 1536], P('seq', 'ctx')
- attn_gain_grad: float32 [1536], P(('seq', 'ctx'))
- qkv_weight_grad: float32 [1536, 2048], P(('seq', 'ctx'))
- qkv_bias_grad: float32 [1792], P(('seq', 'ctx'))
- out_weight_grad: float32 [1536, 1536], P(('seq', 'ctx'))
- mlp_gain_grad: float32 [1536], P(('seq', 'ctx'))
- gate_weight_grad: float32 [1536, 8960], P(('seq', 'ctx'))
- up_weight_grad: float32 [1536, 8960], P(('seq', 'ctx'))
- down_weight_grad: float32 [8960, 1536], P(('seq', 'ctx'))
- value_bias_grad: float32 [256], P(('seq', 'ctx'))
Inputs may be any that keep to these rules, and one draw needn't show every extreme that they name: `lengths`: each length is a multiple of 128; in every draw at least one sequence has length exactly 1024 and at least one is shorter.
All inputs are finite; a program needn't handle non-finite values.
Results may differ from a plain program's by a relative error of at most 0.025.
Values may be sent and summed in bfloat16 or wider, within the bound.
A program may use at most 512 MiB of HBM per device.

v0:
```python
import jax
import jax.numpy as jnp
from jax import lax
from jax.sharding import PartitionSpec as P

HEADS = 12
KV_HEADS = 2
HEAD = 128
QDIM = 1536
KVDIM = 256


EPSILON = 1e-06
ROPE_BASE = 1000000.0
MASKED = -1e30


def product(left, right):
    return jnp.dot(left, right, preferred_element_type=jnp.float32)


def contract_rows(left, right):
    return lax.dot_general(
        left, right, (((0,), (0,)), ((), ())), preferred_element_type=jnp.float32
    )


def contract_cols(left, right):
    return lax.dot_general(
        left, right, (((1,), (1,)), ((), ())), preferred_element_type=jnp.float32
    )


def rows_term(left, right):
    return contract_rows(left, right)


def rms_scale(values, gain):
    return values * lax.rsqrt(jnp.mean(values * values, axis=-1, keepdims=True) + EPSILON) * gain


def rotate(values, positions):
    half_width = values.shape[-1] // 2
    frequency = ROPE_BASE ** (-jnp.arange(half_width, dtype=jnp.float32) * 2.0 / values.shape[-1])
    angles = positions[:, None] * frequency[None, :]
    cosine = jnp.cos(angles)[:, None, :]
    sine_part = jnp.sin(angles)[:, None, :]
    first_half = values[..., :half_width]
    second = values[..., half_width:]
    return jnp.concatenate(
        [first_half * cosine - second * sine_part, second * cosine + first_half * sine_part],
        axis=-1,
    )


def shards(
    tokens,
    lengths,
    attn_gain,
    qkv_weight,
    qkv_bias,
    out_weight,
    mlp_gain,
    gate_weight,
    up_weight,
    down_weight,
    out_grad,
):
    group_size = HEADS // KV_HEADS
    scale_factor = HEAD ** (-0.5)
    inputs = tokens[0].astype(jnp.float32)
    local_rows = inputs.shape[0]
    seq_length = lengths[0]
    positions = lax.axis_index("ctx") * local_rows + jnp.arange(local_rows, dtype=jnp.int32)
    pos_float = positions.astype(jnp.float32)
    living = (positions < seq_length).astype(jnp.float32)[:, None]
    attention_set = (
        lax.all_gather(attn_gain, ("seq", "ctx"), axis=0, tiled=True),
        lax.all_gather(qkv_weight, ("seq", "ctx"), axis=0, tiled=True),
        lax.all_gather(qkv_bias, ("seq", "ctx"), axis=0, tiled=True),
        lax.all_gather(out_weight, ("seq", "ctx"), axis=0, tiled=True),
    )
    ffn_set = (
        lax.all_gather(mlp_gain, ("seq", "ctx"), axis=0, tiled=True),
        lax.all_gather(gate_weight, ("seq", "ctx"), axis=0, tiled=True),
        lax.all_gather(up_weight, ("seq", "ctx"), axis=0, tiled=True),
        lax.all_gather(down_weight, ("seq", "ctx"), axis=0, tiled=True),
    )
    gain_one = attention_set[0].astype(jnp.float32)
    normed_one = rms_scale(inputs, gain_one).astype(jnp.bfloat16)
    project = product(normed_one, attention_set[1]) + attention_set[2].astype(jnp.float32)
    queries = rotate(project[:, :QDIM].reshape(local_rows, HEADS, HEAD), pos_float).astype(
        jnp.bfloat16
    )
    own_keys = (
        rotate(project[:, QDIM : QDIM + KVDIM].reshape(local_rows, KV_HEADS, HEAD), pos_float)
        .reshape(local_rows, KVDIM)
        .astype(jnp.bfloat16)
    )
    own_values = project[:, QDIM + KVDIM :].astype(jnp.bfloat16)
    all_keys, all_values = (
        lax.all_gather(own_keys, "ctx", axis=0, tiled=True),
        lax.all_gather(own_values, "ctx", axis=0, tiled=True),
    )
    seq_total = all_keys.shape[0]
    key_pos = jnp.arange(seq_total, dtype=jnp.int32)
    allowed = (key_pos[None, :] <= positions[:, None]) & (key_pos[None, :] < seq_length)
    query_heads = jnp.transpose(queries, (1, 0, 2))
    head_ids = jnp.arange(HEADS, dtype=jnp.int32)

    def forward_head(head_item):
        query_one, head_index = head_item
        column = head_index // group_size * HEAD
        key_one = lax.dynamic_slice_in_dim(all_keys, column, HEAD, 1)
        value_one = lax.dynamic_slice_in_dim(all_values, column, HEAD, 1)
        scores = jnp.where(allowed, contract_cols(query_one, key_one) * scale_factor, MASKED)
        largest = jnp.max(scores, axis=1, keepdims=True)
        exponent = jnp.exp(scores - largest)
        summed = jnp.sum(exponent, axis=1, keepdims=True)
        attn_probs = (exponent / summed).astype(jnp.bfloat16)
        return (product(attn_probs, value_one), (largest + jnp.log(summed))[:, 0])

    mixed_heads, log_totals = lax.map(forward_head, (query_heads, head_ids))
    attended = jnp.transpose(mixed_heads, (1, 0, 2)).reshape(local_rows, QDIM).astype(jnp.bfloat16)
    middle = inputs + product(attended, attention_set[3])
    gain_two = ffn_set[0].astype(jnp.float32)
    normed_two = rms_scale(middle, gain_two).astype(jnp.bfloat16)
    gate_pre = product(normed_two, ffn_set[1])
    up_pre = product(normed_two, ffn_set[2])
    activated = (gate_pre * jax.nn.sigmoid(gate_pre) * up_pre).astype(jnp.bfloat16)
    output = ((middle + product(activated, ffn_set[3])) * living).astype(jnp.bfloat16)
    attention_set = (
        lax.all_gather(attn_gain, ("seq", "ctx"), axis=0, tiled=True),
        lax.all_gather(qkv_weight, ("seq", "ctx"), axis=0, tiled=True),
        lax.all_gather(qkv_bias, ("seq", "ctx"), axis=0, tiled=True),
        lax.all_gather(out_weight, ("seq", "ctx"), axis=0, tiled=True),
    )
    all_keys, all_values = (
        lax.all_gather(own_keys, "ctx", axis=0, tiled=True),
        lax.all_gather(own_values, "ctx", axis=0, tiled=True),
    )
    back_gain, back_gate, back_up, back_down = (
        lax.all_gather(mlp_gain, ("seq", "ctx"), axis=0, tiled=True),
        lax.all_gather(gate_weight, ("seq", "ctx"), axis=0, tiled=True),
        lax.all_gather(up_weight, ("seq", "ctx"), axis=0, tiled=True),
        lax.all_gather(down_weight, ("seq", "ctx"), axis=0, tiled=True),
    )
    cotangent = out_grad[0].astype(jnp.float32) * living
    cot_low = cotangent.astype(jnp.bfloat16)
    grad_act = contract_cols(cot_low, back_down)
    _, act_pull = jax.vjp(
        lambda gate_in, up_in: gate_in * jax.nn.sigmoid(gate_in) * up_in, gate_pre, up_pre
    )
    grad_gate, grad_up = act_pull(grad_act)
    grad_gate = grad_gate.astype(jnp.bfloat16)
    grad_up = grad_up.astype(jnp.bfloat16)
    grad_normed_two = contract_cols(grad_gate, back_gate) + contract_cols(grad_up, back_up)
    _, second_pull = jax.vjp(rms_scale, middle, gain_two)
    grad_mid_norm, grad_gain_two = second_pull(grad_normed_two)
    grad_middle = cotangent + grad_mid_norm
    ff_width = grad_gate.shape[1]
    both_hidden = jnp.concatenate([grad_gate, grad_up], axis=1)
    gate_up_grads = lax.psum_scatter(
        rows_term(normed_two, both_hidden), ("seq", "ctx"), scatter_dimension=0, tiled=True
    )
    grad_down_w = lax.psum_scatter(
        rows_term(activated, cot_low), ("seq", "ctx"), scatter_dimension=0, tiled=True
    )
    grad_branch = grad_middle.astype(jnp.bfloat16)
    grad_mixed = contract_cols(grad_branch, attention_set[3]).astype(jnp.bfloat16)
    grad_heads = jnp.transpose(grad_mixed.reshape(local_rows, HEADS, HEAD), (1, 0, 2))
    empty_grads = jnp.zeros((seq_total, KVDIM), jnp.float32)

    def backward_head(running, head_item):
        key_grads, value_grads = running
        query_one, grad_one, total_one, head_index = head_item
        column = head_index // group_size * HEAD
        key_one = lax.dynamic_slice_in_dim(all_keys, column, HEAD, 1)
        value_one = lax.dynamic_slice_in_dim(all_values, column, HEAD, 1)
        scores = jnp.where(allowed, contract_cols(query_one, key_one) * scale_factor, MASKED)
        attn_probs = jnp.exp(scores - total_one[:, None])
        grad_probs = contract_cols(grad_one, value_one)
        grad_scores = (
            attn_probs * (grad_probs - jnp.sum(attn_probs * grad_probs, axis=1, keepdims=True))
        ).astype(jnp.bfloat16)
        grad_query = product(grad_scores, key_one) * scale_factor
        key_part = contract_rows(grad_scores, query_one) * scale_factor
        value_part = contract_rows(attn_probs.astype(jnp.bfloat16), grad_one)
        key_grads = lax.dynamic_update_slice_in_dim(
            key_grads, lax.dynamic_slice_in_dim(key_grads, column, HEAD, 1) + key_part, column, 1
        )
        value_grads = lax.dynamic_update_slice_in_dim(
            value_grads,
            lax.dynamic_slice_in_dim(value_grads, column, HEAD, 1) + value_part,
            column,
            1,
        )
        return ((key_grads, value_grads), grad_query)

    (key_grads, value_grads), grad_queries = lax.scan(
        backward_head, (empty_grads, empty_grads), (query_heads, grad_heads, log_totals, head_ids)
    )
    own_key_grads, own_value_grads = (
        lax.psum_scatter(
            key_grads.astype(jnp.bfloat16), "ctx", scatter_dimension=0, tiled=True
        ).astype(jnp.float32),
        lax.psum_scatter(
            value_grads.astype(jnp.bfloat16), "ctx", scatter_dimension=0, tiled=True
        ).astype(jnp.float32),
    )
    grad_out_w = lax.psum_scatter(
        rows_term(attended, grad_branch), ("seq", "ctx"), scatter_dimension=0, tiled=True
    )
    _, query_pull = jax.vjp(
        lambda rows_in: rotate(rows_in, pos_float),
        jnp.zeros((local_rows, HEADS, HEAD), jnp.float32),
    )
    _, key_pull = jax.vjp(
        lambda rows_in: rotate(rows_in, pos_float),
        jnp.zeros((local_rows, KV_HEADS, HEAD), jnp.float32),
    )
    grad_q_raw = query_pull(jnp.transpose(grad_queries, (1, 0, 2)))[0].reshape(local_rows, QDIM)
    grad_k_raw = key_pull(own_key_grads.reshape(local_rows, KV_HEADS, HEAD))[0].reshape(
        local_rows, KVDIM
    )
    grad_project = jnp.concatenate([grad_q_raw, grad_k_raw, own_value_grads], axis=1).astype(
        jnp.bfloat16
    )
    grad_qkv_w = lax.psum_scatter(
        rows_term(normed_one, grad_project), ("seq", "ctx"), scatter_dimension=0, tiled=True
    )
    grad_bias = jnp.sum(grad_project.astype(jnp.float32), axis=0)
    grad_normed_one = contract_cols(grad_project, attention_set[1])
    _, first_pull = jax.vjp(rms_scale, inputs, gain_one)
    grad_in_norm, grad_gain_one = first_pull(grad_normed_one)
    grad_inputs = (grad_middle + grad_in_norm).astype(jnp.bfloat16)
    qk_width = QDIM + KVDIM
    small_sums = (
        lax.psum_scatter(grad_gain_one, ("seq", "ctx"), scatter_dimension=0, tiled=True),
        lax.psum_scatter(grad_bias[:qk_width], ("seq", "ctx"), scatter_dimension=0, tiled=True),
        lax.psum_scatter(grad_gain_two, ("seq", "ctx"), scatter_dimension=0, tiled=True),
        lax.psum_scatter(grad_bias[qk_width:], ("seq", "ctx"), scatter_dimension=0, tiled=True),
    )
    return (
        output[None],
        grad_inputs[None],
        small_sums[0],
        grad_qkv_w,
        small_sums[1],
        grad_out_w,
        small_sums[2],
        gate_up_grads[:, :ff_width],
        gate_up_grads[:, ff_width:],
        grad_down_w,
        small_sums[3],
    )


def solution(mesh):
    placed = (
        P("seq", "ctx", None),
        P("seq"),
        P(("seq", "ctx")),
        P(("seq", "ctx"), None),
        P(("seq", "ctx")),
        P(("seq", "ctx"), None),
        P(("seq", "ctx")),
        P(("seq", "ctx"), None),
        P(("seq", "ctx"), None),
        P(("seq", "ctx"), None),
        P("seq", "ctx", None),
    )
    return jax.shard_map(
        shards,
        mesh=mesh,
        in_specs=placed,
        out_specs=(
            P("seq", "ctx", None),
            P("seq", "ctx", None),
            P(("seq", "ctx")),
            P(("seq", "ctx"), None),
            P(("seq", "ctx")),
            P(("seq", "ctx"), None),
            P(("seq", "ctx")),
            P(("seq", "ctx"), None),
            P(("seq", "ctx"), None),
            P(("seq", "ctx"), None),
            P(("seq", "ctx")),
        ),
        check_vma=False,
    )
```

profile of v0, /device:TPU:0, one launch (start us, length us, event | category | flops | bytes accessed | tf_op | source)
XLA Modules:
  0.0 2658.5 jit_solution(12542236973076870578)
XLA Ops:
  13.8 42.5 %all-reduce.13 = (bf16[2048]{0:T(1024)(128)(2,1)S(1)}, bf16[1536]{0:T(1024)(128)(2,1)S(1)}, bf16[1536]{0:T(1024)(128)(2,1)S(1)}) all-reduce(bf16[2048]{0:T(1024)(128)(2,1)S(1)} %dynamic-update-slice.1, bf16[1536]{0:T(1024)(128)(2,1)S(1)} %dynamic-update-slice, ...), channel_id=1, replica_groups=mesh['seq'=4,'ctx'=8] {'seq','ctx'}, use_global_device_ids=true, to_apply=%add.5 | all-reduce | flops 5120 | bytes 20480
  58.2 25.1 all-gather.6.cloned.1.call-done
  89.4 28.5 %all_gather.40 = bf16[1024,256]{0,1:T(8,128)(2,1)S(1)} all-gather(bf16[128,256]{0,1:T(8,128)(2,1)S(1)} %bitcast.156), channel_id=1, replica_groups=mesh['seq'=4,'ctx'=8] {'ctx'}, dimensions={0}, use_global_device_ids=true | all-gather | bytes 589824 | tf_op jit(solution)/shard_map/all_gather | solution.py:102
  118.1 34.8 %all_gather.41 = bf16[1024,256]{1,0:T(8,128)(2,1)} all-gather(bf16[128,256]{1,0:T(8,128)(2,1)S(1)} %slice.61), channel_id=1, replica_groups=mesh['seq'=4,'ctx'=8] {'ctx'}, dimensions={0}, use_global_device_ids=true | all-gather | bytes 589824 | tf_op jit(solution)/shard_map/all_gather | solution.py:103
  152.9 63.3 %while.34 = (s32[]{:T(128)}, bf16[12,128,128]{1,2,0:T(8,128)(2,1)S(1)}, f32[12,128]{1,0:T(8,128)S(1)}, bf16[12,128,128]{2,1,0:T(8,128)(2,1)}, s32[12]{0:T(128)S(...) while((s32[]{:T(128)}, ...), condition=%wide.region_4.5_spmd.clone.clone, body=%wide.region_1.4_spmd.clone.sunk.clone | while | flops 68419472 | bytes 2202393 | solution.py:123
  220.4 102.0 %all-gather.12.cloned.1.call-done = bf16[1536,8960]{1,0:T(8,128)(2,1)} async-done(((bf16[48,8960]{1,0:T(8,128)(2,1)}), bf16[1536,8960]{1,0:T(8,128)(2,1)}) %all-gather.12.cloned.1.call-update) | async-done | bytes 27525136 | tf_op jit(solution)/shard_map/all_gather | solution.py:86
  322.4 14.8 fusion.83
  337.2 152.2 %all-gather.10.cloned.1.call-done = bf16[1536,8960]{1,0:T(8,128)(2,1)} async-done(((bf16[48,8960]{1,0:T(8,128)(2,1)}), bf16[1536,8960]{1,0:T(8,128)(2,1)}) %all-gather.10.cloned.1.call-update) | async-done | bytes 27525136 | tf_op jit(solution)/shard_map/all_gather | solution.py:85
  489.4 14.7 fusion.82
  504.2 152.3 %all-gather.14.cloned.1.call-done = bf16[8960,1536]{1,0:T(8,128)(2,1)} async-done(((bf16[280,1536]{1,0:T(8,128)(2,1)}), bf16[8960,1536]{1,0:T(8,128)(2,1)}) %all-gather.14.cloned.1.call-update) | async-done | bytes 27525136 | tf_op jit(solution)/shard_map/all_gather | solution.py:87
  656.5 17.8 multiply_convert_fusion.1
  674.3 15.5 fusion.84
  689.8 15.5 multiply_reduce_fusion.1
  712.6 145.3 %while.35 = (s32[]{:T(128)}, f32[1024,256]{0,1:T(8,128)}, f32[1024,256]{0,1:T(8,128)S(1)}, f32[12,128,128]{1,2,0:T(8,128)}, s32[12]{0:T(128)S(1)}, /*index=5*/bf...) while((s32[]{:T(128)}, f32[1024,256]{0,1:T(8,128)}, ...), condition=%wide.region_9.10_spmd.clone.clone, body=%wide.region_7.9_spmd.clone.sunk.clone | while | flops 169623440 | bytes 15667533 | solution.py:200
  865.3 40.0 %fusion.44 = f32[1536,17920]{1,0:T(8,128)} fusion(bf16[128,1536]{1,0:T(8,128)(2,1)} %copy-done.11, bf16[128,8960]{1,0:T(8,128)(2,1)} %get-tuple-element.473, bf16[128,8960]{1,0:T(8,128)(2,1)S(1)} %copy-done.4), kind=kOutput, calls=%fused_computation.62 | convolution fusion | flops 7055605760 | bytes 115081216 | tf_op jit(solution)/shard_map/dot_general | solution.py:23
  913.0 9.5 reduce-scatter.19.cloned.1.call-done
  924.0 63.2 %reduce-scatter.21.cloned.1.call-done = bf16[128,256]{1,0:T(8,128)(2,1)} async-done(((bf16[1024,256]{1,0:T(8,128)(2,1)}), bf16[128,256]{1,0:T(8,128)(2,1)}) %reduce-scatter.21.cloned.1.call-update) | async-done | bytes 65552
  996.3 35.0 %fusion.66 = f32[8960,1536]{1,0:T(8,128)} fusion(bf16[128,8960]{1,0:T(8,128)(2,1)S(1)} %copy-done.5, bf16[1,128,1536]{2,1,0:T(8,128)(2,1)S(1)} %copy-done.17, f32[128]{0:T(128)S(1)} %compare_convert_fusion), kind=kOutput, calls=%fused_computation.111 | convolution fusion | flops 3523805184 | bytes 57737728 | tf_op jit(solution)/shard_map/dot_general | solution.py:23
  1032.5 17.9 fusion.51
  1057.5 40.2 %all-reduce.12 = (f32[1536]{0:T(1024)S(1)}, f32[1792]{0:T(1024)S(1)}, f32[1536]{0:T(1024)S(1)}, f32[256]{0:T(256)S(1)}) all-reduce(f32[1536]{0:T(1024)S(1)} %get-tuple-element.416, f32[1792]{0:T(1024)S(1)} %bitcast.157, f32[1536]{0:T(1024)S(1)} %copy-done.31, f32[256]{0:T(256)S(1)} %slice.55), channel_id=4, replica_groups=mesh['seq'=4,'ctx'=8] {'seq','ctx'}, use_global_device_ids=true, to_apply=%region_14.15.clone | all-reduce | flops 5120 | bytes 40960
  1101.1 777.9 %reduce-scatter.17.cloned.1.call-done = f32[48,17920]{1,0:T(8,128)} async-done(((f32[1536,17920]{1,0:T(8,128)}), f32[48,17920]{1,0:T(8,128)}) %reduce-scatter.17.cloned.1.call-update) | async-done | bytes 3440656 | tf_op jit(solution)/shard_map/reduce_scatter | solution.py:163
  1882.9 138.3 %reduce-scatter.15.cloned.1.call-done = f32[48,1536]{1,0:T(8,128)} async-done(((f32[1536,1536]{1,0:T(8,128)}), f32[48,1536]{1,0:T(8,128)}) %reduce-scatter.15.cloned.1.call-update) | async-done | bytes 294928 | tf_op jit(solution)/shard_map/reduce_scatter | solution.py:211
  2021.2 161.1 %reduce-scatter.13.cloned.1.call-done = f32[48,2048]{1,0:T(8,128)} async-done(((f32[1536,2048]{1,0:T(8,128)}), f32[48,2048]{1,0:T(8,128)}) %reduce-scatter.13.cloned.1.call-update) | async-done | bytes 393232 | tf_op jit(solution)/shard_map/reduce_scatter | solution.py:229
  2182.3 469.4 %reduce-scatter.23.cloned.1.call-done = f32[280,1536]{1,0:T(8,128)} async-done(((f32[8960,1536]{1,0:T(8,128)}), f32[280,1536]{1,0:T(8,128)}) %reduce-scatter.23.cloned.1.call-update) | async-done | bytes 1720336
  (446 shorter events, 226.0 us)
Async XLA Ops:
  7.2 76.1 %all-gather.6.cloned.1.call-start = ((), (), s32[]{:S(2)}) async-start(), calls=%async_computation.6 | async-start | bytes 6488064 | tf_op jit(solution)/shard_map/all_gather | solution.py:79
  7.9 208.3 %all-gather.8.cloned.1.call-start = ((), (), s32[]{:S(2)}) async-start(), calls=%async_computation.7 | async-start | bytes 4866048 | tf_op jit(solution)/shard_map/all_gather | solution.py:81
  8.7 313.8 %all-gather.12.cloned.1.call-start = ((), (), s32[]{:S(2)}) async-start(), calls=%async_computation.9 | async-start | bytes 28385280 | tf_op jit(solution)/shard_map/all_gather | solution.py:86
  9.4 480.1 %all-gather.10.cloned.1.call-start = ((), (), s32[]{:S(2)}) async-start(), calls=%async_computation.8 | async-start | bytes 28385280 | tf_op jit(solution)/shard_map/all_gather | solution.py:85
  10.0 646.5 %all-gather.14.cloned.1.call-start = ((), (), s32[]{:S(2)}) async-start(), calls=%async_computation.10 | async-start | bytes 28385280 | tf_op jit(solution)/shard_map/all_gather | solution.py:87
  10.6 911.9 %reduce-scatter.19.cloned.1.call-start = ((), (), s32[]{:S(2)}) async-start(), calls=%async_computation.14 | async-start | bytes 589824
  56.7 32.4 %copy-start.18 = (f32[128,64]{1,0:T(8,128)}, f32[128,64]{1,0:T(8,128)S(1)}, u32[]{:S(2)}) copy-start(f32[128,64]{1,0:T(8,128)S(1)} %get-tuple-element.490) | copy-start | bytes 98308
  56.7 32.4 %copy-start.20 = (f32[128,64]{1,0:T(8,128)}, f32[128,64]{1,0:T(8,128)S(1)}, u32[]{:S(2)}) copy-start(f32[128,64]{1,0:T(8,128)S(1)} %get-tuple-element.491) | copy-start | bytes 98308
  152.9 64.1 %copy-start.9 = (bf16[1,128,1536]{2,1,0:T(8,128)(2,1)S(1)}, bf16[1,128,1536]{2,1,0:T(8,128)(2,1)}, u32[]{:S(2)}) copy-start(bf16[1,128,1536]{2,1,0:T(8,128)(2,1)} %param.15) | copy-start | bytes 1179652
  216.2 121.0 %copy-start.12 = (bf16[12,128,128]{1,2,0:T(8,128)(2,1)}, bf16[12,128,128]{1,2,0:T(8,128)(2,1)S(1)}, u32[]{:S(2)}) copy-start(bf16[12,128,128]{1,2,0:T(8,128)(2,1)S(1)} %get-tuple-element.254) | copy-start | bytes 1179652
  220.2 485.1 %copy-start = (f32[128,1536]{1,0:T(8,128)}, f32[128,1536]{1,0:T(8,128)S(1)}, u32[]{:S(2)}) copy-start(f32[128,1536]{1,0:T(8,128)S(1)} %get-tuple-element.493) | copy-start | bytes 2359300
  220.4 269.1 %copy-start.11 = (bf16[128,1536]{1,0:T(8,128)(2,1)}, bf16[128,1536]{1,0:T(8,128)(2,1)S(1)}, u32[]{:S(2)}) copy-start(bf16[128,1536]{1,0:T(8,128)(2,1)S(1)} %multiply_convert_fusion.3) | copy-start | bytes 1179652
  337.2 319.2 %copy-start.16 = (bf16[1,128,1536]{2,1,0:T(8,128)(2,1)S(1)}, bf16[1,128,1536]{2,1,0:T(8,128)(2,1)}, u32[]{:S(2)}) copy-start(bf16[1,128,1536]{2,1,0:T(8,128)(2,1)} %param.25) | copy-start | bytes 1179652
  862.2 124.9 %reduce-scatter.21.cloned.1.call-start = ((), (), s32[]{:S(2)}) async-start(), calls=%async_computation.15 | async-start | bytes 589824
  865.2 1013.7 %reduce-scatter.17.cloned.1.call-start = ((), (), s32[]{:S(2)}) async-start(), calls=%async_computation.13 | async-start | bytes 113541120 | tf_op jit(solution)/shard_map/reduce_scatter | solution.py:163
  905.3 1115.9 %reduce-scatter.15.cloned.1.call-start = ((), (), s32[]{:S(2)}) async-start(), calls=%async_computation.12 | async-start | bytes 9732096 | tf_op jit(solution)/shard_map/reduce_scatter | solution.py:211
  911.7 76.5 %copy-start.10 = (bf16[1,128,1536]{2,1,0:T(8,128)(2,1)S(1)}, bf16[1,128,1536]{2,1,0:T(8,128)(2,1)}, u32[]{:S(2)}) copy-start(bf16[1,128,1536]{2,1,0:T(8,128)(2,1)} %param.15) | copy-start | bytes 1179652
  911.7 76.5 %copy-start.30 = (f32[1536]{0:T(1024)S(1)}, f32[1536]{0:T(1024)}, u32[]{:S(2)}) copy-start(f32[1536]{0:T(1024)} %copy-done.29) | copy-start | bytes 18436
  911.7 76.5 %copy-start.33 = (f32[128]{0:T(128)S(1)}, f32[128]{0:T(128)}, u32[]{:S(2)}) copy-start(f32[128]{0:T(128)} %copy-done.32) | copy-start | bytes 1540
  911.7 1270.6 %reduce-scatter.13.cloned.1.call-start = ((), (), s32[]{:S(2)}) async-start(), calls=%async_computation.11 | async-start | bytes 12976128 | tf_op jit(solution)/shard_map/reduce_scatter | solution.py:229
  913.0 81.6 %copy-start.14 = (bf16[128,12,128]{0,2,1:T(8,128)(2,1)}, bf16[128,12,128]{0,2,1:T(8,128)(2,1)S(1)}, u32[]{:S(2)}) copy-start(bf16[128,12,128]{0,2,1:T(8,128)(2,1)S(1)} %add_convert_fusion) | copy-start | bytes 1179652
  994.6 1657.1 %reduce-scatter.23.cloned.1.call-start = ((), (), s32[]{:S(2)}) async-start(), calls=%async_computation.16 | async-start | bytes 56770560
  1050.4 49.6 %copy-start.35 = (f32[128]{0:T(128)S(1)}, f32[128]{0:T(128)}, u32[]{:S(2)}) copy-start(f32[128]{0:T(128)} %copy-done.34) | copy-start | bytes 1540
  1050.4 49.7 %copy-start.8 = (f32[128,1536]{1,0:T(8,128)S(1)}, f32[128,1536]{1,0:T(8,128)}, u32[]{:S(2)}) copy-start(f32[128,1536]{1,0:T(8,128)} %copy-done.6) | copy-start | bytes 2359300
  (23 other events, 259.8 us)
Sparse Core Ops, SparseCore 0:
  11.0 72.2 all-gather.5
  86.3 67.0 all-gather.7
  156.4 166.0 all-gather.11
  325.3 164.1 all-gather.9
  492.3 164.1 all-gather.13
  862.4 60.0 reduce-scatter.18
  926.2 60.9 reduce-scatter.20
  993.6 885.3 reduce-scatter.16
  1886.4 134.7 reduce-scatter.14
  2027.7 154.5 reduce-scatter.12
  2190.4 461.2 reduce-scatter.22
where the time goes:
time: 2670 us; the launch traced here: 2660 us
  waiting for transfers between devices  2050 us (77%)
  matrix products  299 us (11%)
  blocking collectives  146 us (5%)
  local copies, waits for them, and re-layouts  82.7 us (3%)
  loops' own time  48.7 us (2%)
    reduce_scatter x1, waiting for transfers between devices, shards(): lax.psum_scatter(rows_term(normed_two, both_hidden), ('seq', 'ctx'), scat...  778 us
    unnamed x14, waiting for transfers between devices  545 us
    reduce_scatter x1, waiting for transfers between devices, shards(): lax.psum_scatter(rows_term(normed_one, grad_project), ('seq', 'ctx'), sca...  161 us
    all_gather x1, waiting for transfers between devices, shards(): lax.all_gather(down_weight, ('seq', 'ctx'), axis=0, tiled=True)  152 us
    all_gather x1, waiting for transfers between devices, shards(): lax.all_gather(gate_weight, ('seq', 'ctx'), axis=0, tiled=True)  152 us
    reduce_scatter x1, waiting for transfers between devices, shards(): lax.psum_scatter(rows_term(attended, grad_branch), ('seq', 'ctx'), scatte...  138 us
    dot_general x28, matrix products, contract_rows(): lax.dot_general(left, right, (((0,), (0,)), ((), ())), preferred_element_...  111 us
    dot_general x41, matrix products, contract_cols(): lax.dot_general(left, right, (((1,), (1,)), ((), ())), preferred_element_...  104 us
  transfers between devices with their start and end apart: 11, of which 10 were waited for; matrix products, arithmetic and copies ran while one was open for 8% of the time, Pallas kernels for 0%

commit v1 on v0

v1 whole, which is shorter than its diff:
```python
import jax
import jax.numpy as jnp
from jax import lax
from jax.sharding import PartitionSpec as P

HEADS = 12
KV_HEADS = 2
HEAD = 128
QDIM = 1536
KVDIM = 256
GROUP = HEADS // KV_HEADS

EPSILON = 1e-06
ROPE_BASE = 1000000.0
MASKED = -1e30
SCALE = HEAD ** (-0.5)
BF = jnp.bfloat16
F32 = jnp.float32
BOTH = ("seq", "ctx")


def product(left, right):
    return jnp.dot(left, right, preferred_element_type=F32)


def contract_rows(left, right):
    return lax.dot_general(left, right, (((0,), (0,)), ((), ())), preferred_element_type=F32)


def contract_cols(left, right):
    return lax.dot_general(left, right, (((1,), (1,)), ((), ())), preferred_element_type=F32)


def inverse_rms(values):
    return lax.rsqrt(jnp.mean(values * values, axis=-1, keepdims=True) + EPSILON)


def rms_back(values, inverse, scaled_grad):
    inner = jnp.mean(scaled_grad * values, axis=-1, keepdims=True)
    return inverse * scaled_grad - values * (inverse * inverse * inverse) * inner


def rope_tables(positions):
    half = HEAD // 2
    frequency = ROPE_BASE ** (-jnp.arange(half, dtype=F32) * 2.0 / HEAD)
    angles = positions.astype(F32)[:, None] * frequency[None, :]
    return jnp.cos(angles), jnp.sin(angles)


def rotate(values, cosine, sine):
    half = HEAD // 2
    first, second = values[..., :half], values[..., half:]
    cosine, sine = cosine[:, None, :], sine[:, None, :]
    return jnp.concatenate([first * cosine - second * sine, second * cosine + first * sine], -1)


def gather(values, axes):
    return lax.all_gather(values, axes, axis=0, tiled=True)


def scatter(values, axes):
    return lax.psum_scatter(values, axes, scatter_dimension=0, tiled=True)


def shards(
    tokens,
    lengths,
    attn_gain,
    qkv_weight,
    qkv_bias,
    out_weight,
    mlp_gain,
    gate_weight,
    up_weight,
    down_weight,
    out_grad,
):
    seqs, parts = lax.axis_size("seq"), lax.axis_size("ctx")
    inputs = tokens[0].astype(F32)
    rows, width = inputs.shape
    owned, hidden = gate_weight.shape
    piece = down_weight.shape[0]
    chunk = hidden // parts
    length = lengths[0]
    positions = lax.axis_index("ctx") * rows + jnp.arange(rows, dtype=jnp.int32)
    living = (positions < length).astype(F32)[:, None]
    cosine, sine = rope_tables(positions)

    gain_one = attn_gain.astype(F32)[:, None]
    gain_two = mlp_gain.astype(F32)[:, None]
    qkv_all = gather((qkv_weight.astype(F32) * gain_one).astype(BF), BOTH)
    bias_all = gather(qkv_bias, BOTH).astype(F32)
    out_all = gather(out_weight, BOTH)

    def to_chunks(weight):
        scaled = (weight.astype(F32) * gain_two).astype(BF)
        return scaled.reshape(owned, seqs, parts, piece).transpose(2, 0, 1, 3)

    both = jnp.stack([to_chunks(gate_weight), to_chunks(up_weight)], axis=1)
    both = lax.all_to_all(both.reshape(parts, 2, owned, chunk), "ctx", 0, 0)
    both = lax.all_gather(both, "seq", axis=0)
    gate_chunk = both[:, :, 0].reshape(width, chunk)
    up_chunk = both[:, :, 1].reshape(width, chunk)
    down_chunk = gather(down_weight, "seq")
    cotangent = out_grad[0].astype(F32) * living
    cot_all = gather(cotangent.astype(BF), "ctx")

    inverse_one = inverse_rms(inputs)
    normed_one = (inputs * inverse_one).astype(BF)
    project = product(normed_one, qkv_all) + bias_all
    queries = rotate(project[:, :QDIM].reshape(rows, HEADS, HEAD), cosine, sine).astype(BF)
    own_keys = rotate(
        project[:, QDIM : QDIM + KVDIM].reshape(rows, KV_HEADS, HEAD), cosine, sine
    ).astype(BF)
    own_values = project[:, QDIM + KVDIM :].astype(BF).reshape(rows, KV_HEADS, HEAD)
    keys, values = gather(own_keys, "ctx"), gather(own_values, "ctx")
    key_pos = jnp.arange(rows * parts, dtype=jnp.int32)
    allowed = (key_pos[None, :] <= positions[:, None]) & (key_pos[None, :] < length)
    grouped = queries.reshape(rows, KV_HEADS, GROUP, HEAD)
    scores = jnp.einsum("qgha,kga->ghqk", grouped, keys, preferred_element_type=F32) * SCALE
    scores = jnp.where(allowed, scores, MASKED)
    largest = jnp.max(scores, axis=-1, keepdims=True)
    exponent = jnp.exp(scores - largest)
    summed = jnp.sum(exponent, axis=-1, keepdims=True)
    probs = exponent / summed
    probs_low = probs.astype(BF)
    attended = jnp.einsum("ghqk,kga->qgha", probs_low, values, preferred_element_type=F32)
    attended = attended.reshape(rows, QDIM).astype(BF)
    middle = inputs + product(attended, out_all)

    inverse_two = inverse_rms(middle)
    normed_two = gather((middle * inverse_two).astype(BF), "ctx")
    gate_pre = product(normed_two, gate_chunk)
    up_pre = product(normed_two, up_chunk)
    sig = jax.nn.sigmoid(gate_pre)
    activated = (gate_pre * sig * up_pre).astype(BF)
    grad_act = contract_cols(cot_all, down_chunk)
    grad_gate = (grad_act * up_pre * (sig + gate_pre * sig * (1.0 - sig))).astype(BF)
    grad_up = (grad_act * gate_pre * sig).astype(BF)
    scaled_two = contract_cols(grad_gate, gate_chunk) + contract_cols(grad_up, up_chunk)
    scaled_two = scatter(scaled_two.astype(BF), "ctx").astype(F32)
    branch = scatter(product(activated, down_chunk).astype(BF), "ctx").astype(F32)
    output = ((middle + branch) * living).astype(BF)
    grad_down = scatter(contract_rows(activated, cot_all).astype(BF), "seq").astype(F32)
    raw = jnp.stack([contract_rows(normed_two, grad_gate), contract_rows(normed_two, grad_up)], 1)
    raw = scatter(raw.astype(BF), "seq").reshape(parts, owned, 2, chunk)
    raw = lax.all_to_all(raw, "ctx", 0, 0).astype(F32)
    raw = raw.reshape(parts, owned, 2, seqs, piece).transpose(2, 1, 3, 0, 4)
    raw = raw.reshape(2, owned, hidden)
    grad_mlp_gain = jnp.sum(raw[0] * gate_weight.astype(F32) + raw[1] * up_weight.astype(F32), 1)

    grad_middle = cotangent + rms_back(middle, inverse_two, scaled_two)
    grad_branch = grad_middle.astype(BF)
    grad_out = scatter(contract_rows(attended, grad_branch).astype(BF), BOTH).astype(F32)
    grad_mixed = contract_cols(grad_branch, out_all).astype(BF)
    grad_mixed = grad_mixed.reshape(rows, KV_HEADS, GROUP, HEAD)
    grad_probs = jnp.einsum("qgha,kga->ghqk", grad_mixed, values, preferred_element_type=F32)
    inner = jnp.sum(probs * grad_probs, axis=-1, keepdims=True)
    grad_scores = (probs * (grad_probs - inner)).astype(BF)
    grad_q = jnp.einsum("ghqk,kga->qgha", grad_scores, keys, preferred_element_type=F32) * SCALE
    grad_k = jnp.einsum("ghqk,qgha->kga", grad_scores, grouped, preferred_element_type=F32) * SCALE
    grad_v = jnp.einsum("ghqk,qgha->kga", probs_low, grad_mixed, preferred_element_type=F32)
    grad_k = scatter(grad_k.astype(BF), "ctx").astype(F32)
    grad_v = scatter(grad_v.astype(BF), "ctx").astype(F32)
    grad_q = rotate(grad_q.reshape(rows, HEADS, HEAD), cosine, -sine).reshape(rows, QDIM)
    grad_k = rotate(grad_k, cosine, -sine).reshape(rows, KVDIM)
    grad_project = jnp.concatenate([grad_q, grad_k, grad_v.reshape(rows, KVDIM)], axis=1)
    grad_project = grad_project.astype(BF)
    raw_qkv = scatter(contract_rows(normed_one, grad_project).astype(BF), BOTH).astype(F32)
    grad_attn_gain = jnp.sum(raw_qkv * qkv_weight.astype(F32), axis=1)
    grad_bias = jnp.sum(grad_project.astype(F32), axis=0)
    qk_width = QDIM + KVDIM
    grad_qk_bias = scatter(grad_bias[:qk_width], BOTH)
    grad_value_bias = scatter(grad_bias[qk_width:], BOTH)
    scaled_one = contract_cols(grad_project, qkv_all)
    grad_inputs = (grad_middle + rms_back(inputs, inverse_one, scaled_one)).astype(BF)
    return (
        output[None],
        grad_inputs[None],
        grad_attn_gain,
        raw_qkv * gain_one,
        grad_qk_bias,
        grad_out,
        grad_mlp_gain,
        raw[0] * gain_two,
        raw[1] * gain_two,
        grad_down,
        grad_value_bias,
    )


def solution(mesh):
    rows, vector = P(BOTH, None), P(BOTH)
    token = P("seq", "ctx", None)
    return jax.shard_map(
        shards,
        mesh=mesh,
        in_specs=(token, P("seq"), vector, rows, vector, rows, vector, rows, rows, rows, token),
        out_specs=(token, token, vector, rows, vector, rows, vector, rows, rows, rows, vector),
        check_vma=False,
    )
```

time: 2670 us -> 1080 us (0.40)
  waiting for transfers between devices: 2050 us -> 624 us
  matrix products: 299 us -> 115 us
  blocking collectives: 146 us -> 214 us
  loops' own time: 48.7 us -> 0 us
    reduce_scatter x3 -> x6, waiting for transfers between devices: 1080 us -> 360 us  [scatter(): return lax.psum_scatter(values, axes, scatter_dimension=0, tiled=True)]
    unnamed x14 -> x16, waiting for transfers between devices: 545 us -> 124 us
    all_gather x5 -> x6, waiting for transfers between devices: 432 us -> 140 us  [the longest x5 135 us: gather(): return lax.all_gather(values, axes, axis=0, tiled=True)]
    dot_general x28 -> x5, matrix products: 111 us -> 32.1 us  [contract_rows(): lax.dot_general(left, right, (((0,), (0,)), ((), ())), preferred_element_...]
    all_to_all x0 -> x1, blocking collectives: none -> 73.6 us  [shards(): both = lax.all_to_all(both.reshape(parts, 2, owned, chunk), 'ctx', 0, 0)]
    dot_general x41 -> x5, matrix products: 104 us -> 31.9 us  [contract_cols(): lax.dot_general(left, right, (((1,), (1,)), ((), ())), preferred_element_...]
    another operation x2 -> x0, loops' own time: 48.7 us -> none  [the longest x1 24.8 us: shards(): lax.scan(backward_head, (empty_grads, empty_grads), (query_heads, grad_he...]
    dot_general x29 -> x10, matrix products: 84.4 us -> 46.5 us  [the longest x5 30.8 us: product(): return jnp.dot(left, right, preferred_element_type=F32)]
  transfers between devices with their start and end apart: 11 -> 15, of which waited for: 10 -> 12; matrix products, arithmetic and copies ran while one was open for 8% -> 14% of each run, Pallas kernels for 0% -> 0%
where the time goes in v1:
time: 1080 us; the launch traced here: 1070 us
  waiting for transfers between devices  624 us (58%)
  blocking collectives  214 us (20%)
  matrix products  115 us (11%)
  local copies, waits for them, and re-layouts  60.6 us (6%)
  other arithmetic  32.1 us (3%)
  between operations  15.6 us (1%)
    reduce_scatter x6, waiting for transfers between devices, scatter(): return lax.psum_scatter(values, axes, scatter_dimension=0, tiled=True)  360 us
    all_gather x5, waiting for transfers between devices, gather(): return lax.all_gather(values, axes, axis=0, tiled=True)  135 us
    unnamed x16, waiting for transfers between devices  124 us
    unnamed x2, blocking collectives  78.2 us
    all_to_all x1, blocking collectives, shards(): both = lax.all_to_all(both.reshape(parts, 2, owned, chunk), 'ctx', 0, 0)  73.6 us
    all_gather x2, blocking collectives, gather(): return lax.all_gather(values, axes, axis=0, tiled=True)  62.7 us
    dot_general x5, matrix products, contract_rows(): lax.dot_general(left, right, (((0,), (0,)), ((), ())), preferred_element_...  32.1 us
    dot_general x5, matrix products, contract_cols(): lax.dot_general(left, right, (((1,), (1,)), ((), ())), preferred_element_...  31.9 us
  transfers between devices with their start and end apart: 15, of which 12 were waited for; matrix products, arithmetic and copies ran while one was open for 14% of the time, Pallas kernels for 0%

profile of v1, /device:TPU:0, one launch (start us, length us, event | category | flops | bytes accessed | tf_op | source)
XLA Modules:
  0.0 1068.2 jit_solution(9029783843264816896)
XLA Ops:
  23.0 73.6 %all_to_all.10 = bf16[8,2,48,1120]{3,2,1,0:T(8,128)(2,1)} all-to-all(bf16[8,2,48,1120]{3,2,1,0:T(8,128)(2,1)S(1)} %copy.131), channel_id=1, replica_groups=mesh['seq'=4,'ctx'=8] {'ctx'}, dimensions={0} | all-to-all | bytes 3440640 | tf_op jit(solution)/shard_map/all_to_all | solution.py:100
  97.0 38.4 %all-reduce = bf16[2048]{0:T(1024)(128)(2,1)S(1)} all-reduce(bf16[2048]{0:T(1024)(128)(2,1)S(1)} %dynamic-update-slice), channel_id=1, replica_groups=mesh['seq'=4,'ctx'=8] {'seq','ctx'}, use_global_device_ids=true, to_apply=%add | all-reduce | flops 2048 | bytes 8192
  142.9 31.2 %all_gather.32 = bf16[1024,2,128]{0,2,1:T(8,128)(2,1)S(1)} all-gather(bf16[128,2,128]{0,2,1:T(8,128)(2,1)S(1)} %bitcast.192), channel_id=1, replica_groups=mesh['seq'=4,'ctx'=8] {'ctx'}, dimensions={0}, use_global_device_ids=true | all-gather | bytes 589824 | tf_op jit(solution)/shard_map/all_gather | solution.py:58
  174.1 31.5 %all_gather.33 = bf16[1024,2,128]{2,0,1:T(8,128)(2,1)S(1)} all-gather(bf16[128,2,128]{2,0,1:T(8,128)(2,1)S(1)} %pad_maximum_fusion.5), channel_id=1, replica_groups=mesh['seq'=4,'ctx'=8] {'ctx'}, dimensions={0}, use_global_device_ids=true | all-gather | bytes 589824 | tf_op jit(solution)/shard_map/all_gather | solution.py:58
  224.8 6.6 fusion.69
  231.4 56.5 %all-gather.12.cloned.1.call-done = bf16[1024,1536]{1,0:T(8,128)(2,1)} async-done(((bf16[128,1536]{1,0:T(8,128)(2,1)}), bf16[1024,1536]{1,0:T(8,128)(2,1)}) %all-gather.12.cloned.1.call-update) | async-done | bytes 3145744 | tf_op jit(solution)/shard_map/all_gather | solution.py:58
  287.9 9.1 fusion.77
  302.9 15.3 %all-gather.14.cloned.1.call-done = bf16[1120,1536]{1,0:T(8,128)(2,1)} async-done(((bf16[280,1536]{1,0:T(8,128)(2,1)}), bf16[1120,1536]{1,0:T(8,128)(2,1)}) %all-gather.14.cloned.1.call-update) | async-done | bytes 3440656 | tf_op jit(solution)/shard_map/all_gather | solution.py:58
  318.2 63.1 %all-gather.16.cloned.1.call-done = bf16[1024,1536]{1,0:T(8,128)(2,1)} async-done(((bf16[128,1536]{1,0:T(8,128)(2,1)}), bf16[1024,1536]{1,0:T(8,128)(2,1)}) %all-gather.16.cloned.1.call-update) | async-done | bytes 3145744 | tf_op jit(solution)/shard_map/all_gather | solution.py:58
  381.3 12.3 %multiply_convert_fusion = (bf16[1024,1120]{0,1:T(8,128)(2,1)S(1)}, bf16[1024,1120]{0,1:T(8,128)(2,1)S(1)}, bf16[1024,1120]{0,1:T(8,128)(2,1)}) fusion(f32[1024,1120]{0,1:T(8,128)} %fusion.77, f32[1024,1120]{0,1:T(8,128)} %fusion.78, bf16[1024,1536]{1,0:T(8,128)(2,1)} %all-gather.16.cloned.1.call-done, bf16[1120,1536]{1,0:T(8,128)(2,1)} %all-gather.14.cloned.1.call-done), kind=kOutput, calls=%fused_computation.18 | convolution fusion | flops 3540418560 | bytes 22642688 | tf_op jit(solution)/shard_map/dot_general | solution.py:31
  404.0 8.7 convolution_convert_fusion.5
  412.7 64.3 %reduce-scatter.15.cloned.1.call-done = bf16[128,1536]{1,0:T(8,128)(2,1)} async-done(((bf16[1024,1536]{1,0:T(8,128)(2,1)}), bf16[128,1536]{1,0:T(8,128)(2,1)}) %reduce-scatter.15.cloned.1.call-update) | async-done | bytes 393232 | tf_op jit(solution)/shard_map/reduce_scatter | solution.py:62
  478.2 76.1 %reduce-scatter.13.cloned.1.call-done = bf16[128,1536]{1,0:T(8,128)(2,1)} async-done(((bf16[1024,1536]{1,0:T(8,128)(2,1)}), bf16[128,1536]{1,0:T(8,128)(2,1)}) %reduce-scatter.13.cloned.1.call-update) | async-done | bytes 393232 | tf_op jit(solution)/shard_map/reduce_scatter | solution.py:62
  569.0 8.1 fusion.2
  584.1 6.5 fusion.1
  594.1 10.2 copy.171
  604.3 8.1 convolution_convert_fusion.2
  620.7 9.5 reduce-scatter.17.cloned.1.call-done
  632.3 63.0 %reduce-scatter.25.cloned.1.call-done = bf16[128,256]{1,0:T(8,128)(2,1)} async-done(((bf16[1024,256]{1,0:T(8,128)(2,1)}), bf16[128,256]{1,0:T(8,128)(2,1)}) %reduce-scatter.25.cloned.1.call-update) | async-done | bytes 65552
  700.9 59.6 %reduce-scatter.27.cloned.1.call-done = bf16[384,2240]{1,0:T(8,128)(2,1)} async-done(((bf16[1536,2240]{1,0:T(8,128)(2,1)}), bf16[384,2240]{1,0:T(8,128)(2,1)}) %reduce-scatter.27.cloned.1.call-update) | async-done | bytes 1720336
  773.9 29.0 %reduce-scatter.23.cloned.1.call-done = bf16[280,1536]{1,0:T(8,128)(2,1)} async-done(((bf16[1120,1536]{1,0:T(8,128)(2,1)}), bf16[280,1536]{1,0:T(8,128)(2,1)}) %reduce-scatter.23.cloned.1.call-update) | async-done | bytes 860176 | tf_op jit(solution)/shard_map/reduce_scatter | solution.py:62
  805.7 39.8 %all-reduce.3 = (f32[1792]{0:T(1024)S(1)}, f32[256]{0:T(256)S(1)}) all-reduce(f32[1792]{0:T(1024)S(1)} %bitcast.193, f32[256]{0:T(256)S(1)} %slice.89), channel_id=8, replica_groups=mesh['seq'=4,'ctx'=8] {'seq','ctx'}, use_global_device_ids=true, to_apply=%region_14.15.clone | all-reduce | flops 2048 | bytes 16384
  853.0 62.5 %reduce-scatter.21.cloned.1.call-done = bf16[48,1536]{1,0:T(8,128)(2,1)} async-done(((bf16[1536,1536]{1,0:T(8,128)(2,1)}), bf16[48,1536]{1,0:T(8,128)(2,1)}) %reduce-scatter.21.cloned.1.call-update) | async-done | bytes 147472 | tf_op jit(solution)/shard_map/reduce_scatter | solution.py:62
  917.1 118.2 %reduce-scatter.19.cloned.1.call-done = bf16[48,2048]{1,0:T(8,128)(2,1)} async-done(((bf16[1536,2048]{1,0:T(8,128)(2,1)}), bf16[48,2048]{1,0:T(8,128)(2,1)}) %reduce-scatter.19.cloned.1.call-update) | async-done | bytes 196624 | tf_op jit(solution)/shard_map/reduce_scatter | solution.py:62
  (186 shorter events, 151.4 us)
Async XLA Ops:
  7.2 130.4 %all-gather.8.cloned.1.call-start = ((), (), s32[]{:S(2)}) async-start(), calls=%async_computation.10 | async-start | bytes 6488064 | tf_op jit(solution)/shard_map/all_gather | solution.py:58
  10.1 203.8 %all-gather.10.cloned.1.call-start = ((), (), s32[]{:S(2)}) async-start(), calls=%async_computation.11 | async-start | bytes 4866048 | tf_op jit(solution)/shard_map/all_gather | solution.py:58
  10.9 214.0 %all-gather.18.cloned.1.call-start = ((), (), s32[]{:S(2)}) async-start(), calls=%async_computation.21 | async-start | bytes 8847360 | tf_op jit(solution)/shard_map/all_gather | solution.py:101
  23.0 73.8 %copy-start.26 = (bf16[64]{0:T(256)(128)(2,1)S(1)}, bf16[64]{0:T(256)(128)(2,1)}, u32[]{:S(2)}) copy-start(bf16[64]{0:T(256)(128)(2,1)} %param.15) | copy-start | bytes 388
  23.0 114.1 %copy-start = (bf16[1,128,1536]{2,1,0:T(8,128)(2,1)S(1)}, bf16[1,128,1536]{2,1,0:T(8,128)(2,1)}, u32[]{:S(2)}) copy-start(bf16[1,128,1536]{2,1,0:T(8,128)(2,1)} %param.11) | copy-start | bytes 1179652
  96.7 191.3 %all-gather.12.cloned.1.call-start = ((), (), s32[]{:S(2)}) async-start(), calls=%async_computation.12 | async-start | bytes 3538944 | tf_op jit(solution)/shard_map/all_gather | solution.py:58
  142.3 68.1 %copy-start.10 = (bf16[128,12,64]{2,0,1:T(8,128)(2,1)}, bf16[128,12,64]{2,0,1:T(8,128)(2,1)S(1)}, u32[]{:S(2)}) copy-start(bf16[128,12,64]{2,0,1:T(8,128)(2,1)S(1)} %copy.127) | copy-start | bytes 589828
  142.6 67.9 %copy-start.12 = (bf16[128,12,64]{2,0,1:T(8,128)(2,1)}, bf16[128,12,64]{2,0,1:T(8,128)(2,1)S(1)}, u32[]{:S(2)}) copy-start(bf16[128,12,64]{2,0,1:T(8,128)(2,1)S(1)} %copy.126) | copy-start | bytes 589828
  218.3 100.0 %all-gather.14.cloned.1.call-start = ((), (), s32[]{:S(2)}) async-start(), calls=%async_computation.13 | async-start | bytes 4300800 | tf_op jit(solution)/shard_map/all_gather | solution.py:58
  218.8 162.5 %all-gather.16.cloned.1.call-start = ((), (), s32[]{:S(2)}) async-start(), calls=%async_computation.15 | async-start | bytes 3538944 | tf_op jit(solution)/shard_map/all_gather | solution.py:58
  219.8 257.2 %reduce-scatter.15.cloned.1.call-start = ((), (), s32[]{:S(2)}) async-start(), calls=%async_computation.16 | async-start | bytes 3538944 | tf_op jit(solution)/shard_map/reduce_scatter | solution.py:62
  287.9 9.1 copy-start.3
  287.9 9.1 copy-start.25
  381.3 12.3 %copy-start.5 = (bf16[4,8,1,48,1120]{4,3,2,1,0:T(8,128)(2,1)S(1)}, bf16[4,8,1,48,1120]{4,3,2,1,0:T(8,128)(2,1)}, u32[]{:S(2)}) copy-start(bf16[4,8,1,48,1120]{4,3,2,1,0:T(8,128)(2,1)} %get-tuple-element.16) | copy-start | bytes 10321924
  403.8 150.5 %reduce-scatter.13.cloned.1.call-start = ((), (), s32[]{:S(2)}) async-start(), calls=%async_computation.14 | async-start | bytes 3538944 | tf_op jit(solution)/shard_map/reduce_scatter | solution.py:62
  412.7 217.5 %reduce-scatter.17.cloned.1.call-start = ((), (), s32[]{:S(2)}) async-start(), calls=%async_computation.17 | async-start | bytes 589824 | tf_op jit(solution)/shard_map/reduce_scatter | solution.py:62
  556.6 8.5 copy-start.1
  568.9 126.4 %reduce-scatter.25.cloned.1.call-start = ((), (), s32[]{:S(2)}) async-start(), calls=%async_computation.22 | async-start | bytes 589824
  583.8 176.7 %reduce-scatter.27.cloned.1.call-start = ((), (), s32[]{:S(2)}) async-start(), calls=%async_computation.23 | async-start | bytes 8847360
  604.3 198.7 %reduce-scatter.23.cloned.1.call-start = ((), (), s32[]{:S(2)}) async-start(), calls=%async_computation.20 | async-start | bytes 4300800 | tf_op jit(solution)/shard_map/reduce_scatter | solution.py:62
  612.4 303.1 %reduce-scatter.21.cloned.1.call-start = ((), (), s32[]{:S(2)}) async-start(), calls=%async_computation.19 | async-start | bytes 4866048 | tf_op jit(solution)/shard_map/reduce_scatter | solution.py:62
  617.3 418.1 %reduce-scatter.19.cloned.1.call-start = ((), (), s32[]{:S(2)}) async-start(), calls=%async_computation.18 | async-start | bytes 6488064 | tf_op jit(solution)/shard_map/reduce_scatter | solution.py:62
  768.4 269.4 %all-to-all-start.1 = ((bf16[8,48,2,1120]{3,1,2,0:T(8,128)(2,1)}), bf16[8,48,2,1120]{3,1,2,0:T(8,128)(2,1)S(1)}, u32[]{:S(2)}, u32[]{:S(2)}) async-start(bf16[8,48,2,1120]{3,1,2,0:T(8,128)(2,1)} %copy.144), calls=%async_computation.6 | async-start | bytes 3538944 | tf_op jit(solution)/shard_map/all_to_all | solution.py:147
  846.7 188.7 %copy-start.24 = (f32[48]{0:T(128)S(1)}, f32[48]{0:T(128)}, u32[]{:S(2)}) copy-start(f32[48]{0:T(128)} %copy-done.23) | copy-start | bytes 580
  (22 other events, 90.4 us)
Sparse Core Ops, SparseCore 0:
  11.6 87.9 all-gather.7
  102.6 69.9 all-gather.9
  174.1 50.6 all-gather.17
  227.4 60.4 all-gather.11
  289.3 28.8 all-gather.13
  320.8 60.4 all-gather.15
  403.9 73.0 reduce-scatter.14
  480.6 73.6 reduce-scatter.12
  569.0 61.1 reduce-scatter.16
  634.3 60.8 reduce-scatter.24
  697.8 62.6 reduce-scatter.26
  763.1 39.8 reduce-scatter.22
  808.4 107.0 reduce-scatter.20
  921.9 113.3 reduce-scatter.18

commit v2 on v1

--- a/solution.py
+++ b/solution.py
@@ -1,6 +1,11 @@
+import functools
+
 import jax
 import jax.numpy as jnp
+import numpy as np
 from jax import lax
+from jax.experimental import pallas as pl
+from jax.experimental.pallas import tpu as pltpu
 from jax.sharding import PartitionSpec as P
 
 HEADS = 12
@@ -19,6 +24,10 @@
 BOTH = ("seq", "ctx")
 
 
+DMA = pltpu.SemaphoreType.DMA
+MESH = pl.DeviceIdType.MESH
+
+
 def product(left, right):
     return jnp.dot(left, right, preferred_element_type=F32)
 
@@ -62,7 +71,7 @@
     return lax.psum_scatter(values, axes, scatter_dimension=0, tiled=True)
 
 
-def shards(
+def plain_shards(
     tokens,
     lengths,
     attn_gain,
@@ -189,11 +198,809 @@
     )
 
 
+class Place:
+    def __init__(self, n):
+        self.n = n
+        self.s, self.c = lax.axis_index("seq"), lax.axis_index("ctx")
+        self.me = self.s * n + self.c
+        self.core = lax.rem(self.s, 2)
+        self.sib = self.s + 1 - 2 * self.core
+        self.far = lax.rem(self.s + 2, 4)
+        half = self.c // 2
+        self.pos = half + lax.rem(self.c, 2) * (n - 1 - 2 * half)
+        self.nxt, self.prv = self.at(1), self.at(-1)
+    def at(self, offset):
+        p = lax.rem(self.pos + offset + 2 * self.n, self.n)
+        return 2 * p + (p // (self.n // 2)) * (2 * self.n - 1 - 4 * p)
+
+def send(src, dst, ssem, rsem, seq, ctx):
+    copy = pltpu.make_async_remote_copy(src, dst, ssem, rsem, device_id=(seq, ctx), device_id_type=MESH)
+    copy.start()
+
+def arrived(dst, rsem, place):
+    pltpu.make_async_remote_copy(dst, dst, rsem, rsem, device_id=(place.s, place.c), device_id_type=MESH).wait_recv()
+
+def sent(src, ssem, place):
+    pltpu.make_async_remote_copy(src, src, ssem, ssem, device_id=(place.s, place.c), device_id_type=MESH).wait_send()
+
+def enter(place, whole_group=True):
+    barrier = pltpu.get_barrier_semaphore()
+    def greet(d, z):
+        pl.semaphore_signal(barrier, inc=1, device_id=(place.s, lax.rem(place.c + d, place.n)), device_id_type=MESH)
+        return z
+    lax.fori_loop(1, place.n, greet, 0)
+    pl.semaphore_signal(barrier, inc=1, device_id=(place.sib, place.c), device_id_type=MESH)
+    pl.semaphore_signal(barrier, inc=1, device_id=(place.far, place.c), device_id_type=MESH)
+    pl.semaphore_wait(barrier, place.n + 1)
+
+
+def rope(values, table_c, table_s):
+    return values * table_c + pltpu.roll(values, HEAD // 2, 1) * table_s
+
+def forward_kernel(n, length_ref, x_ref, og_ref, qkv, outw, gu, down, tables,
+                   gu_all, down_all, cot_all, n2_all, qkv_all, out_all, kv_all, q_out, att_out, mid_out,
+                   qkv_v, out_v, xh_v, cot_v, kv_v, q_v, att_v, mid_v, n2_v, tab_v,
+                   local, save, q_recv, q_ring, q_sib, q_far, o_recv, o_ring, o_far, o_sib,
+                   g_recv, g_send, g_far, g_sib, d_recv, d_far, d_sib, c_recv, c_ring,
+                   k_recv, k_ring, n_recv, n_ring):
+    pc = Place(n)
+    me, s, c = pc.me, pc.s, pc.c
+    rows, width = x_ref.shape
+    owned, piece = gu.shape[2], down.shape[0]
+    ohalf, chalf = outw.shape[1] // 2, width // 2
+    steps = n - 1
+    length = length_ref[0]
+    ways = ((0, -1, pc.nxt), (1, 1, pc.prv))
+
+    def o_slot(i, f): return out_v.at[i, :, pl.ds(f * ohalf, ohalf)]
+    def half_of(ref, f): return ref.at[:, pl.ds(f * chalf, chalf)]
+    def c_slot(i, f): return cot_all.at[i, :, pl.ds(f * chalf, chalf)]
+    def n_slot(i, f): return n2_all.at[i, :, pl.ds(f * chalf, chalf)]
+    def k_slot(i, f): return kv_v.at[i, :, pl.ds(f * KVDIM, KVDIM)]
+    def g_slot(i): return gu_all.at[:, pl.ds(pl.multiple_of(i * owned, owned), owned), :]
+    def d_slot(i): return down_all.at[pl.ds(pl.multiple_of(i * piece, piece), piece), :]
+
+    enter(pc)
+    first = pl.multiple_of(c * rows, rows)
+    lc = [pltpu.make_async_copy(a, b, local.at[i]) for i, (a, b) in enumerate((
+        (qkv, qkv_v.at[me]), (outw, out_v.at[me]), (gu.at[c], g_slot(me)), (down, d_slot(s)),
+        (tables.at[:, pl.ds(first, rows), :], tab_v)))]
+    for copy in lc: copy.start()
+    send(qkv, qkv_v.at[me], q_far.at[0], q_recv.at[me], pc.far, c)
+    send(qkv, qkv_v.at[me], q_sib.at[me], q_recv.at[me], pc.sib, c)
+    for f, _, to in ways:
+        src = outw.at[:, pl.ds(f * ohalf, ohalf)]
+        send(src, o_slot(me, f), o_ring.at[f, c], o_recv.at[f, me], s, to)
+        send(src, o_slot(me, f), o_far.at[f, c], o_recv.at[f, me], pc.far, c)
+        send(src, o_slot(me, f), o_sib.at[f, me], o_recv.at[f, me], pc.sib, c)
+    send(down, d_slot(s), d_far.at[0], d_recv.at[s], pc.far, c)
+    send(down, d_slot(s), d_sib.at[s], d_recv.at[s], pc.sib, c)
+    x = x_ref[...].astype(F32)
+    xh_v[...] = (x * inverse_rms(x)).astype(BF)
+    slot_pos = c * rows + lax.broadcasted_iota(jnp.int32, (rows, width), 0)
+    cot_v[...] = jnp.where(slot_pos < length, og_ref[...].astype(F32), 0.0).astype(BF)
+    other = pc.far * n + c
+    arrived(qkv_v.at[other], q_recv.at[other], pc)
+    lc[0].wait()
+    for f, _, to in ways:
+        i = (2 * f + pc.core) * n + c
+        send(qkv_v.at[i], qkv_v.at[i], q_ring.at[f, c], q_recv.at[i], s, to)
+    send(qkv_v.at[other], qkv_v.at[other], q_sib.at[other], q_recv.at[other], pc.sib, c)
+
+    def turn_q(t, z):
+        for f, sign, to in ways:
+            src = pc.at(sign * (t + 1))
+            i = (2 * f + pc.core) * n + src
+            arrived(qkv_v.at[i], q_recv.at[i], pc)
+            @pl.when(t < steps - 1)
+            def _():
+                send(qkv_v.at[i], qkv_v.at[i], q_ring.at[f, src], q_recv.at[i], s, to)
+            send(qkv_v.at[i], qkv_v.at[i], q_sib.at[i], q_recv.at[i], pc.sib, c)
+        for f, sign, to in ways:
+            src = pc.at(sign * (t + 1))
+            j = s * n + src
+            arrived(o_slot(j, f), o_recv.at[f, j], pc)
+            @pl.when(t < steps - 1)
+            def _():
+                send(o_slot(j, f), o_slot(j, f), o_ring.at[f, src], o_recv.at[f, j], s, to)
+            send(o_slot(j, f), o_slot(j, f), o_far.at[f, src], o_recv.at[f, j], pc.far, c)
+            send(o_slot(j, f), o_slot(j, f), o_sib.at[f, j], o_recv.at[f, j], pc.sib, c)
+        return z
+    lax.fori_loop(0, steps, turn_q, 0)
+
+    own_cot = pltpu.make_async_copy(cot_v, cot_all.at[c], local.at[5])
+    own_cot.start()
+    for f, _, to in ways:
+        send(half_of(cot_v, f), c_slot(c, f), c_ring.at[f, c], c_recv.at[f, c], s, to)
+    def feed(d, z):
+        to = lax.rem(c + d, n)
+        send(gu.at[to], g_slot(me), g_send.at[to], g_recv.at[me], s, to)
+        return z
+    lax.fori_loop(1, n, feed, 0)
+    send(gu.at[c], g_slot(me), g_far.at[c], g_recv.at[me], pc.far, c)
+    send(gu.at[c], g_slot(me), g_sib.at[me], g_recv.at[me], pc.sib, c)
+
+    def rest_q(t, z):
+        for plane in range(2):
+            i = (2 * plane + 1 - pc.core) * n + t
+            arrived(qkv_v.at[i], q_recv.at[i], pc)
+        return z
+    lax.fori_loop(0, n, rest_q, 0)
+    lc[4].wait()
+    owners = 4 * n
+    qk = QDIM + 2 * KVDIM
+    tile = 256
+    xh = xh_v[...]
+    def bias_of(j):
+        parts = []
+        for k in range(tile // 128):
+            d = 2 * (2 * j + k)
+            row = qkv_v[d, 0:1, qk : qk + 128] + qkv_v[d + 1, 0:1, qk : qk + 128]
+            parts.append(row)
+        return jnp.concatenate(parts, 1).astype(F32)
+    def project(j):
+        w = qkv_v[:, :, pl.ds(pl.multiple_of(j * tile, tile), tile)].reshape(owners * owned, tile)
+        return product(xh, w) + bias_of(j)
+    tc, ts = tab_v[0], tab_v[1]
+    keys = project(QDIM // tile)
+    for k in range(KV_HEADS):
+        kv_v[c, :, k * HEAD : (k + 1) * HEAD] = rope(keys[:, k * HEAD : (k + 1) * HEAD], tc, ts).astype(BF)
+    kv_v[c, :, KVDIM:] = project(QDIM // tile + 1).astype(BF)
+    for f, _, to in ways:
+        send(k_slot(c, f), k_slot(c, f), k_ring.at[f, c], k_recv.at[f, c], s, to)
+    def queries(j, z):
+        p = project(j)
+        for k in range(tile // HEAD):
+            q_v[j * (tile // HEAD) + k] = rope(p[:, k * HEAD : (k + 1) * HEAD], tc, ts).astype(BF)
+        return z
+    lax.fori_loop(0, QDIM // tile, queries, 0)
+    q_save = pltpu.make_async_copy(qkv_v, qkv_all, save.at[0])
+    q_save.start()
+    q_save2 = pltpu.make_async_copy(q_v, q_out, save.at[1])
+    q_save2.start()
+    def turn_k(t, z):
+        for f, sign, to in ways:
+            src = pc.at(sign * (t + 1))
+            arrived(k_slot(src, f), k_recv.at[f, src], pc)
+            @pl.when(t < steps - 1)
+            def _():
+                send(k_slot(src, f), k_slot(src, f), k_ring.at[f, src], k_recv.at[f, src], s, to)
+        for f, sign, to in ways:
+            src = pc.at(sign * (t + 1))
+            arrived(c_slot(src, f), c_recv.at[f, src], pc)
+            @pl.when(t < steps - 1)
+            def _():
+                send(c_slot(src, f), c_slot(src, f), c_ring.at[f, src], c_recv.at[f, src], s, to)
+        return z
+    lax.fori_loop(0, steps, turn_k, 0)
+    kv_save = pltpu.make_async_copy(kv_v, kv_all, save.at[2])
+    kv_save.start()
+
+    total = n * rows
+    at_row = c * rows + lax.broadcasted_iota(jnp.int32, (rows, total), 0)
+    at_col = lax.broadcasted_iota(jnp.int32, (rows, total), 1)
+    allowed = (at_col <= at_row) & (at_col < length)
+    def head(h, z):
+        col = pl.multiple_of(h // GROUP * HEAD, HEAD)
+        key = kv_v[:, :, pl.ds(col, HEAD)].reshape(total, HEAD)
+        val = kv_v[:, :, pl.ds(pl.multiple_of(KVDIM + col, HEAD), HEAD)].reshape(total, HEAD)
+        scores = jnp.where(allowed, contract_cols(q_v[h], key) * SCALE, MASKED)
+        e = jnp.exp(scores - jnp.max(scores, axis=1, keepdims=True))
+        probs = (e / jnp.sum(e, axis=1, keepdims=True)).astype(BF)
+        att_v[:, pl.ds(pl.multiple_of(h * HEAD, HEAD), HEAD)] = product(probs, val).astype(BF)
+        return z
+    lax.fori_loop(0, HEADS, head, 0)
+    a_save = pltpu.make_async_copy(att_v, att_out, save.at[3])
+    a_save.start()
+
+    def across_o(t, z):
+        for f, sign, to in ways:
+            j = pc.far * n + pc.at(sign * t)
+            arrived(o_slot(j, f), o_recv.at[f, j], pc)
+            send(o_slot(j, f), o_slot(j, f), o_sib.at[f, j], o_recv.at[f, j], pc.sib, c)
+        return z
+    lax.fori_loop(0, n, across_o, 0)
+    def rest_o(t, z):
+        for plane in range(2):
+            i = (2 * plane + 1 - pc.core) * n + t
+            for f in range(2): arrived(o_slot(i, f), o_recv.at[f, i], pc)
+        return z
+    lax.fori_loop(0, n, rest_o, 0)
+    lc[1].wait()
+    o_save = pltpu.make_async_copy(out_v, out_all, save.at[4])
+    o_save.start()
+    att = att_v[...]
+    def mix(j, z):
+        cols = pl.ds(pl.multiple_of(j * tile, tile), tile)
+        w = out_v[:, :, cols].reshape(owners * owned, tile)
+        mid_v[:, cols] = x_ref[:, cols].astype(F32) + product(att, w)
+        return z
+    lax.fori_loop(0, width // tile, mix, 0)
+    m_save = pltpu.make_async_copy(mid_v, mid_out, save.at[5])
+    m_save.start()
+    mid = mid_v[...]
+    n2_v[...] = (mid * inverse_rms(mid)).astype(BF)
+    own_n2 = pltpu.make_async_copy(n2_v, n2_all.at[c], local.at[6])
+    own_n2.start()
+    for f, _, to in ways:
+        send(half_of(n2_v, f), n_slot(c, f), n_ring.at[f, c], n_recv.at[f, c], s, to)
+    def turn_n(t, z):
+        for f, sign, to in ways:
+            src = pc.at(sign * (t + 1))
+            arrived(n_slot(src, f), n_recv.at[f, src], pc)
+            @pl.when(t < steps - 1)
+            def _():
+                send(n_slot(src, f), n_slot(src, f), n_ring.at[f, src], n_recv.at[f, src], s, to)
+        src = lax.rem(c + n - 1 - t, n)
+        k = s * n + src
+        arrived(g_slot(k), g_recv.at[k], pc)
+        send(g_slot(k), g_slot(k), g_far.at[src], g_recv.at[k], pc.far, c)
+        send(g_slot(k), g_slot(k), g_sib.at[k], g_recv.at[k], pc.sib, c)
+        return z
+    lax.fori_loop(0, steps, turn_n, 0)
+    arrived(d_slot(pc.far), d_recv.at[pc.far], pc)
+    send(d_slot(pc.far), d_slot(pc.far), d_sib.at[pc.far], d_recv.at[pc.far], pc.sib, c)
+    def across(t, z):
+        k = pc.far * n + lax.rem(c + n - t, n)
+        arrived(g_slot(k), g_recv.at[k], pc)
+        send(g_slot(k), g_slot(k), g_sib.at[k], g_recv.at[k], pc.sib, c)
+        return z
+    lax.fori_loop(0, n, across, 0)
+    for plane in range(2):
+        row = 2 * plane + 1 - pc.core
+        arrived(d_slot(row), d_recv.at[row], pc)
+        def rest(t, z):
+            i = row * n + t
+            arrived(g_slot(i), g_recv.at[i], pc)
+            return z
+        lax.fori_loop(0, n, rest, 0)
+    for copy in lc[2:4] + [own_cot, own_n2, q_save, q_save2, kv_save, a_save, o_save, m_save]: copy.wait()
+    o_any = outw.at[:, pl.ds(0, ohalf)]
+    sent(qkv, q_far.at[0], pc)
+    sent(down, d_far.at[0], pc)
+    for plane in range(2):
+        row = 2 * plane + pc.core
+        sent(down, d_sib.at[row], pc)
+        def tail(t, z):
+            i = row * n + t
+            sent(qkv, q_sib.at[i], pc)
+            sent(gu.at[0], g_sib.at[i], pc)
+            for f in range(2): sent(o_any, o_sib.at[f, i], pc)
+            return z
+        lax.fori_loop(0, n, tail, 0)
+    def tail2(t, z):
+        src = lax.rem(c + t, n)
+        sent(gu.at[0], g_far.at[src], pc)
+        for f in range(2): sent(o_any, o_far.at[f, src], pc)
+        @pl.when(t > 0)
+        def _():
+            sent(gu.at[0], g_send.at[src], pc)
+        return z
+    lax.fori_loop(0, n, tail2, 0)
+    def tail3(t, z):
+        for f, sign, _ in ways:
+            src = pc.at(sign * t)
+            sent(qkv, q_ring.at[f, src], pc)
+            sent(o_any, o_ring.at[f, src], pc)
+            sent(half_of(cot_v, f), c_ring.at[f, src], pc)
+            sent(half_of(n2_v, f), n_ring.at[f, src], pc)
+            sent(k_slot(c, f), k_ring.at[f, src], pc)
+        return z
+    lax.fori_loop(0, steps, tail3, 0)
+
+def forward_call(n, length, x, og, qkv, outw, gu, down, tables):
+    N = 4 * n
+    owned, piece = gu.shape[2], down.shape[0]
+    rows, width = x.shape
+    S = jax.ShapeDtypeStruct
+    shapes = [S((2, N * owned, gu.shape[3]), BF), S((4 * piece, width), BF), S((n, rows, width), BF),
+              S((n, rows, width), BF), S((N,) + qkv.shape, BF), S((N,) + outw.shape, BF),
+              S((n, rows, 2 * KVDIM), BF), S((HEADS, rows, HEAD), BF), S((rows, QDIM), BF), S((rows, width), F32)]
+    anys = pl.BlockSpec(memory_space=pl.ANY)
+    vmem = pl.BlockSpec(memory_space=pltpu.VMEM)
+    V = pltpu.VMEM
+    scratch = [V((N,) + qkv.shape, BF), V((N,) + outw.shape, BF), V((rows, width), BF), V((rows, width), BF),
+               V((n, rows, 2 * KVDIM), BF), V((HEADS, rows, HEAD), BF), V((rows, QDIM), BF), V((rows, width), F32),
+               V((rows, width), BF), V((2, rows, HEAD), F32),
+               DMA((7,)), DMA((6,)), DMA((N,)), DMA((2, n)), DMA((N,)), DMA((1,)), DMA((2, N)), DMA((2, n)), DMA((2, n)), DMA((2, N)),
+               DMA((N,)), DMA((n,)), DMA((n,)), DMA((N,)), DMA((4,)), DMA((1,)), DMA((4,)), DMA((2, n)), DMA((2, n)),
+               DMA((2, n)), DMA((2, n)), DMA((2, n)), DMA((2, n))]
+    return pl.pallas_call(
+        functools.partial(forward_kernel, n),
+        out_shape=shapes,
+        in_specs=[pl.BlockSpec(memory_space=pltpu.SMEM), vmem, vmem] + [anys] * 5,
+        out_specs=[anys] * len(shapes),
+        scratch_shapes=scratch,
+        compiler_params=pltpu.CompilerParams(collective_id=0, has_side_effects=True, vmem_limit_bytes=48 * 2**20),
+    )(length, x, og, qkv, outw, gu, down, tables)
+
+
+def ffn_kernel(n, gu_all, down_all, cot_all, n2_all, u_own, o_own, graw, ddown,
+               gu_v, down_v, cot_v, n2_v, act_v, gg_v, gp_v, ub, ob, dgu_v, dd_v, r0g, r1g, r0d, r1d,
+               load, rows_in, u_recv, u_send, o_recv, o_send, gs0, gr0, gs1, gr1, gs2, gr2, ds0, dr0, ds1, dr1):
+    pc = Place(n)
+    s, c = pc.s, pc.c
+    _, rows, width = n2_all.shape
+    chunk = gu_all.shape[2]
+    half = rows // 2
+    steps = n - 1
+    ways = ((0, -1, pc.nxt), (1, 1, pc.prv))
+    weights = [pltpu.make_async_copy(gu_all, gu_v, load.at[0]), pltpu.make_async_copy(down_all, down_v, load.at[1])]
+    def fetch(t, z):
+        for f, sign, _ in ways:
+            q = pc.at(sign * (t + 1))
+            part = pl.ds(f * half, half)
+            pltpu.make_async_copy(n2_all.at[q, part, :], n2_v.at[t, part, :], rows_in.at[0, f, t]).start()
+            pltpu.make_async_copy(cot_all.at[q, part, :], cot_v.at[t, part, :], rows_in.at[1, f, t]).start()
+        return z
+    lax.fori_loop(0, 1, fetch, 0)
+    for w in weights: w.start()
+    lax.fori_loop(1, n, fetch, 0)
+    enter(pc)
+    for w in weights: w.wait()
+    tile = 384
+    def slot(buf, f, i): return buf.at[f, i]
+    def step(t, z):
+        for f in range(2):
+            part = pl.ds(f * half, half)
+            pltpu.make_async_copy(n2_all.at[0, part, :], n2_v.at[t, part, :], rows_in.at[0, f, t]).wait()
+            pltpu.make_async_copy(cot_all.at[0, part, :], cot_v.at[t, part, :], rows_in.at[1, f, t]).wait()
+        def hidden(j, y):
+            cols = pl.ds(pl.multiple_of(j * tile, tile), tile)
+            gate = product(n2_v[t], gu_v[0, :, cols])
+            up = product(n2_v[t], gu_v[1, :, cols])
+            grad = contract_cols(cot_v[t], down_v[cols, :])
+            sig = jax.nn.sigmoid(gate)
+            gs = gate * sig
+            act_v[t, :, cols] = (gs * up).astype(BF)
+            gg_v[t, :, cols] = (grad * up * (sig + gs * (1.0 - sig))).astype(BF)
+            gp_v[t, :, cols] = (grad * gs).astype(BF)
+            return y
+        lax.fori_loop(0, chunk // tile, hidden, 0)
+        here = lax.rem(t + n - 1, n)
+        @pl.when(t > 0)
+        def _():
+            for f in range(2): arrived(slot(ub, f, here), u_recv.at[f, here], pc)
+        def wide(j, y):
+            cols = pl.ds(pl.multiple_of(j * tile, tile), tile)
+            u = contract_cols(gg_v[t], gu_v[0, cols, :]) + contract_cols(gp_v[t], gu_v[1, cols, :])
+            o = product(act_v[t], down_v[:, cols])
+            for f in range(2):
+                mine = slice(f * half, (f + 1) * half)
+                before = jnp.where(t > 0, ub[f, here, :, cols].astype(F32), 0.0)
+                both = u[mine] + before
+                ub[f, here, :, cols] = both.astype(BF)
+                u_own[mine, cols] = both
+                ob[f, t, :, cols] = o[mine].astype(BF)
+            return y
+        lax.fori_loop(0, width // tile, wide, 0)
+        @pl.when(t < steps)
+        def _():
+            for f, _, to in ways:
+                send(slot(ub, f, here), slot(ub, f, t), u_send.at[f, t], u_recv.at[f, t], s, to)
+        return z
+    lax.fori_loop(0, n, step, 0)
+
+    all_rows = n * rows
+    plane = gu_all.shape[1] // 4
+    piece = down_all.shape[0] // 4
+    owned = plane // n
+    core, y = pc.core, s // 2
+    def turn_o(t):
+        for f, _, to in ways:
+            if t == 0:
+                send(ob.at[f, 0], ob.at[f, n], o_send.at[f, 0], o_recv.at[f, 0], s, to)
+            else:
+                here = n + t - 1
+                arrived(ob.at[f, here], o_recv.at[f, t - 1], pc)
+                ob[f, here] = (ob[f, here].astype(F32) + ob[f, t].astype(F32)).astype(BF)
+                if t < steps:
+                    send(ob.at[f, here], ob.at[f, n + t], o_send.at[f, t], o_recv.at[f, t], s, to)
+                else:
+                    o_own[f * half : (f + 1) * half, :] = ob[f, here].astype(F32)
+    def cols_of(j): return pl.ds(j * tile, tile)
+    wide_pieces = [(0, j, a) for j in range(chunk // tile) for a in range(2)]
+    down_pieces = [(1, j, 0) for j in range(width // tile)]
+    def compute(p):
+        kind, j, a = p
+        if kind == 0:
+            lhs, rhs = n2_v[...].reshape(all_rows, width), (gg_v, gp_v)[a]
+            grad = contract_rows(lhs, rhs[:, :, cols_of(j)].reshape(all_rows, tile))
+            dgu_v[a, :, :, :, cols_of(j)] = grad.astype(BF).reshape(2, 2, plane, tile)
+            send(dgu_v.at[a, :, 1 - core, :, cols_of(j)], r0g.at[a, :, :, cols_of(j)],
+                 gs0.at[a, j], gr0.at[a, j], pc.sib, c)
+        else:
+            grad = contract_rows(act_v[...].reshape(all_rows, chunk), cot_v[:, :, cols_of(j)].reshape(all_rows, tile))
+            dd_v[:, :, :, cols_of(j)] = grad.astype(BF).reshape(2, 2, piece, tile)
+            send(dd_v.at[:, 1 - core, :, cols_of(j)], r0d.at[:, :, cols_of(j)], ds0.at[j], dr0.at[j], pc.sib, c)
+    def add_core(p):
+        kind, j, a = p
+        cols = cols_of(j)
+        if kind == 0:
+            arrived(r0g.at[a, :, :, cols], gr0.at[a, j], pc)
+            for k in range(2):
+                r0g[a, k, :, cols] = (r0g[a, k, :, cols].astype(F32) + dgu_v[a, k, core, :, cols].astype(F32)).astype(BF)
+            send(r0g.at[a, 1 - y, :, cols], r1g.at[a, :, cols], gs1.at[a, j], gr1.at[a, j], pc.far, c)
+        else:
+            arrived(r0d.at[:, :, cols], dr0.at[j], pc)
+            for k in range(2):
+                r0d[k, :, cols] = (r0d[k, :, cols].astype(F32) + dd_v[k, core, :, cols].astype(F32)).astype(BF)
+            send(r0d.at[1 - y, :, cols], r1d.at[:, cols], ds1.at[j], dr1.at[j], pc.far, c)
+    def add_far(p):
+        kind, j, a = p
+        cols = cols_of(j)
+        if kind == 0:
+            arrived(r1g.at[a, :, cols], gr1.at[a, j], pc)
+            r1g[a, :, cols] = (r1g[a, :, cols].astype(F32) + r0g[a, y, :, cols].astype(F32)).astype(BF)
+            def hand(d, z):
+                to = lax.rem(c + d, n)
+                src = r1g.at[a, pl.ds(pl.multiple_of(to * owned, owned), owned), cols]
+                send(src, graw.at[c, a, :, cols], gs2.at[a, j, to], gr2.at[a, j, c], s, to)
+                return z
+            lax.fori_loop(1, n, hand, 0)
+            mine = r1g.at[a, pl.ds(pl.multiple_of(c * owned, owned), owned), cols]
+            pltpu.make_async_copy(mine, graw.at[c, a, :, cols], gs2.at[a, j, c]).start()
+        else:
+            arrived(r1d.at[:, cols], dr1.at[j], pc)
+            ddown[:, cols] = r1d[:, cols].astype(F32) + r0d[y, :, cols].astype(F32)
+    order = wide_pieces + down_pieces
+    turn_o(0)
+    for i, p in enumerate(order):
+        compute(p)
+        if i: add_core(order[i - 1])
+        if i in (3, 7): turn_o(1 + i // 4)
+    add_core(order[-1])
+    for i, p in enumerate(order):
+        add_far(p)
+        if i < steps - 2: turn_o(3 + i)
+    for kind, j, a in order:
+        cols = cols_of(j)
+        if kind == 0:
+            sent(r0g.at[a, :, :, cols], gs0.at[a, j], pc)
+            sent(r1g.at[a, :, cols], gs1.at[a, j], pc)
+            block = graw.at[c, a, :, cols]
+            def last(d, z):
+                k = lax.rem(c + d, n)
+                arrived(graw.at[k, a, :, cols], gr2.at[a, j, k], pc)
+                sent(block, gs2.at[a, j, k], pc)
+                return z
+            lax.fori_loop(1, n, last, 0)
+            pltpu.make_async_copy(r1g.at[a, pl.ds(0, owned), cols], block, gs2.at[a, j, c]).wait()
+        else:
+            sent(r0d.at[:, :, cols], ds0.at[j], pc)
+            sent(r1d.at[:, cols], ds1.at[j], pc)
+    def tail(t, z):
+        for f in range(2):
+            sent(ub.at[f, 0], u_send.at[f, t], pc)
+            sent(ob.at[f, 0], o_send.at[f, t], pc)
+        return z
+    lax.fori_loop(0, steps, tail, 0)
+
+def ffn_call(n, gu_all, down_all, cot_all, n2_all):
+    S, V = jax.ShapeDtypeStruct, pltpu.VMEM
+    _, rows, width = n2_all.shape
+    chunk = gu_all.shape[2]
+    half = rows // 2
+    plane, piece = gu_all.shape[1] // 4, down_all.shape[0] // 4
+    a, b = chunk // 384, width // 384
+    anys = pl.BlockSpec(memory_space=pl.ANY)
+    vmem = pl.BlockSpec(memory_space=pltpu.VMEM)
+    return pl.pallas_call(
+        functools.partial(ffn_kernel, n),
+        out_shape=[S((rows, width), F32), S((rows, width), F32), S((n, 2, plane // n, chunk), BF), S((piece, width), F32)],
+        in_specs=[anys] * 4,
+        out_specs=[vmem, vmem, anys, vmem],
+        scratch_shapes=[V(gu_all.shape, BF), V(down_all.shape, BF), V(cot_all.shape, BF), V(n2_all.shape, BF)]
+        + [V((n, rows, chunk), BF)] * 3 + [V((2, n, half, width), BF), V((2, 2 * n, half, width), BF)]
+        + [V((2, 2, 2, plane, chunk), BF), V((2, 2, piece, width), BF), V((2, 2, plane, chunk), BF), V((2, plane, chunk), BF),
+           V((2, piece, width), BF), V((piece, width), BF)]
+        + [DMA((2,)), DMA((2, 2, n)), DMA((2, n)), DMA((2, n)), DMA((2, n)), DMA((2, n))]
+        + [DMA((2, a))] * 4 + [DMA((2, a, n))] * 2 + [DMA((b,))] * 4,
+        compiler_params=pltpu.CompilerParams(collective_id=1, has_side_effects=True, vmem_limit_bytes=62 * 2**20),
+    )(gu_all, down_all, cot_all, n2_all)
+
+
+def add_low(left, right):
+    return (left.astype(F32) + right.astype(F32)).astype(BF)
+
+class Reduce:
+    def __init__(self, pc, far_first, p, r0, r1, r2, r3, ss, rs, i):
+        self.pc, self.far_first, self.p = pc, far_first, p
+        self.r0, self.r1, self.r2, self.r3, self.ss, self.rs, self.i = r0, r1, r2, r3, ss, rs, i
+        self.y, self.x, self.z = pc.s // 2, lax.rem(pc.c, 2), pc.c // 2
+        self.xp = pc.c + 1 - 2 * self.x
+    def go(self, k, src, dst, seq, ctx):
+        send(src, dst, self.ss.at[self.i, k], self.rs.at[self.i, k], seq, ctx)
+    def come(self, k, dst):
+        arrived(dst, self.rs.at[self.i, k], self.pc)
+    def stage0(self):
+        pc = self.pc
+        self.go(0, self.p.at[:, 1 - pc.core], self.r0, pc.sib, pc.c)
+    def stage1(self):
+        pc, r0 = self.pc, self.r0
+        self.come(0, r0)
+        r0[...] = add_low(r0[...], self.p[:, pc.core])
+        if self.far_first: self.go(1, r0.at[1 - self.y], self.r1, pc.far, pc.c)
+        else: self.go(1, r0.at[:, :, 1 - self.x], self.r1, pc.s, self.xp)
+    def stage2(self):
+        pc, r0, r1 = self.pc, self.r0, self.r1
+        self.come(1, r1)
+        if self.far_first:
+            r1[...] = add_low(r1[...], r0[self.y])
+            self.go(2, r1.at[:, 1 - self.x], self.r2, pc.s, self.xp)
+        else:
+            r1[...] = add_low(r1[...], r0[:, :, self.x])
+            self.go(2, r1.at[1 - self.y], self.r2, pc.far, pc.c)
+    def stage3(self):
+        pc, r1, r2, n = self.pc, self.r1, self.r2, self.pc.n
+        self.come(2, r2)
+        r2[...] = add_low(r2[...], r1[:, self.x] if self.far_first else r1[self.y])
+        def hand(d, w):
+            to = lax.rem(self.z + d, n // 2)
+            send(r2.at[to], self.r3.at[self.z], self.ss.at[self.i, 2 + d], self.rs.at[self.i, 2 + d], pc.s, 2 * to + self.x)
+            return w
+        lax.fori_loop(1, n // 2, hand, 0)
+    def stage4(self):
+        n = self.pc.n
+        total = self.r2[self.z].astype(F32)
+        for d in range(1, n // 2):
+            src = lax.rem(self.z + n // 2 - d, n // 2)
+            arrived(self.r3.at[src], self.rs.at[self.i, 2 + d], self.pc)
+            total = total + self.r3[src].astype(F32)
+        return total
+    def finish(self):
+        sent(self.r0, self.ss.at[self.i, 0], self.pc)
+        sent(self.r1, self.ss.at[self.i, 1], self.pc)
+        sent(self.r2, self.ss.at[self.i, 2], self.pc)
+        for d in range(1, self.pc.n // 2):
+            sent(self.r2.at[0], self.ss.at[self.i, 2 + d], self.pc)
+
+def backward_kernel(n, length_ref, x_ref, og_ref, mid_ref, u_ref, o_ref, att_ref, q_ref, kv_ref, qkv_ref, out_ref, tables,
+                    y_out, dx_out, dout_out, dqkv_out,
+                    tab_v, gm_v, gb_v, dm_v, gp_v, p_v, gs_v, dkv_v, kx, kz, *rest):
+    pieces = 6
+    bufs, (local, kxs, kxr, kzs, kzr, ss, rs) = rest[: 5 * pieces], rest[5 * pieces :]
+    pc = Place(n)
+    s, c = pc.s, pc.c
+    rows, width = x_ref.shape
+    total = n * rows
+    length = length_ref[0]
+    x, z = lax.rem(c, 2), c // 2
+    xp = c + 1 - 2 * x
+    red = [Reduce(pc, i % 2 == 0, *bufs[5 * i : 5 * i + 5], ss, rs, i) for i in range(pieces)]
+    tab = pltpu.make_async_copy(tables.at[:, pl.ds(pl.multiple_of(c * rows, rows), rows), :], tab_v, local.at[0])
+    tab.start()
+    enter(pc)
+    pos = c * rows + lax.broadcasted_iota(jnp.int32, (rows, width), 0)
+    live = pos < length
+    mid = mid_ref[...]
+    gm = jnp.where(live, og_ref[...].astype(F32), 0.0) + rms_back(mid, inverse_rms(mid), u_ref[...])
+    gm_v[...] = gm
+    gb_v[...] = gm.astype(BF)
+    y_out[...] = jnp.where(live, mid + o_ref[...], 0.0).astype(BF)
+    owned = out_ref.shape[1]
+    owners = 4 * n
+    def mix(j, w):
+        weight = out_ref[pl.ds(j * 8, 8)].reshape(8 * owned, width)
+        r = contract_cols(gb_v[...], weight).astype(BF)
+        for k in range(8 * owned // HEAD):
+            dm_v[j * (8 * owned // HEAD) + k] = r[:, k * HEAD : (k + 1) * HEAD]
+        return w
+    lax.fori_loop(0, owners // 8, mix, 0)
+    gb = gb_v[...]
+    for i in range(2):
+        w = width // 2
+        grad = contract_rows(att_ref[...], gb[:, i * w : (i + 1) * w])
+        red[i].p[...] = grad.astype(BF).reshape(red[i].p.shape)
+        red[i].stage0()
+    tab.wait()
+    tc, ts = tab_v[0], tab_v[1]
+
+    at_row = c * rows + lax.broadcasted_iota(jnp.int32, (rows, total), 0)
+    at_col = lax.broadcasted_iota(jnp.int32, (rows, total), 1)
+    allowed = (at_col <= at_row) & (at_col < length)
+    def group(g):
+        key = kv_ref[:, :, g * HEAD : (g + 1) * HEAD].reshape(total, HEAD)
+        val = kv_ref[:, :, KVDIM + g * HEAD : KVDIM + (g + 1) * HEAD].reshape(total, HEAD)
+        def head(i, w):
+            h = g * GROUP + i
+            part = pl.ds(pl.multiple_of(i * rows, rows), rows)
+            scores = jnp.where(allowed, contract_cols(q_ref[h], key) * SCALE, MASKED)
+            e = jnp.exp(scores - jnp.max(scores, axis=1, keepdims=True))
+            probs = e / jnp.sum(e, axis=1, keepdims=True)
+            gprobs = contract_cols(dm_v[h], val)
+            inner = jnp.sum(probs * gprobs, axis=1, keepdims=True)
+            gs = (probs * (gprobs - inner)).astype(BF)
+            p_v[part, :] = probs.astype(BF)
+            gs_v[part, :] = gs
+            dq = product(gs, key) * SCALE
+            gp_v[:, pl.ds(pl.multiple_of(h * HEAD, HEAD), HEAD)] = (dq * tc - pltpu.roll(dq, HEAD // 2, 1) * ts).astype(BF)
+            return w
+        lax.fori_loop(0, GROUP, head, 0)
+        mine = slice(g * GROUP, (g + 1) * GROUP)
+        dk = contract_rows(gs_v[...], q_ref[mine].reshape(GROUP * rows, HEAD)) * SCALE
+        dv = contract_rows(p_v[...], dm_v[mine].reshape(GROUP * rows, HEAD))
+        lanes = slice(g * 2 * HEAD, g * 2 * HEAD + 2 * HEAD)
+        dkv_v[:, :, :, lanes] = jnp.concatenate([dk, dv], 1).astype(BF).reshape(n // 2, 2, rows, 2 * HEAD)
+        send(dkv_v.at[:, 1 - x, :, lanes], kx.at[:, :, lanes], kxs.at[g], kxr.at[g], s, xp)
+    def kv_x(g):
+        lanes = slice(g * 2 * HEAD, g * 2 * HEAD + 2 * HEAD)
+        arrived(kx.at[:, :, lanes], kxr.at[g], pc)
+        kx[:, :, lanes] = add_low(kx[:, :, lanes], dkv_v[:, x, :, lanes])
+        for d in range(1, n // 2):
+            to = lax.rem(z + d, n // 2)
+            send(kx.at[to, :, lanes], kz.at[z, :, lanes], kzs.at[g, d], kzr.at[g, d], s, 2 * to + x)
+    def kv_z(g):
+        lanes = slice(g * 2 * HEAD, g * 2 * HEAD + 2 * HEAD)
+        sumkv = kx[z, :, lanes].astype(F32)
+        for d in range(1, n // 2):
+            src = lax.rem(z + n // 2 - d, n // 2)
+            arrived(kz.at[src, :, lanes], kzr.at[g, d], pc)
+            sumkv = sumkv + kz[src, :, lanes].astype(F32)
+        dk, dv = sumkv[:, :HEAD], sumkv[:, HEAD:]
+        k0, v0 = QDIM + g * HEAD, QDIM + KVDIM + g * HEAD
+        gp_v[:, k0 : k0 + HEAD] = (dk * tc - pltpu.roll(dk, HEAD // 2, 1) * ts).astype(BF)
+        gp_v[:, v0 : v0 + HEAD] = dv.astype(BF)
+    xin = x_ref[...].astype(F32)
+    inverse = inverse_rms(xin)
+    def joint(i, first, w):
+        xh = (x_ref[...].astype(F32) * inverse).astype(BF)
+        grad = contract_rows(xh, gp_v[:, first : first + w]).astype(BF)
+        shape = red[i].p.shape[:-1] + (w,)
+        red[i].p[..., :w] = grad.reshape(shape)
+    group(0)
+    red[0].stage1(); red[1].stage1()
+    group(1)
+    kv_x(0)
+    red[0].stage2(); red[1].stage2()
+    third = QDIM // 3
+    for i in range(3):
+        joint(2 + i, i * third, third)
+        red[2 + i].stage0()
+        if i == 0: kv_x(1)
+    red[0].stage3(); red[1].stage3()
+    red[2].stage1(); red[3].stage1(); red[4].stage1()
+    kv_z(0); kv_z(1)
+    joint(5, QDIM, 2 * KVDIM)
+    sums = jnp.sum(gp_v[...].astype(F32), axis=0, keepdims=True)
+    p5 = red[5].p
+    qk_width = QDIM + KVDIM
+    at = lax.broadcasted_iota(jnp.int32, (owned, HEAD), 0)
+    for d in range(owners):
+        tiles = (qk_width // owners * d // HEAD, qk_width // owners * d // HEAD + 1, (qk_width + KVDIM // owners * d) // HEAD)
+        part = jnp.zeros((owned, HEAD), F32)
+        for k, t in enumerate(tiles):
+            part = jnp.where(at == k, sums[:, t * HEAD : t * HEAD + HEAD], part)
+        plane = d // n
+        p5[plane // 2, plane % 2, d % n // 2, d % 2, :, 2 * KVDIM :] = part.astype(BF)
+    red[5].stage0()
+    red[2].stage2(); red[3].stage2(); red[4].stage2()
+    red[5].stage1()
+    qk = QDIM + 2 * KVDIM
+    gp = gp_v[...]
+    def back(j, w):
+        weight = qkv_ref[pl.ds(j * 8, 8), :, :qk].reshape(8 * owned, qk)
+        cols = pl.ds(pl.multiple_of(j * 8 * owned, 8 * owned), 8 * owned)
+        dx_out[:, cols] = contract_cols(gp, weight)
+        return w
+    lax.fori_loop(0, owners // 8, back, 0)
+    red[2].stage3(); red[3].stage3(); red[4].stage3()
+    red[5].stage2()
+    dx_out[...] = gm_v[...] + rms_back(x_ref[...].astype(F32), inverse, dx_out[...])
+    for i in range(2):
+        dout_out[:, i * (width // 2) : (i + 1) * (width // 2)] = red[i].stage4()
+    red[5].stage3()
+    for i in range(3):
+        dqkv_out[:, i * third : (i + 1) * third] = red[2 + i].stage4()
+    dqkv_out[:, QDIM:] = red[5].stage4()
+    for r in red: r.finish()
+    for g in range(2):
+        lanes = slice(g * 2 * HEAD, g * 2 * HEAD + 2 * HEAD)
+        sent(kx.at[:, :, lanes], kxs.at[g], pc)
+        for d in range(1, n // 2): sent(kx.at[0, :, lanes], kzs.at[g, d], pc)
+
+def backward_call(n, length, x, og, mid, u, o, att, q, kv, qkv_all, out_all, tables):
+    S, V = jax.ShapeDtypeStruct, pltpu.VMEM
+    rows, width = x.shape
+    owned = qkv_all.shape[1]
+    anys = pl.BlockSpec(memory_space=pl.ANY)
+    vmem = pl.BlockSpec(memory_space=pltpu.VMEM)
+    m = n // 2
+    scratch = [V((2, rows, HEAD), F32), V((rows, width), F32), V((rows, width), BF), V((HEADS, rows, HEAD), BF),
+               V((rows, QDIM + 2 * KVDIM), BF), V((GROUP * rows, n * rows), BF), V((GROUP * rows, n * rows), BF),
+               V((m, 2, rows, 2 * KVDIM), BF), V((m, rows, 2 * KVDIM), BF), V((m, rows, 2 * KVDIM), BF)]
+    for i, w in enumerate((width // 2, width // 2, QDIM // 3, QDIM // 3, QDIM // 3, 2 * KVDIM + HEAD)):
+        one = (m, 2, owned, w) if i % 2 == 0 else (2, m, owned, w)
+        scratch += [V((2, 2, m, 2, owned, w), BF), V((2, m, 2, owned, w), BF), V(one, BF), V((m, owned, w), BF), V((m, owned, w), BF)]
+    scratch += [DMA((1,)), DMA((2,)), DMA((2,)), DMA((2, m)), DMA((2, m)), DMA((6, 2 + m)), DMA((6, 2 + m))]
+    return pl.pallas_call(
+        functools.partial(backward_kernel, n),
+        out_shape=[S((rows, width), BF), S((rows, width), F32), S((owned, width), F32), S((owned, qkv_all.shape[2]), F32)],
+        in_specs=[pl.BlockSpec(memory_space=pltpu.SMEM)] + [vmem] * 10 + [anys],
+        out_specs=[vmem] * 4,
+        scratch_shapes=scratch,
+        compiler_params=pltpu.CompilerParams(collective_id=2, has_side_effects=True, vmem_limit_bytes=62 * 2**20),
+    )(length, x, og, mid, u, o, att, q, kv, qkv_all, out_all, tables)
+
+
+def kernel_shards(
+    tokens,
+    lengths,
+    attn_gain,
+    qkv_weight,
+    qkv_bias,
+    out_weight,
+    mlp_gain,
+    gate_weight,
+    up_weight,
+    down_weight,
+    out_grad,
+):
+    seqs, parts = lax.axis_size("seq"), lax.axis_size("ctx")
+    rows, width = tokens.shape[1:]
+    owned, hidden = gate_weight.shape
+    piece = down_weight.shape[0]
+    padded = -(-piece // 32) * 32
+    owners = seqs * parts
+    me = lax.axis_index("seq") * parts + lax.axis_index("ctx")
+    gain_one = attn_gain.astype(F32)[:, None]
+    gain_two = mlp_gain.astype(F32)[:, None]
+    half = HEAD // 2
+    frequency = np.float32(ROPE_BASE) ** (-np.arange(half, dtype=np.float32) * np.float32(2.0 / HEAD))
+    angles = np.arange(rows * parts, dtype=np.float32)[:, None] * frequency.astype(np.float32)[None, :]
+    cosine, sine = np.cos(angles), np.sin(angles)
+    tables = jnp.asarray(np.stack([np.concatenate([cosine, cosine], 1), np.concatenate([-sine, sine], 1)]), F32)
+    share = qkv_bias.shape[0]
+    extra = jnp.zeros((owned, HEAD), BF)
+    extra = lax.dynamic_update_slice(extra, qkv_bias[None], (0, lax.rem(me, HEAD // share) * share))
+    joint = jnp.concatenate([(qkv_weight.astype(F32) * gain_one).astype(BF), extra], axis=1)
+
+    def to_chunks(weight):
+        scaled = (weight.astype(F32) * gain_two).astype(BF).reshape(owned, seqs, parts, piece)
+        scaled = jnp.pad(scaled, ((0, 0), (0, 0), (0, 0), (0, padded - piece)))
+        return scaled.transpose(2, 0, 1, 3).reshape(parts, owned, seqs * padded)
+
+    both = jnp.stack([to_chunks(gate_weight), to_chunks(up_weight)], axis=1)
+    down = jnp.pad(down_weight, ((0, padded - piece), (0, 0)))
+    x, og = tokens[0], out_grad[0]
+    gu_all, down_all, cot_all, n2_all, qkv_all, out_all, kv_all, q, att, mid = forward_call(
+        parts, lengths, x, og, joint, out_weight, both, down, tables
+    )
+    u, o, raw, grad_down = ffn_call(parts, gu_all, down_all, cot_all, n2_all)
+    output, grad_inputs, grad_out, raw_qkv = backward_call(
+        parts, lengths, x, og, mid, u, o, att, q, kv_all, qkv_all, out_all, tables
+    )
+    raw = raw.reshape(parts, 2, owned, seqs, padded)[..., :piece].transpose(1, 2, 3, 0, 4)
+    raw = raw.reshape(2, owned, hidden).astype(F32)
+    grad_mlp_gain = jnp.sum(raw[0] * gate_weight.astype(F32) + raw[1] * up_weight.astype(F32), 1)
+    qk = QDIM + 2 * KVDIM
+    bias_rows, raw_qkv = raw_qkv[:3, qk:], raw_qkv[:, :qk]
+    grad_attn_gain = jnp.sum(raw_qkv * qkv_weight.astype(F32), axis=1)
+    per, per_value = (QDIM + KVDIM) // owners, KVDIM // owners
+    grad_qk_bias = lax.dynamic_slice_in_dim(bias_rows[:2].reshape(2 * HEAD), lax.rem(per * me, HEAD), per)
+    grad_value_bias = lax.dynamic_slice_in_dim(bias_rows[2], lax.rem(per_value * me, HEAD), per_value)
+    return (
+        output[None],
+        grad_inputs.astype(BF)[None],
+        grad_attn_gain,
+        raw_qkv * gain_one,
+        grad_qk_bias,
+        grad_out,
+        grad_mlp_gain,
+        raw[0] * gain_two,
+        raw[1] * gain_two,
+        grad_down[:piece],
+        grad_value_bias,
+    )
+
+
 def solution(mesh):
+    seqs, parts = mesh.shape["seq"], mesh.shape["ctx"]
+    tiled = seqs == 4 and parts == 8 and 1536 // (seqs * parts) % 16 == 0
     rows, vector = P(BOTH, None), P(BOTH)
     token = P("seq", "ctx", None)
     return jax.shard_map(
-        shards,
+        kernel_shards if tiled else plain_shards,
         mesh=mesh,
         in_specs=(token, P("seq"), vector, rows, vector, rows, vector, rows, rows, rows, token),
         out_specs=(token, token, vector, rows, vector, rows, vector, rows, rows, rows, vector),

time: 1080 us -> 516 us (0.48)
  waiting for transfers between devices: 624 us -> 0 us
  Pallas kernels: 0 us -> 455 us
  blocking collectives: 214 us -> 0 us
  matrix products: 115 us -> 0 us
  local copies, waits for them, and re-layouts: 60.6 us -> 34.6 us
  other arithmetic: 32.1 us -> 15.9 us
  between operations: 15.6 us -> 2.09 us
    pallas_call x0 -> x3, Pallas kernels: none -> 455 us  [the longest x1 205 us: forward_call(): pl.pallas_call(functools.partial(forward_kernel, n), out_shape=shapes, in...]
    reduce_scatter x6 -> x0, waiting for transfers between devices: 360 us -> none  [scatter(): return lax.psum_scatter(values, axes, scatter_dimension=0, tiled=True)]
    all_gather x6 -> x0, waiting for transfers between devices: 140 us -> none  [the longest x5 135 us: gather(): return lax.all_gather(values, axes, axis=0, tiled=True)]
    unnamed x16 -> x0, waiting for transfers between devices: 124 us -> none
    dot_general x20 -> x0, matrix products: 110 us -> none  [the longest x5 32.1 us: contract_rows(): lax.dot_general(left, right, (((0,), (0,)), ((), ())), preferred_element_...]
    unnamed x2 -> x0, blocking collectives: 78.2 us -> none
    all_to_all x1 -> x0, blocking collectives: 73.6 us -> none  [shards(): both = lax.all_to_all(both.reshape(parts, 2, owned, chunk), 'ctx', 0, 0)]
    all_gather x2 -> x0, blocking collectives: 62.7 us -> none  [gather(): return lax.all_gather(values, axes, axis=0, tiled=True)]
  transfers between devices with their start and end apart: 15 -> 0, of which waited for: 12 -> 0; matrix products, arithmetic and copies ran while one was open for 14% -> 0% of each run, Pallas kernels for 0% -> 0%
where the time goes in v2:
time: 516 us; the launch traced here: 508 us
  Pallas kernels  455 us (88%)
  local copies, waits for them, and re-layouts  34.6 us (7%)
  other arithmetic  15.9 us (3%)
    pallas_call x1, Pallas kernels, forward_call(): pl.pallas_call(functools.partial(forward_kernel, n), out_shape=shapes, in...  205 us
    pallas_call x1, Pallas kernels, ffn_call(): pl.pallas_call(functools.partial(ffn_kernel, n), out_shape=[S((rows, widt...  153 us
    pallas_call x1, Pallas kernels, backward_call(): pl.pallas_call(functools.partial(backward_kernel, n), out_shape=[S((rows,...  97.2 us

profile of v2, /device:TPU:0, one launch (start us, length us, event | category | flops | bytes accessed | tf_op | source)
XLA Modules:
  0.0 507.8 jit_solution(12072556961574236640)
XLA Ops:
  0.7 0.8 dynamic_update_slice.3
  2.1 1.0 fusion.4
  3.8 1.8 fusion
  5.6 2.4 reshape.43
  9.0 0.8 stack_reshape.6
  9.8 2.4 reshape.44
  13.2 0.8 stack_reshape.7
  14.0 1.5 pad_maximum_fusion.gu
  16.9 205.3 %shard_map.203 = (bf16[2,1536,1152]{2,1,0:T(8,128)(2,1)}, bf16[1152,1536]{1,0:T(8,128)(2,1)}, bf16[8,128,1536]{2,1,0:T(8,128)(2,1)}, bf16[8,128,1536]{2,1,0:T(8,...) custom-call(s32[1]{0:T(128)S(6)} %copy.30.length_ref, ...), custom_call_target="tpu_custom_call" | custom-call | tf_op jit(solution)/shard_map/pallas_call | solution.py:508
  222.2 1.0 copy-done.3
  223.1 0.9 copy-done.4
  225.5 152.8 %shard_map.204 = (f32[128,1536]{1,0:T(8,128)}, f32[128,1536]{1,0:T(8,128)}, bf16[8,2,48,1152]{3,2,1,0:T(8,128)(2,1)}, f32[288,1536]{1,0:T(8,128)}) custom-call(bf16[2,1536,1152]{2,1,0:T(8,128)(2,1)} %get-tuple-element.30.gu_all, bf16[1152,1536]{1,0:T(8,128)(2,1)} %get-tuple-element.31.down_all, bf16[8,128,1536]{2,1,0:T(8,128)(2,1)} %get-tuple-element.32.cot_all, ...), custom_call_target="tpu_custom_call" | custom-call | tf_op jit(solution)/shard_map/pallas_call | solution.py:688
  378.4 4.8 reshape.46
  383.8 2.2 fusion.6
  386.1 1.4 copy.25
  387.4 2.4 squeeze.17
  389.8 3.0 copy.26
  392.9 2.4 squeeze.18
  395.2 5.1 %broadcast_multiply_fusion = (f32[48,8960]{1,0:T(8,128)}, f32[48]{0:T(128)}, f32[48,8960]{1,0:T(8,128)}) fusion(f32[48,8960]{1,0:T(8,128)} %squeeze.18, f32[48]{0:T(128)S(1)} %convert_element_type.46, bf16[48,8960]{1,0:T(8,128)(2,1)} %param.20, f32[48,8960]{1,0:T(8,128)} %squeeze.17, bf16[48,8960]{1,0:T(8,128)(2,1)S(1)} %copy-done.8), kind=kLoop, calls=%fused_computation.12 | loop fusion | flops 3440592 | bytes 8601984 | tf_op jit(solution)/shard_map/mul | solution.py:991
  400.3 97.2 %shard_map.205 = (bf16[128,1536]{1,0:T(8,128)(2,1)}, f32[128,1536]{1,0:T(8,128)}, f32[48,1536]{1,0:T(8,128)}, f32[48,2176]{1,0:T(8,128)}) custom-call(s32[1]{0:T(128)S(6)} %copy.30.length_ref, bf16[128,1536]{1,0:T(8,128)(2,1)} %bitcast.22, bf16[128,1536]{1,0:T(8,128)(2,1)} %bitcast.24, f32[128,1536]{1,0:T(8,128)} %copy-done.4, ...), custom_call_target="tpu_custom_call" | custom-call | tf_op jit(solution)/shard_map/pallas_call | solution.py:916
  497.5 2.6 slice_multiply_fusion
  500.1 1.9 convert_bitcast_fusion.1
  504.6 1.3 slice.33
  505.9 0.7 copy.31
  (41 shorter events, 9.4 us)
Async XLA Ops:
  14.0 2.3 copy-start.10
  14.0 2.4 copy-start.2
  15.5 1.3 copy-start
  15.5 1.4 copy-start.1
  15.5 1.4 copy-start.7
  222.2 1.0 copy-start.3
  223.1 0.9 copy-start.4
  224.0 0.7 copy-start.5
  224.8 0.7 copy-start.6
  392.9 2.4 copy-start.8
  400.3 97.2 %copy-start.11 = (bf16[48,2048]{1,0:T(8,128)(2,1)S(1)}, bf16[48,2048]{1,0:T(8,128)(2,1)}, u32[]{:S(2)}) copy-start(bf16[48,2048]{1,0:T(8,128)(2,1)} %param.15) | copy-start | bytes 589828
  497.5 7.1 %copy-start.9 = (f32[288,1536]{1,0:T(8,128)S(1)}, f32[288,1536]{1,0:T(8,128)}, u32[]{:S(2)}) copy-start(f32[288,1536]{1,0:T(8,128)} %get-tuple-element.46) | copy-start | bytes 5308420
  504.6 1.3 copy-start.12
  504.6 2.1 copy-start.13

commit v3 on v2

v3 whole, which is shorter than its diff:
```python
import functools

import jax
import jax.numpy as jnp
import numpy as np
from jax import lax
from jax.experimental import pallas as pl
from jax.experimental.pallas import tpu as pltpu
from jax.sharding import PartitionSpec as P

HEADS = 12
KV_HEADS = 2
HEAD = 128
QDIM = 1536
KVDIM = 256
GROUP = HEADS // KV_HEADS

EPSILON = 1e-06
ROPE_BASE = 1000000.0
MASKED = -1e30
SCALE = HEAD ** (-0.5)
BF = jnp.bfloat16
F32 = jnp.float32
BOTH = ("seq", "ctx")


DMA = pltpu.SemaphoreType.DMA
MESH = pl.DeviceIdType.MESH


def product(left, right):
    return jnp.dot(left, right, preferred_element_type=F32)


def contract_rows(left, right):
    return lax.dot_general(left, right, (((0,), (0,)), ((), ())), preferred_element_type=F32)


def contract_cols(left, right):
    return lax.dot_general(left, right, (((1,), (1,)), ((), ())), preferred_element_type=F32)


def inverse_rms(values):
    return lax.rsqrt(jnp.mean(values * values, axis=-1, keepdims=True) + EPSILON)


def rms_back(values, inverse, scaled_grad):
    inner = jnp.mean(scaled_grad * values, axis=-1, keepdims=True)
    return inverse * scaled_grad - values * (inverse * inverse * inverse) * inner


def rope_tables(positions):
    half = HEAD // 2
    frequency = ROPE_BASE ** (-jnp.arange(half, dtype=F32) * 2.0 / HEAD)
    angles = positions.astype(F32)[:, None] * frequency[None, :]
    return jnp.cos(angles), jnp.sin(angles)


def rotate(values, cosine, sine):
    half = HEAD // 2
    first, second = values[..., :half], values[..., half:]
    cosine, sine = cosine[:, None, :], sine[:, None, :]
    return jnp.concatenate([first * cosine - second * sine, second * cosine + first * sine], -1)


def gather(values, axes):
    return lax.all_gather(values, axes, axis=0, tiled=True)


def scatter(values, axes):
    return lax.psum_scatter(values, axes, scatter_dimension=0, tiled=True)


def plain_shards(
    tokens,
    lengths,
    attn_gain,
    qkv_weight,
    qkv_bias,
    out_weight,
    mlp_gain,
    gate_weight,
    up_weight,
    down_weight,
    out_grad,
):
    seqs, parts = lax.axis_size("seq"), lax.axis_size("ctx")
    inputs = tokens[0].astype(F32)
    rows, width = inputs.shape
    owned, hidden = gate_weight.shape
    piece = down_weight.shape[0]
    chunk = hidden // parts
    length = lengths[0]
    positions = lax.axis_index("ctx") * rows + jnp.arange(rows, dtype=jnp.int32)
    living = (positions < length).astype(F32)[:, None]
    cosine, sine = rope_tables(positions)

    gain_one = attn_gain.astype(F32)[:, None]
    gain_two = mlp_gain.astype(F32)[:, None]
    qkv_all = gather((qkv_weight.astype(F32) * gain_one).astype(BF), BOTH)
    bias_all = gather(qkv_bias, BOTH).astype(F32)
    out_all = gather(out_weight, BOTH)

    def to_chunks(weight):
        scaled = (weight.astype(F32) * gain_two).astype(BF)
        return scaled.reshape(owned, seqs, parts, piece).transpose(2, 0, 1, 3)

    both = jnp.stack([to_chunks(gate_weight), to_chunks(up_weight)], axis=1)
    both = lax.all_to_all(both.reshape(parts, 2, owned, chunk), "ctx", 0, 0)
    both = lax.all_gather(both, "seq", axis=0)
    gate_chunk = both[:, :, 0].reshape(width, chunk)
    up_chunk = both[:, :, 1].reshape(width, chunk)
    down_chunk = gather(down_weight, "seq")
    cotangent = out_grad[0].astype(F32) * living
    cot_all = gather(cotangent.astype(BF), "ctx")

    inverse_one = inverse_rms(inputs)
    normed_one = (inputs * inverse_one).astype(BF)
    project = product(normed_one, qkv_all) + bias_all
    queries = rotate(project[:, :QDIM].reshape(rows, HEADS, HEAD), cosine, sine).astype(BF)
    own_keys = rotate(
        project[:, QDIM : QDIM + KVDIM].reshape(rows, KV_HEADS, HEAD), cosine, sine
    ).astype(BF)
    own_values = project[:, QDIM + KVDIM :].astype(BF).reshape(rows, KV_HEADS, HEAD)
    keys, values = gather(own_keys, "ctx"), gather(own_values, "ctx")
    key_pos = jnp.arange(rows * parts, dtype=jnp.int32)
    allowed = (key_pos[None, :] <= positions[:, None]) & (key_pos[None, :] < length)
    grouped = queries.reshape(rows, KV_HEADS, GROUP, HEAD)
    scores = jnp.einsum("qgha,kga->ghqk", grouped, keys, preferred_element_type=F32) * SCALE
    scores = jnp.where(allowed, scores, MASKED)
    largest = jnp.max(scores, axis=-1, keepdims=True)
    exponent = jnp.exp(scores - largest)
    summed = jnp.sum(exponent, axis=-1, keepdims=True)
    probs = exponent / summed
    probs_low = probs.astype(BF)
    attended = jnp.einsum("ghqk,kga->qgha", probs_low, values, preferred_element_type=F32)
    attended = attended.reshape(rows, QDIM).astype(BF)
    middle = inputs + product(attended, out_all)

    inverse_two = inverse_rms(middle)
    normed_two = gather((middle * inverse_two).astype(BF), "ctx")
    gate_pre = product(normed_two, gate_chunk)
    up_pre = product(normed_two, up_chunk)
    sig = jax.nn.sigmoid(gate_pre)
    activated = (gate_pre * sig * up_pre).astype(BF)
    grad_act = contract_cols(cot_all, down_chunk)
    grad_gate = (grad_act * up_pre * (sig + gate_pre * sig * (1.0 - sig))).astype(BF)
    grad_up = (grad_act * gate_pre * sig).astype(BF)
    scaled_two = contract_cols(grad_gate, gate_chunk) + contract_cols(grad_up, up_chunk)
    scaled_two = scatter(scaled_two.astype(BF), "ctx").astype(F32)
    branch = scatter(product(activated, down_chunk).astype(BF), "ctx").astype(F32)
    output = ((middle + branch) * living).astype(BF)
    grad_down = scatter(contract_rows(activated, cot_all).astype(BF), "seq").astype(F32)
    raw = jnp.stack([contract_rows(normed_two, grad_gate), contract_rows(normed_two, grad_up)], 1)
    raw = scatter(raw.astype(BF), "seq").reshape(parts, owned, 2, chunk)
    raw = lax.all_to_all(raw, "ctx", 0, 0).astype(F32)
    raw = raw.reshape(parts, owned, 2, seqs, piece).transpose(2, 1, 3, 0, 4)
    raw = raw.reshape(2, owned, hidden)
    grad_mlp_gain = jnp.sum(raw[0] * gate_weight.astype(F32) + raw[1] * up_weight.astype(F32), 1)

    grad_middle = cotangent + rms_back(middle, inverse_two, scaled_two)
    grad_branch = grad_middle.astype(BF)
    grad_out = scatter(contract_rows(attended, grad_branch).astype(BF), BOTH).astype(F32)
    grad_mixed = contract_cols(grad_branch, out_all).astype(BF)
    grad_mixed = grad_mixed.reshape(rows, KV_HEADS, GROUP, HEAD)
    grad_probs = jnp.einsum("qgha,kga->ghqk", grad_mixed, values, preferred_element_type=F32)
    inner = jnp.sum(probs * grad_probs, axis=-1, keepdims=True)
    grad_scores = (probs * (grad_probs - inner)).astype(BF)
    grad_q = jnp.einsum("ghqk,kga->qgha", grad_scores, keys, preferred_element_type=F32) * SCALE
    grad_k = jnp.einsum("ghqk,qgha->kga", grad_scores, grouped, preferred_element_type=F32) * SCALE
    grad_v = jnp.einsum("ghqk,qgha->kga", probs_low, grad_mixed, preferred_element_type=F32)
    grad_k = scatter(grad_k.astype(BF), "ctx").astype(F32)
    grad_v = scatter(grad_v.astype(BF), "ctx").astype(F32)
    grad_q = rotate(grad_q.reshape(rows, HEADS, HEAD), cosine, -sine).reshape(rows, QDIM)
    grad_k = rotate(grad_k, cosine, -sine).reshape(rows, KVDIM)
    grad_project = jnp.concatenate([grad_q, grad_k, grad_v.reshape(rows, KVDIM)], axis=1)
    grad_project = grad_project.astype(BF)
    raw_qkv = scatter(contract_rows(normed_one, grad_project).astype(BF), BOTH).astype(F32)
    grad_attn_gain = jnp.sum(raw_qkv * qkv_weight.astype(F32), axis=1)
    grad_bias = jnp.sum(grad_project.astype(F32), axis=0)
    qk_width = QDIM + KVDIM
    grad_qk_bias = scatter(grad_bias[:qk_width], BOTH)
    grad_value_bias = scatter(grad_bias[qk_width:], BOTH)
    scaled_one = contract_cols(grad_project, qkv_all)
    grad_inputs = (grad_middle + rms_back(inputs, inverse_one, scaled_one)).astype(BF)
    return (
        output[None],
        grad_inputs[None],
        grad_attn_gain,
        raw_qkv * gain_one,
        grad_qk_bias,
        grad_out,
        grad_mlp_gain,
        raw[0] * gain_two,
        raw[1] * gain_two,
        grad_down,
        grad_value_bias,
    )


class Place:
    def __init__(self, n):
        self.n = n
        self.s, self.c = lax.axis_index("seq"), lax.axis_index("ctx")
        self.me = self.s * n + self.c
        self.core = lax.rem(self.s, 2)
        self.sib = self.s + 1 - 2 * self.core
        self.far = lax.rem(self.s + 2, 4)
        half = self.c // 2
        self.pos = half + lax.rem(self.c, 2) * (n - 1 - 2 * half)
        self.nxt, self.prv = self.at(1), self.at(-1)
    def at(self, offset):
        p = lax.rem(self.pos + offset + 2 * self.n, self.n)
        return 2 * p + (p // (self.n // 2)) * (2 * self.n - 1 - 4 * p)

def send(src, dst, ssem, rsem, seq, ctx):
    copy = pltpu.make_async_remote_copy(src, dst, ssem, rsem, device_id=(seq, ctx), device_id_type=MESH)
    copy.start()

def arrived(dst, rsem, place):
    pltpu.make_async_remote_copy(dst, dst, rsem, rsem, device_id=(place.s, place.c), device_id_type=MESH).wait_recv()

def sent(src, ssem, place):
    pltpu.make_async_remote_copy(src, src, ssem, ssem, device_id=(place.s, place.c), device_id_type=MESH).wait_send()

def enter(place, whole_group=True):
    barrier = pltpu.get_barrier_semaphore()
    def greet(d, z):
        pl.semaphore_signal(barrier, inc=1, device_id=(place.s, lax.rem(place.c + d, place.n)), device_id_type=MESH)
        return z
    lax.fori_loop(1, place.n, greet, 0)
    pl.semaphore_signal(barrier, inc=1, device_id=(place.sib, place.c), device_id_type=MESH)
    pl.semaphore_signal(barrier, inc=1, device_id=(place.far, place.c), device_id_type=MESH)
    pl.semaphore_wait(barrier, place.n + 1)


def add_low(left, right):
    return (left.astype(F32) + right.astype(F32)).astype(BF)

class RingGather:
    def __init__(self, pc, slots, ssem, rsem, index=None):
        self.pc, self.slots, self.ssem, self.rsem, self.index = pc, slots, ssem, rsem, index
        self.steps, self.half = pc.n // 2, slots.shape[2] // 2
        self.ways = ((0, -1, pc.nxt), (1, 1, pc.prv))
    def slot(self, offset):
        return self.index[offset] if self.index else self.pc.at(offset)
    def part(self, ref, f, t):
        return ref if t < self.steps - 1 else ref.at[:, pl.ds(f * self.half, self.half)]
    def hop(self, t, own=None):
        for f, sign, to in self.ways:
            src = self.slots.at[self.slot(sign * t)] if own is None else own
            there = self.slots.at[self.slot(sign * (t + 1) if self.index else sign * t)]
            send(self.part(src, f, t), self.part(there, f, t), self.ssem.at[f, t], self.rsem.at[f, t], self.pc.s, to)
    def turn(self, t):
        for f, sign, _ in self.ways:
            arrived(self.part(self.slots.at[self.slot(sign * (t + 1))], f, t), self.rsem.at[f, t], self.pc)
        if t + 1 < self.steps: self.hop(t + 1)
    def finish(self):
        for f in range(2):
            for t in range(self.steps): sent(self.part(self.slots.at[0], f, t), self.ssem.at[f, t], self.pc)

class RingSum:
    def __init__(self, pc, term, index, held_half, held, ssem, rsem, out):
        self.pc, self.term, self.index, self.out = pc, term, index, out
        self.held_half, self.held, self.ssem, self.rsem = held_half, held, ssem, rsem
        self.steps, self.half = pc.n // 2, term.shape[2] // 2
    def turn(self, t):
        pc, ahead = self.pc, self.steps - t
        for f, sign, to in ((0, 1, pc.nxt), (1, -1, pc.prv)):
            cols = slice(f * self.half, (f + 1) * self.half)
            i = self.index[sign * ahead]
            if t == 1:
                arrived(self.held_half.at[f], self.rsem.at[f, 0], pc)
                self.term[i, :, cols] = add_low(self.term[i, :, cols], self.held_half[f])
            elif t > 1:
                arrived(self.held.at[f, t - 2], self.rsem.at[f, t - 1], pc)
                if t < self.steps: self.term[i] = add_low(self.term[i], self.held[f, t - 2])
            if t == 0:
                src, dst = self.term.at[i, :, pl.ds(f * self.half, self.half)], self.held_half.at[f]
            elif t < self.steps:
                src, dst = self.term.at[i], self.held.at[f, t - 1]
            if t < self.steps: send(src, dst, self.ssem.at[f, t], self.rsem.at[f, t], pc.s, to)
        if t == self.steps:
            i = self.index[0]
            self.out[...] = self.term[i].astype(F32) + self.held[0, t - 2].astype(F32) + self.held[1, t - 2].astype(F32)
    def finish(self):
        for f in range(2):
            sent(self.held_half.at[f], self.ssem.at[f, 0], self.pc)
            for t in range(1, self.steps): sent(self.held.at[f, 0], self.ssem.at[f, t], self.pc)

class Spread:
    def __init__(self, pc, x_first, w, ss, rs, i):
        self.pc, self.x_first, self.w, self.ss, self.rs, self.i = pc, x_first, w, ss, rs, i
        self.y, self.x, self.z = pc.s // 2, lax.rem(pc.c, 2), pc.c // 2
        self.xp = pc.c + 1 - 2 * self.x
        self.deep = pc.n // 2
    def go(self, k, part, seq, ctx):
        send(part, part, self.ss.at[self.i, k], self.rs.at[self.i, k], seq, ctx)
    def come(self, k, part):
        arrived(part, self.rs.at[self.i, k], self.pc)
    def both(self, k, part, sib_k, seq, ctx, sib_part):
        self.go(k, part, seq, ctx)
        self.go(sib_k, sib_part, self.pc.sib, self.pc.c)
    def begin(self):
        own = self.w.at[self.y, self.pc.core, self.z, self.x]
        for d in range(1, self.deep):
            self.go(d - 1, own, self.pc.s, 2 * lax.rem(self.z + d, self.deep) + self.x)
    def stage1(self):
        pc, w, y, x = self.pc, self.w, self.y, self.x
        for d in range(1, self.deep):
            self.come(d - 1, w.at[y, pc.core, lax.rem(self.z + self.deep - d, self.deep), x])
        column = w.at[y, pc.core, :, x]
        if self.x_first: self.both(self.deep, column, self.deep + 2, pc.s, self.xp, column)
        else: self.both(self.deep, column, self.deep + 2, pc.far, pc.c, column)
    def stage2(self):
        pc, w, y, x = self.pc, self.w, self.y, self.x
        if self.x_first:
            new = w.at[y, pc.core, :, 1 - x]
            self.come(self.deep, new)
            self.both(self.deep + 1, w.at[y, pc.core], self.deep + 3, pc.far, pc.c, new)
        else:
            new = w.at[1 - y, pc.core, :, x]
            self.come(self.deep, new)
            self.both(self.deep + 1, w.at[:, pc.core, :, x], self.deep + 3, pc.s, self.xp, new)
    def stage3(self):
        pc, w, y, x = self.pc, self.w, self.y, self.x
        new = w.at[1 - y, pc.core] if self.x_first else w.at[:, pc.core, :, 1 - x]
        self.come(self.deep + 1, new)
        self.go(self.deep + 4, new, pc.sib, pc.c)
    def stage4(self):
        pc, w, y, x = self.pc, self.w, self.y, self.x
        other = 1 - pc.core
        self.come(self.deep + 2, w.at[y, other, :, x])
        self.come(self.deep + 3, w.at[y, other, :, 1 - x] if self.x_first else w.at[1 - y, other, :, x])
        self.come(self.deep + 4, w.at[1 - y, other] if self.x_first else w.at[:, other, :, 1 - x])
    def finish(self):
        w, four = self.w, self.w.at[0, 0, :, 0]
        eight = w.at[0, 0] if self.x_first else w.at[:, 0, :, 0]
        for d in range(1, self.deep): sent(w.at[0, 0, 0, 0], self.ss.at[self.i, d - 1], self.pc)
        for k, part in enumerate((four, eight, four, four, eight)): sent(part, self.ss.at[self.i, self.deep + k], self.pc)

def windows(n, piece, padded):
    for part in range(n):
        for plane in range(4):
            whole, packed = (plane * n + part) * piece, plane * padded
            first, packed_first = whole // 128 * 128, packed // 128 * 128
            span = -(-(whole + piece) // 128) * 128 - first
            packed_span = -(-(packed + piece) // 128) * 128 - packed_first
            yield part, whole - first, packed - packed_first, first, span, packed_first, packed_span

def shift_lanes(block, span, shift):
    if block.shape[1] < span:
        block = jnp.concatenate([block, jnp.zeros((block.shape[0], span - block.shape[1]), block.dtype)], 1)
    shift = shift % block.shape[1]
    return pltpu.roll(block, shift, 1) if shift else block

def place_back(raw, a, out):
    n, _, owned, chunk = raw.shape
    piece, padded = out.shape[1] // (4 * n), chunk // 4
    for part, at, packed_at, first, span, packed_first, packed_span in windows(n, piece, padded):
        block = raw[part, a, :, packed_first : packed_first + packed_span].astype(F32)
        block = shift_lanes(block, span, at - packed_at)[:, :span]
        lane = lax.broadcasted_iota(jnp.int32, block.shape, 1)
        here = (lane >= at) & (lane < at + piece)
        out[:, first : first + span] = jnp.where(here, block, out[:, first : first + span])

def place_out(weight, gain, a, packs):
    n, _, owned, chunk = packs.shape
    piece, padded = weight.shape[1] // (4 * n), chunk // 4
    for part in range(n): packs[part, a] = jnp.zeros((owned, chunk), BF)
    for part, at, packed_at, first, span, packed_first, packed_span in windows(n, piece, padded):
        block = weight[:, first : first + span].astype(F32) * gain
        block = shift_lanes(block, packed_span, packed_at - at)[:, :packed_span]
        lane = lax.broadcasted_iota(jnp.int32, block.shape, 1)
        here = (lane >= packed_at) & (lane < packed_at + piece)
        before = packs[part, a, :, packed_first : packed_first + packed_span].astype(F32)
        packs[part, a, :, packed_first : packed_first + packed_span] = jnp.where(here, block, before).astype(BF)


def rope(values, table_c, table_s):
    return values * table_c + pltpu.roll(values, HEAD // 2, 1) * table_s

def forward_kernel(n, length_ref, x_ref, og_ref, qw_ref, g1_ref, b_ref, gate_ref, up_ref, g2_ref, down, outw, tables,
                   gu_all, down_all, cot_all, qkv_all, out_all, kv_all, q_out, att_out, mid_out, n2_out,
                   w_kv, w_q0, w_q1, w_q2, w_o0, w_o1, xh_v, cot_v, kv_v, q_v, tab_v, pack_v,
                   local, save, ss, rs, g_recv, g_send, g_far, g_sib, d_recv, d_far, d_sib, c_recv, c_send,
                   kz_s, kz_r, kx_s, kx_r):
    pc = Place(n)
    me, s, c = pc.me, pc.s, pc.c
    y, x, z, xp = s // 2, lax.rem(c, 2), c // 2, c + 1 - 2 * lax.rem(c, 2)
    rows, width = x_ref.shape
    owned, piece = qw_ref.shape[0], down.shape[0]
    length = length_ref[0]
    third, owners, deep = QDIM // 3, 4 * n, n // 2

    def g_slot(i): return gu_all.at[:, pl.ds(pl.multiple_of(i * owned, owned), owned), :]
    def d_slot(i): return down_all.at[pl.ds(pl.multiple_of(i * piece, piece), piece), :]

    spreads = [Spread(pc, i % 2 == 0, w, ss, rs, i) for i, w in enumerate((w_kv, w_q0, w_q1, w_q2, w_o0, w_o1))]
    kvs, q0, q1, q2, o0, o1 = spreads
    cring = RingGather(pc, cot_all, c_send, c_recv)
    ohalf = width // 2
    lc = [pltpu.make_async_copy(a, b, local.at[i]) for i, (a, b) in enumerate((
        (outw.at[:, pl.ds(0, ohalf)], w_o0.at[y, pc.core, z, x]), (outw.at[:, pl.ds(ohalf, ohalf)], w_o1.at[y, pc.core, z, x]),
        (down, d_slot(s)), (tables.at[:, pl.ds(pl.multiple_of(c * rows, rows), rows), :], tab_v)))]
    for copy in lc: copy.start()
    g1 = g1_ref[...]
    def scaled(first, w): return (qw_ref[:, first : first + w].astype(F32) * g1).astype(BF)
    w_kv[y, pc.core, z, x, :, : 2 * KVDIM] = scaled(QDIM, 2 * KVDIM)
    share = b_ref.shape[1]
    bias = b_ref[...].astype(F32)
    rest = jnp.zeros((1, HEAD - share), F32)
    odd = lax.rem(me, 2) == 1
    row = jnp.where(odd, jnp.concatenate([rest, bias], 1), jnp.concatenate([bias, rest], 1))
    first_row = lax.broadcasted_iota(jnp.int32, (owned, HEAD), 0) == 0
    w_kv[y, pc.core, z, x, :, 2 * KVDIM :] = jnp.where(first_row, row, 0.0).astype(BF)
    for i, w in enumerate((w_q0, w_q1, w_q2)): w[y, pc.core, z, x] = scaled(i * third, third)
    slot_pos = c * rows + lax.broadcasted_iota(jnp.int32, (rows, width), 0)
    cot_v[...] = jnp.where(slot_pos < length, og_ref[...].astype(F32), 0.0).astype(BF)
    enter(pc)
    def gu_turn(t):
        k = s * n + lax.rem(c + n - t, n)
        arrived(g_slot(k), g_recv.at[k], pc)
        send(g_slot(k), g_slot(k), g_far.at[lax.rem(c + n - t, n)], g_recv.at[k], pc.far, c)
        send(g_slot(k), g_slot(k), g_sib.at[k], g_recv.at[k], pc.sib, c)
    for p in (kvs, q0, q1, q2): p.begin()
    send(down, d_slot(s), d_far.at[0], d_recv.at[s], pc.far, c)
    send(down, d_slot(s), d_sib.at[s], d_recv.at[s], pc.sib, c)
    own_cot = pltpu.make_async_copy(cot_v, cot_all.at[c], local.at[4])
    own_cot.start()
    xf = x_ref[...].astype(F32)
    xh_v[...] = (xf * inverse_rms(xf)).astype(BF)
    g2 = g2_ref[...]
    place_out(gate_ref, g2, 0, pack_v)
    kvs.stage1()
    q0.stage1()
    place_out(up_ref, g2, 1, pack_v)
    q1.stage1()
    kvs.stage2()
    own_gu = pltpu.make_async_copy(pack_v.at[c], g_slot(me), local.at[5])
    own_gu.start()
    def feed(d, v):
        to = lax.rem(c + d, n)
        send(pack_v.at[to], g_slot(me), g_send.at[to], g_recv.at[me], s, to)
        return v
    q2.stage1()
    lax.fori_loop(1, n, feed, 0)
    q0.stage2()
    kvs.stage3()
    q1.stage2()
    lc[0].wait(); lc[1].wait()
    o0.begin(); o1.begin()
    q2.stage2()
    q0.stage3()
    q1.stage3()
    q2.stage3()
    send(pack_v.at[c], g_slot(me), g_far.at[c], g_recv.at[me], pc.far, c)
    send(pack_v.at[c], g_slot(me), g_sib.at[me], g_recv.at[me], pc.sib, c)
    kvs.stage4()
    lc[3].wait()
    tc, ts = tab_v[0], tab_v[1]
    xh = xh_v[...]
    def bias_of(tile):
        d = 2 * tile
        def part(i):
            plane, place = i // n, i % n
            return w_kv[plane // 2, plane % 2, place // 2, place % 2, 0:1, 2 * KVDIM :].astype(F32)
        return part(d) + part(d + 1)
    kv = product(xh, w_kv[..., : 2 * KVDIM].reshape(owners * owned, 2 * KVDIM))
    for k in range(2 * KV_HEADS):
        lanes = slice(k * HEAD, (k + 1) * HEAD)
        one = kv[:, lanes] + bias_of(QDIM // HEAD + k)
        kv_v[z, x, :, lanes] = (rope(one, tc, ts) if k < KV_HEADS else one).astype(BF)
    own_kv = kv_v.at[z, x]
    for d in range(1, deep):
        send(own_kv, own_kv, kz_s.at[d], kz_r.at[d], s, 2 * lax.rem(z + d, deep) + x)
    send(own_kv, own_kv, kx_s.at[0], kx_r.at[0], s, xp)
    o0.stage1(); o1.stage1()
    for i, p in enumerate((q0, q1, q2)):
        p.stage4()
        r = product(xh, p.w[...].reshape(owners * owned, third))
        for k in range(third // HEAD):
            h = i * (third // HEAD) + k
            q_v[h] = rope(r[:, k * HEAD : (k + 1) * HEAD] + bias_of(h), tc, ts).astype(BF)
    for d in range(1, deep):
        block = kv_v.at[lax.rem(z + deep - d, deep), x]
        arrived(block, kz_r.at[d], pc)
        send(block, block, kx_s.at[d], kx_r.at[d], s, xp)
    cring.hop(0, cot_v)
    o0.stage2(); o1.stage2()
    saves = [pltpu.make_async_copy(q_v, q_out, save.at[0])]
    for i, (p, first) in enumerate(((kvs, QDIM), (q0, 0), (q1, third), (q2, 2 * third))):
        saves.append(pltpu.make_async_copy(p.w, qkv_all.at[:, :, :, :, :, pl.ds(first, p.w.shape[5])], save.at[1 + i]))
    for copy in saves: copy.start()
    for d in range(deep):
        arrived(kv_v.at[lax.rem(z + deep - d, deep), 1 - x], kx_r.at[d], pc)

    total = n * rows
    at_row = c * rows + lax.broadcasted_iota(jnp.int32, (rows, total), 0)
    at_col = lax.broadcasted_iota(jnp.int32, (rows, total), 1)
    allowed = (at_col <= at_row) & (at_col < length)
    def heads(first, count):
        def head(h, v):
            col = pl.multiple_of(h // GROUP * HEAD, HEAD)
            key = kv_v[:, :, :, pl.ds(col, HEAD)].reshape(total, HEAD)
            val = kv_v[:, :, :, pl.ds(pl.multiple_of(KVDIM + col, HEAD), HEAD)].reshape(total, HEAD)
            scores = jnp.where(allowed, contract_cols(q_v[h], key) * SCALE, MASKED)
            e = jnp.exp(scores - jnp.max(scores, axis=1, keepdims=True))
            probs = (e / jnp.sum(e, axis=1, keepdims=True)).astype(BF)
            att_out[:, pl.ds(pl.multiple_of(h * HEAD, HEAD), HEAD)] = product(probs, val).astype(BF)
            return v
        lax.fori_loop(first, first + count, head, 0)
    gu_turn(1); gu_turn(2)
    o0.stage3(); o1.stage3()
    heads(0, GROUP)
    gu_turn(3); gu_turn(4)
    cring.turn(0)
    heads(GROUP, GROUP)
    gu_turn(5); gu_turn(6); gu_turn(7)
    o0.stage4(); o1.stage4()
    saves2 = [pltpu.make_async_copy(kv_v, kv_all, save.at[5])]
    for i, p in enumerate((o0, o1)):
        saves2.append(pltpu.make_async_copy(p.w, out_all.at[:, :, :, :, :, pl.ds(i * ohalf, ohalf)], save.at[6 + i]))
    for copy in saves2: copy.start()
    cring.turn(1)
    att = att_out[...]
    for i, p in enumerate((o0, o1)):
        lanes = slice(i * ohalf, (i + 1) * ohalf)
        mid_out[:, lanes] = x_ref[:, lanes].astype(F32) + product(att, p.w[...].reshape(owners * owned, ohalf))
    mid = mid_out[...]
    n2_out[...] = (mid * inverse_rms(mid)).astype(BF)
    cring.turn(2)
    arrived(d_slot(pc.far), d_recv.at[pc.far], pc)
    send(d_slot(pc.far), d_slot(pc.far), d_sib.at[pc.far], d_recv.at[pc.far], pc.sib, c)
    def across(t, v):
        k = pc.far * n + lax.rem(c + n - t, n)
        arrived(g_slot(k), g_recv.at[k], pc)
        send(g_slot(k), g_slot(k), g_sib.at[k], g_recv.at[k], pc.sib, c)
        return v
    lax.fori_loop(0, n, across, 0)
    cring.turn(3)
    for plane in range(2):
        other = 2 * plane + 1 - pc.core
        arrived(d_slot(other), d_recv.at[other], pc)
        def come(t, v):
            i = other * n + t
            arrived(g_slot(i), g_recv.at[i], pc)
            return v
        lax.fori_loop(0, n, come, 0)
    for copy in [lc[2], own_cot, own_gu] + saves + saves2: copy.wait()
    for p in spreads: p.finish()
    cring.finish()
    for d in range(1, deep): sent(own_kv, kz_s.at[d], pc)
    for d in range(deep): sent(own_kv, kx_s.at[d], pc)
    sent(down, d_far.at[0], pc)
    block = pack_v.at[0]
    for plane in range(2):
        own = 2 * plane + pc.core
        sent(down, d_sib.at[own], pc)
        def tail(t, v):
            sent(block, g_sib.at[own * n + t], pc)
            return v
        lax.fori_loop(0, n, tail, 0)
    def tail2(t, v):
        src = lax.rem(c + t, n)
        sent(block, g_far.at[src], pc)
        @pl.when(t > 0)
        def _():
            sent(block, g_send.at[src], pc)
        return v
    lax.fori_loop(0, n, tail2, 0)

def forward_call(n, length, x, og, qkv, gain_one, bias, gate, up, gain_two, outw, down, tables):
    N, m = 4 * n, n // 2
    rows, width = x.shape
    owned, piece = qkv.shape[0], down.shape[0]
    chunk = 4 * piece
    S, V = jax.ShapeDtypeStruct, pltpu.VMEM
    joint = QDIM + 2 * KVDIM + HEAD
    shapes = [S((2, N * owned, chunk), BF), S((4 * piece, width), BF), S((n, rows, width), BF),
              S((2, 2, m, 2, owned, joint), BF), S((2, 2, m, 2, owned, width), BF), S((m, 2, rows, 2 * KVDIM), BF),
              S((HEADS, rows, HEAD), BF), S((rows, QDIM), BF), S((rows, width), F32), S((rows, width), BF)]
    anys = pl.BlockSpec(memory_space=pl.ANY)
    vmem = pl.BlockSpec(memory_space=pltpu.VMEM)
    scratch = [V((2, 2, m, 2, owned, w), BF) for w in (2 * KVDIM + HEAD,) + (QDIM // 3,) * 3 + (width // 2,) * 2]
    scratch += [V((rows, width), BF), V((rows, width), BF), V((m, 2, rows, 2 * KVDIM), BF), V((HEADS, rows, HEAD), BF),
                V((2, rows, HEAD), F32), V((n, 2, owned, chunk), BF),
                DMA((6,)), DMA((8,)), DMA((6, m + 5)), DMA((6, m + 5)), DMA((N,)), DMA((n,)), DMA((n,)), DMA((N,)),
                DMA((4,)), DMA((1,)), DMA((4,)), DMA((2, m)), DMA((2, m)), DMA((m,)), DMA((m,)), DMA((m,)), DMA((m,))]
    return pl.pallas_call(
        functools.partial(forward_kernel, n),
        out_shape=shapes,
        in_specs=[pl.BlockSpec(memory_space=pltpu.SMEM)] + [vmem] * 9 + [anys] * 2,
        out_specs=[anys] * 7 + [vmem] * 3,
        scratch_shapes=scratch,
        compiler_params=pltpu.CompilerParams(collective_id=0, has_side_effects=True, vmem_limit_bytes=56 * 2**20),
    )(length, x, og, qkv, gain_one, bias, gate, up, gain_two, down, outw, tables)


def ffn_kernel(n, n2_ref, gu_all, down_all, cot_all, u_own, o_own, gsum, ddown,
               gu_v, down_v, cot_v, n2_v, act_v, gg_v, gp_v, ut, uhh, uh, ot, ohh, oh, dgu_v, dd_v, r0g, r1g, r0d, r1d,
               load, rows_in, n_recv, n_send, u_recv, u_send, o_recv, o_send, gs0, gr0, gs1, gr1, save, ds0, dr0, ds1, dr1):
    pc = Place(n)
    s, c = pc.s, pc.c
    _, rows, width = cot_all.shape
    chunk = gu_all.shape[2]
    pairs = n // 2
    weights = [pltpu.make_async_copy(gu_all, gu_v, load.at[0]), pltpu.make_async_copy(down_all, down_v, load.at[1])]
    offsets = [o for j in range(1, pairs) for o in (-j, j)] + [pairs, 0]
    index = {o: i for i, o in enumerate(offsets)}
    index[-pairs] = index[pairs]
    fetch = [pltpu.make_async_copy(cot_all.at[pc.at(o)], cot_v.at[i], rows_in.at[i]) for i, o in enumerate(offsets)]
    for w in weights: w.start()
    for f in fetch: f.start()
    n2_v[index[0]] = n2_ref[...]
    nring = RingGather(pc, n2_v, n_send, n_recv, index)
    uring = RingSum(pc, ut, index, uhh, uh, u_send, u_recv, u_own)
    oring = RingSum(pc, ot, index, ohh, oh, o_send, o_recv, o_own)
    enter(pc)
    nring.hop(0)
    for w in weights: w.wait()
    tall = 2 * rows
    def forward(j):
        pair = slice(2 * j, 2 * j + 2)
        normed = n2_v[pair].reshape(tall, width)
        gate = product(normed, gu_v[0])
        up = product(normed, gu_v[1])
        sig = jax.nn.sigmoid(gate)
        gs = gate * sig
        act = (gs * up).astype(BF)
        act_v[pair] = act.reshape(2, rows, chunk)
        gp_v[pair] = gs.astype(BF).reshape(2, rows, chunk)
        gg_v[pair] = (up * (sig + gs * (1.0 - sig))).astype(BF).reshape(2, rows, chunk)
        ot[pair] = product(act, down_v[...]).astype(BF).reshape(2, rows, width)
    def backward(j):
        pair = slice(2 * j, 2 * j + 2)
        grad = contract_cols(cot_v[pair].reshape(tall, width), down_v[...])
        gg = (grad * gg_v[pair].reshape(tall, chunk).astype(F32)).astype(BF)
        gp = (grad * gp_v[pair].reshape(tall, chunk).astype(F32)).astype(BF)
        gg_v[pair] = gg.reshape(2, rows, chunk)
        gp_v[pair] = gp.reshape(2, rows, chunk)
        ut[pair] = (contract_cols(gg, gu_v[0]) + contract_cols(gp, gu_v[1])).astype(BF).reshape(2, rows, width)

    all_rows = n * rows
    plane = gu_all.shape[1] // 4
    piece = down_all.shape[0] // 4
    core, y = pc.core, s // 2
    tile = 384
    def cols_of(j): return pl.ds(j * tile, tile)
    wide_pieces = [(0, j, a) for j in range(chunk // tile) for a in range(2)]
    down_pieces = [(1, j, 0) for j in range(width // tile)]
    def compute(p):
        kind, j, a = p
        if kind == 0:
            lhs, rhs = n2_v[...].reshape(all_rows, width), (gg_v, gp_v)[a]
            grad = contract_rows(lhs, rhs[:, :, cols_of(j)].reshape(all_rows, tile))
            dgu_v[a, :, :, :, cols_of(j)] = grad.astype(BF).reshape(2, 2, plane, tile)
            send(dgu_v.at[a, :, 1 - core, :, cols_of(j)], r0g.at[a, :, :, cols_of(j)],
                 gs0.at[a, j], gr0.at[a, j], pc.sib, c)
        else:
            grad = contract_rows(act_v[...].reshape(all_rows, chunk), cot_v[:, :, cols_of(j)].reshape(all_rows, tile))
            dd_v[:, :, :, cols_of(j)] = grad.astype(BF).reshape(2, 2, piece, tile)
            send(dd_v.at[:, 1 - core, :, cols_of(j)], r0d.at[:, :, cols_of(j)], ds0.at[j], dr0.at[j], pc.sib, c)
    def add_core(p):
        kind, j, a = p
        cols = cols_of(j)
        if kind == 0:
            arrived(r0g.at[a, :, :, cols], gr0.at[a, j], pc)
            for k in range(2):
                r0g[a, k, :, cols] = add_low(r0g[a, k, :, cols], dgu_v[a, k, core, :, cols])
            send(r0g.at[a, 1 - y, :, cols], r1g.at[a, :, cols], gs1.at[a, j], gr1.at[a, j], pc.far, c)
        else:
            arrived(r0d.at[:, :, cols], dr0.at[j], pc)
            for k in range(2):
                r0d[k, :, cols] = add_low(r0d[k, :, cols], dd_v[k, core, :, cols])
            send(r0d.at[1 - y, :, cols], r1d.at[:, cols], ds1.at[j], dr1.at[j], pc.far, c)
    saves = []
    def add_far(p):
        kind, j, a = p
        cols = cols_of(j)
        if kind == 0:
            arrived(r1g.at[a, :, cols], gr1.at[a, j], pc)
            r1g[a, :, cols] = add_low(r1g[a, :, cols], r0g[a, y, :, cols])
            copy = pltpu.make_async_copy(r1g.at[a, :, cols], gsum.at[a, :, cols], save.at[a, j])
            copy.start()
            saves.append(copy)
        else:
            arrived(r1d.at[:, cols], dr1.at[j], pc)
            ddown[:, cols] = r1d[:, cols].astype(F32) + r0d[y, :, cols].astype(F32)
    for j in range(pairs):
        nring.turn(j)
        forward(j)
    for f in fetch: f.wait()
    backward(3)
    uring.turn(0)
    oring.turn(0)
    compute(down_pieces[0])
    compute(down_pieces[1])
    add_core(down_pieces[0])
    backward(2)
    uring.turn(1)
    add_core(down_pieces[1])
    compute(down_pieces[2])
    backward(1)
    uring.turn(2)
    add_core(down_pieces[2])
    compute(down_pieces[3])
    backward(0)
    uring.turn(3)
    add_core(down_pieces[3])
    oring.turn(1)
    for i, p in enumerate(wide_pieces):
        compute(p)
        if i: add_core(wide_pieces[i - 1])
    add_core(wide_pieces[-1])
    uring.turn(4)
    oring.turn(2)
    for p in down_pieces: add_far(p)
    for i, p in enumerate(wide_pieces):
        add_far(p)
        if i == 1: oring.turn(3)
    oring.turn(4)
    for kind, j, a in wide_pieces + down_pieces:
        cols = cols_of(j)
        if kind == 0:
            sent(r0g.at[a, :, :, cols], gs0.at[a, j], pc)
            sent(r1g.at[a, :, cols], gs1.at[a, j], pc)
        else:
            sent(r0d.at[:, :, cols], ds0.at[j], pc)
            sent(r1d.at[:, cols], ds1.at[j], pc)
    for copy in saves: copy.wait()
    nring.finish()
    uring.finish()
    oring.finish()

def ffn_call(n, n2, gu_all, down_all, cot_all):
    S, V = jax.ShapeDtypeStruct, pltpu.VMEM
    _, rows, width = cot_all.shape
    chunk = gu_all.shape[2]
    plane, piece = gu_all.shape[1] // 4, down_all.shape[0] // 4
    a, b = chunk // 384, width // 384
    anys = pl.BlockSpec(memory_space=pl.ANY)
    vmem = pl.BlockSpec(memory_space=pltpu.VMEM)
    held = [V((2, rows, width // 2), BF), V((2, n // 2 - 1, rows, width), BF)]
    return pl.pallas_call(
        functools.partial(ffn_kernel, n),
        out_shape=[S((rows, width), F32), S((rows, width), F32), S((2, plane, chunk), BF), S((piece, width), F32)],
        in_specs=[vmem] + [anys] * 3,
        out_specs=[vmem, vmem, anys, vmem],
        scratch_shapes=[V(gu_all.shape, BF), V(down_all.shape, BF), V(cot_all.shape, BF), V(cot_all.shape, BF)]
        + [V((n, rows, chunk), BF)] * 3 + [V((n, rows, width), BF)] + held + [V((n, rows, width), BF)] + held
        + [V((2, 2, 2, plane, chunk), BF), V((2, 2, piece, width), BF), V((2, 2, plane, chunk), BF), V((2, plane, chunk), BF),
           V((2, piece, width), BF), V((piece, width), BF)]
        + [DMA((2,)), DMA((n,))] + [DMA((2, n // 2))] * 6
        + [DMA((2, a))] * 5 + [DMA((b,))] * 4,
        compiler_params=pltpu.CompilerParams(collective_id=1, has_side_effects=True, vmem_limit_bytes=63 * 2**20),
    )(n2, gu_all, down_all, cot_all)


class Reduce:
    def __init__(self, pc, far_first, p, r0, r1, r2, r3, ss, rs, i):
        self.pc, self.far_first, self.p = pc, far_first, p
        self.r0, self.r1, self.r2, self.r3, self.ss, self.rs, self.i = r0, r1, r2, r3, ss, rs, i
        self.y, self.x, self.z = pc.s // 2, lax.rem(pc.c, 2), pc.c // 2
        self.xp = pc.c + 1 - 2 * self.x
    def go(self, k, src, dst, seq, ctx):
        send(src, dst, self.ss.at[self.i, k], self.rs.at[self.i, k], seq, ctx)
    def come(self, k, dst):
        arrived(dst, self.rs.at[self.i, k], self.pc)
    def stage0(self):
        pc = self.pc
        self.go(0, self.p.at[:, 1 - pc.core], self.r0, pc.sib, pc.c)
    def stage1(self):
        pc, r0 = self.pc, self.r0
        self.come(0, r0)
        r0[...] = add_low(r0[...], self.p[:, pc.core])
        if self.far_first: self.go(1, r0.at[1 - self.y], self.r1, pc.far, pc.c)
        else: self.go(1, r0.at[:, :, 1 - self.x], self.r1, pc.s, self.xp)
    def stage2(self):
        pc, r0, r1 = self.pc, self.r0, self.r1
        self.come(1, r1)
        if self.far_first:
            r1[...] = add_low(r1[...], r0[self.y])
            self.go(2, r1.at[:, 1 - self.x], self.r2, pc.s, self.xp)
        else:
            r1[...] = add_low(r1[...], r0[:, :, self.x])
            self.go(2, r1.at[1 - self.y], self.r2, pc.far, pc.c)
    def stage3(self):
        pc, r1, r2, n = self.pc, self.r1, self.r2, self.pc.n
        self.come(2, r2)
        r2[...] = add_low(r2[...], r1[:, self.x] if self.far_first else r1[self.y])
        def hand(d, w):
            to = lax.rem(self.z + d, n // 2)
            send(r2.at[to], self.r3.at[self.z], self.ss.at[self.i, 2 + d], self.rs.at[self.i, 2 + d], pc.s, 2 * to + self.x)
            return w
        lax.fori_loop(1, n // 2, hand, 0)
    def stage4(self):
        n = self.pc.n
        total = self.r2[self.z].astype(F32)
        for d in range(1, n // 2):
            src = lax.rem(self.z + n // 2 - d, n // 2)
            arrived(self.r3.at[src], self.rs.at[self.i, 2 + d], self.pc)
            total = total + self.r3[src].astype(F32)
        return total
    def finish(self):
        sent(self.r0, self.ss.at[self.i, 0], self.pc)
        sent(self.r1, self.ss.at[self.i, 1], self.pc)
        sent(self.r2, self.ss.at[self.i, 2], self.pc)
        for d in range(1, self.pc.n // 2):
            sent(self.r2.at[0], self.ss.at[self.i, 2 + d], self.pc)

def backward_kernel(n, length_ref, x_ref, og_ref, mid_ref, u_ref, o_ref, att_ref, q_ref, kv_ref, qkv_ref, out_ref, gate_ref, up_ref, gain_ref, tables, gsum,
                    y_out, dx_out, dout_out, dqkv_out, dgate_out, dup_out, dgain_out,
                    tab_v, gm_v, gb_v, dm_v, gp_v, p_v, gs_v, dkv_v, kx, kz, raw_v, *rest):
    pieces = 6
    bufs, (local, kxs, kxr, kzs, kzr, gss, grs, ss, rs) = rest[: 5 * pieces], rest[5 * pieces :]
    pc = Place(n)
    s, c = pc.s, pc.c
    rows, width = x_ref.shape
    total = n * rows
    length = length_ref[0]
    x, z = lax.rem(c, 2), c // 2
    xp = c + 1 - 2 * x
    red = [Reduce(pc, i % 2 == 0, *bufs[5 * i : 5 * i + 5], ss, rs, i) for i in range(pieces)]
    tab = pltpu.make_async_copy(tables.at[:, pl.ds(pl.multiple_of(c * rows, rows), rows), :], tab_v, local.at[0])
    tab.start()
    enter(pc)
    owned = out_ref.shape[1]
    def g_rows(i): return gsum.at[:, pl.ds(pl.multiple_of(i * owned, owned), owned), :]
    own_raw = pltpu.make_async_copy(g_rows(c), raw_v.at[c], local.at[1])
    own_raw.start()
    def feed(d, w):
        to = lax.rem(c + d, n)
        send(g_rows(to), raw_v.at[c], gss.at[to], grs.at[c], s, to)
        return w
    pos = c * rows + lax.broadcasted_iota(jnp.int32, (rows, width), 0)
    live = pos < length
    mid = mid_ref[...]
    gm = jnp.where(live, og_ref[...].astype(F32), 0.0) + rms_back(mid, inverse_rms(mid), u_ref[...])
    gm_v[...] = gm
    gb_v[...] = gm.astype(BF)
    y_out[...] = jnp.where(live, mid + o_ref[...], 0.0).astype(BF)
    owners = 4 * n
    def mix(j, w):
        weight = out_ref[pl.ds(j * 8, 8)].reshape(8 * owned, width)
        r = contract_cols(gb_v[...], weight).astype(BF)
        for k in range(8 * owned // HEAD):
            dm_v[j * (8 * owned // HEAD) + k] = r[:, k * HEAD : (k + 1) * HEAD]
        return w
    lax.fori_loop(0, owners // 8, mix, 0)
    gb = gb_v[...]
    for i in range(2):
        w = width // 2
        grad = contract_rows(att_ref[...], gb[:, i * w : (i + 1) * w])
        red[i].p[...] = grad.astype(BF).reshape(red[i].p.shape)
        red[i].stage0()
    lax.fori_loop(1, n, feed, 0)
    tab.wait()
    tc, ts = tab_v[0], tab_v[1]

    at_row = c * rows + lax.broadcasted_iota(jnp.int32, (rows, total), 0)
    at_col = lax.broadcasted_iota(jnp.int32, (rows, total), 1)
    allowed = (at_col <= at_row) & (at_col < length)
    def group(g):
        key = kv_ref[:, :, g * HEAD : (g + 1) * HEAD].reshape(total, HEAD)
        val = kv_ref[:, :, KVDIM + g * HEAD : KVDIM + (g + 1) * HEAD].reshape(total, HEAD)
        def head(i, w):
            h = g * GROUP + i
            part = pl.ds(pl.multiple_of(i * rows, rows), rows)
            scores = jnp.where(allowed, contract_cols(q_ref[h], key) * SCALE, MASKED)
            e = jnp.exp(scores - jnp.max(scores, axis=1, keepdims=True))
            probs = e / jnp.sum(e, axis=1, keepdims=True)
            gprobs = contract_cols(dm_v[h], val)
            inner = jnp.sum(probs * gprobs, axis=1, keepdims=True)
            gs = (probs * (gprobs - inner)).astype(BF)
            p_v[part, :] = probs.astype(BF)
            gs_v[part, :] = gs
            dq = product(gs, key) * SCALE
            gp_v[:, pl.ds(pl.multiple_of(h * HEAD, HEAD), HEAD)] = (dq * tc - pltpu.roll(dq, HEAD // 2, 1) * ts).astype(BF)
            return w
        lax.fori_loop(0, GROUP, head, 0)
        mine = slice(g * GROUP, (g + 1) * GROUP)
        dk = contract_rows(gs_v[...], q_ref[mine].reshape(GROUP * rows, HEAD)) * SCALE
        dv = contract_rows(p_v[...], dm_v[mine].reshape(GROUP * rows, HEAD))
        lanes = slice(g * 2 * HEAD, g * 2 * HEAD + 2 * HEAD)
        dkv_v[:, :, :, lanes] = jnp.concatenate([dk, dv], 1).astype(BF).reshape(n // 2, 2, rows, 2 * HEAD)
        send(dkv_v.at[:, 1 - x, :, lanes], kx.at[:, :, lanes], kxs.at[g], kxr.at[g], s, xp)
    def kv_x(g):
        lanes = slice(g * 2 * HEAD, g * 2 * HEAD + 2 * HEAD)
        arrived(kx.at[:, :, lanes], kxr.at[g], pc)
        kx[:, :, lanes] = add_low(kx[:, :, lanes], dkv_v[:, x, :, lanes])
        for d in range(1, n // 2):
            to = lax.rem(z + d, n // 2)
            send(kx.at[to, :, lanes], kz.at[z, :, lanes], kzs.at[g, d], kzr.at[g, d], s, 2 * to + x)
    def kv_z(g):
        lanes = slice(g * 2 * HEAD, g * 2 * HEAD + 2 * HEAD)
        sumkv = kx[z, :, lanes].astype(F32)
        for d in range(1, n // 2):
            src = lax.rem(z + n // 2 - d, n // 2)
            arrived(kz.at[src, :, lanes], kzr.at[g, d], pc)
            sumkv = sumkv + kz[src, :, lanes].astype(F32)
        dk, dv = sumkv[:, :HEAD], sumkv[:, HEAD:]
        k0, v0 = QDIM + g * HEAD, QDIM + KVDIM + g * HEAD
        gp_v[:, k0 : k0 + HEAD] = (dk * tc - pltpu.roll(dk, HEAD // 2, 1) * ts).astype(BF)
        gp_v[:, v0 : v0 + HEAD] = dv.astype(BF)
    xin = x_ref[...].astype(F32)
    inverse = inverse_rms(xin)
    def joint(i, first, w):
        xh = (x_ref[...].astype(F32) * inverse).astype(BF)
        grad = contract_rows(xh, gp_v[:, first : first + w]).astype(BF)
        shape = red[i].p.shape[:-1] + (w,)
        red[i].p[..., :w] = grad.reshape(shape)
    group(0)
    red[0].stage1(); red[1].stage1()
    group(1)
    kv_x(0)
    red[0].stage2(); red[1].stage2()
    third = QDIM // 3
    for i in range(3):
        joint(2 + i, i * third, third)
        red[2 + i].stage0()
        if i == 0: kv_x(1)
    red[0].stage3(); red[1].stage3()
    red[2].stage1(); red[3].stage1(); red[4].stage1()
    kv_z(0); kv_z(1)
    joint(5, QDIM, 2 * KVDIM)
    sums = jnp.sum(gp_v[...].astype(F32), axis=0, keepdims=True)
    p5 = red[5].p
    qk_width = QDIM + KVDIM
    at = lax.broadcasted_iota(jnp.int32, (owned, HEAD), 0)
    for d in range(owners):
        tiles = (qk_width // owners * d // HEAD, qk_width // owners * d // HEAD + 1, (qk_width + KVDIM // owners * d) // HEAD)
        part = jnp.zeros((owned, HEAD), F32)
        for k, t in enumerate(tiles):
            part = jnp.where(at == k, sums[:, t * HEAD : t * HEAD + HEAD], part)
        plane = d // n
        p5[plane // 2, plane % 2, d % n // 2, d % 2, :, 2 * KVDIM :] = part.astype(BF)
    red[5].stage0()
    red[2].stage2(); red[3].stage2(); red[4].stage2()
    red[5].stage1()
    qk = QDIM + 2 * KVDIM
    gp = gp_v[...]
    def back(j, w):
        weight = qkv_ref[pl.ds(j * 8, 8), :, :qk].reshape(8 * owned, qk)
        cols = pl.ds(pl.multiple_of(j * 8 * owned, 8 * owned), 8 * owned)
        dx_out[:, cols] = contract_cols(gp, weight)
        return w
    lax.fori_loop(0, owners // 8, back, 0)
    red[2].stage3(); red[3].stage3(); red[4].stage3()
    red[5].stage2()
    own_raw.wait()
    def fed(d, w):
        src = lax.rem(c + d, n)
        arrived(raw_v.at[src], grs.at[src], pc)
        return w
    lax.fori_loop(1, n, fed, 0)
    place_back(raw_v, 0, dgate_out)
    dx_out[...] = gm_v[...] + rms_back(x_ref[...].astype(F32), inverse, dx_out[...])
    for i in range(2):
        dout_out[:, i * (width // 2) : (i + 1) * (width // 2)] = red[i].stage4()
    red[5].stage3()
    place_back(raw_v, 1, dup_out)
    gain = gain_ref[...]
    dgain_out[...] = jnp.sum(
        dgate_out[...] * gate_ref[...].astype(F32) + dup_out[...] * up_ref[...].astype(F32), axis=1, keepdims=True
    )
    dgate_out[...] = dgate_out[...] * gain
    dup_out[...] = dup_out[...] * gain
    for i in range(3):
        dqkv_out[:, i * third : (i + 1) * third] = red[2 + i].stage4()
    dqkv_out[:, QDIM:] = red[5].stage4()
    for r in red: r.finish()
    def fed_out(d, w):
        sent(raw_v.at[0], gss.at[lax.rem(c + d, n)], pc)
        return w
    lax.fori_loop(1, n, fed_out, 0)
    for g in range(2):
        lanes = slice(g * 2 * HEAD, g * 2 * HEAD + 2 * HEAD)
        sent(kx.at[:, :, lanes], kxs.at[g], pc)
        for d in range(1, n // 2): sent(kx.at[0, :, lanes], kzs.at[g, d], pc)

def backward_call(n, length, x, og, mid, u, o, att, q, kv, qkv_all, out_all, gate, up, gain, tables, gsum):
    S, V = jax.ShapeDtypeStruct, pltpu.VMEM
    rows, width = x.shape
    owned = qkv_all.shape[1]
    anys = pl.BlockSpec(memory_space=pl.ANY)
    vmem = pl.BlockSpec(memory_space=pltpu.VMEM)
    m = n // 2
    scratch = [V((2, rows, HEAD), F32), V((rows, width), F32), V((rows, width), BF), V((HEADS, rows, HEAD), BF),
               V((rows, QDIM + 2 * KVDIM), BF), V((GROUP * rows, n * rows), BF), V((GROUP * rows, n * rows), BF),
               V((m, 2, rows, 2 * KVDIM), BF), V((m, rows, 2 * KVDIM), BF), V((m, rows, 2 * KVDIM), BF),
               V((n, 2, owned, gsum.shape[2]), BF)]
    for i, w in enumerate((width // 2, width // 2, QDIM // 3, QDIM // 3, QDIM // 3, 2 * KVDIM + HEAD)):
        one = (m, 2, owned, w) if i % 2 == 0 else (2, m, owned, w)
        scratch += [V((2, 2, m, 2, owned, w), BF), V((2, m, 2, owned, w), BF), V(one, BF), V((m, owned, w), BF), V((m, owned, w), BF)]
    scratch += [DMA((2,)), DMA((2,)), DMA((2,)), DMA((2, m)), DMA((2, m)), DMA((n,)), DMA((n,)), DMA((6, 2 + m)), DMA((6, 2 + m))]
    return pl.pallas_call(
        functools.partial(backward_kernel, n),
        out_shape=[S((rows, width), BF), S((rows, width), F32), S((owned, width), F32), S((owned, qkv_all.shape[2]), F32),
                   S(gate.shape, F32), S(gate.shape, F32), S((owned, 1), F32)],
        in_specs=[pl.BlockSpec(memory_space=pltpu.SMEM)] + [vmem] * 13 + [anys] * 2,
        out_specs=[vmem] * 7,
        scratch_shapes=scratch,
        compiler_params=pltpu.CompilerParams(collective_id=2, has_side_effects=True, vmem_limit_bytes=62 * 2**20),
    )(length, x, og, mid, u, o, att, q, kv, qkv_all, out_all, gate, up, gain, tables, gsum)


def kernel_shards(
    tokens,
    lengths,
    attn_gain,
    qkv_weight,
    qkv_bias,
    out_weight,
    mlp_gain,
    gate_weight,
    up_weight,
    down_weight,
    out_grad,
):
    seqs, parts = lax.axis_size("seq"), lax.axis_size("ctx")
    rows, width = tokens.shape[1:]
    owned = gate_weight.shape[0]
    piece = down_weight.shape[0]
    padded = -(-piece // 32) * 32
    owners = seqs * parts
    me = lax.axis_index("seq") * parts + lax.axis_index("ctx")
    gain_one = attn_gain.astype(F32)[:, None]
    gain_two = mlp_gain.astype(F32)[:, None]
    half = HEAD // 2
    frequency = np.float32(ROPE_BASE) ** (-np.arange(half, dtype=np.float32) * np.float32(2.0 / HEAD))
    angles = np.arange(rows * parts, dtype=np.float32)[:, None] * frequency.astype(np.float32)[None, :]
    cosine, sine = np.cos(angles), np.sin(angles)
    tables = jnp.asarray(np.stack([np.concatenate([cosine, cosine], 1), np.concatenate([-sine, sine], 1)]), F32)
    down = jnp.pad(down_weight, ((0, padded - piece), (0, 0)))
    x, og = tokens[0], out_grad[0]
    gu_all, down_all, cot_all, qkv_all, out_all, kv_all, q, att, mid, n2 = forward_call(
        parts, lengths, x, og, qkv_weight, gain_one, qkv_bias[None], gate_weight, up_weight, gain_two,
        out_weight, down, tables,
    )
    u, o, gate_up_sum, grad_down = ffn_call(parts, n2, gu_all, down_all, cot_all)
    joint = qkv_all.shape[-1]
    output, grad_inputs, grad_out, raw_qkv, grad_gate, grad_up, grad_mlp_gain = backward_call(
        parts, lengths, x, og, mid, u, o, att, q, kv_all.reshape(parts, rows, 2 * KVDIM),
        qkv_all.reshape(owners, owned, joint), out_all.reshape(owners, owned, width),
        gate_weight, up_weight, gain_two, tables, gate_up_sum,
    )
    qk = QDIM + 2 * KVDIM
    bias_rows, raw_qkv = raw_qkv[:3, qk:], raw_qkv[:, :qk]
    grad_attn_gain = jnp.sum(raw_qkv * qkv_weight.astype(F32), axis=1)
    per, per_value = (QDIM + KVDIM) // owners, KVDIM // owners
    grad_qk_bias = lax.dynamic_slice_in_dim(bias_rows[:2].reshape(2 * HEAD), lax.rem(per * me, HEAD), per)
    grad_value_bias = lax.dynamic_slice_in_dim(bias_rows[2], lax.rem(per_value * me, HEAD), per_value)
    return (
        output[None],
        grad_inputs.astype(BF)[None],
        grad_attn_gain,
        raw_qkv * gain_one,
        grad_qk_bias,
        grad_out,
        grad_mlp_gain[:, 0],
        grad_gate,
        grad_up,
        grad_down[:piece],
        grad_value_bias,
    )


def solution(mesh):
    seqs, parts = mesh.shape["seq"], mesh.shape["ctx"]
    tiled = seqs == 4 and parts == 8 and 1536 // (seqs * parts) % 16 == 0
    rows, vector = P(BOTH, None), P(BOTH)
    token = P("seq", "ctx", None)
    return jax.shard_map(
        kernel_shards if tiled else plain_shards,
        mesh=mesh,
        in_specs=(token, P("seq"), vector, rows, vector, rows, vector, rows, rows, rows, token),
        out_specs=(token, token, vector, rows, vector, rows, vector, rows, rows, rows, vector),
        check_vma=False,
    )
```

time: 516 us -> 411 us (0.80)
  Pallas kernels: 455 us -> 386 us
  local copies, waits for them, and re-layouts: 34.6 us -> 12.2 us
  other arithmetic: 15.9 us -> 6.45 us
    pallas_call x1, Pallas kernels: 205 us -> 148 us  [forward_call(): pl.pallas_call(functools.partial(forward_kernel, n), out_shape=shapes, in...]
    pallas_call x1, Pallas kernels: 153 us -> 127 us  [ffn_call(): pl.pallas_call(functools.partial(ffn_kernel, n), out_shape=[S((rows, widt...]
    pallas_call x1, Pallas kernels: 97.2 us -> 112 us  [backward_call(): pl.pallas_call(functools.partial(backward_kernel, n), out_shape=[S((rows,...]
    reshape x5 -> x0, local copies, waits for them, and re-layouts: 10.5 us -> none  [the longest x4 5.65 us: to_chunks(): (weight.astype(F32) * gain_two).astype(BF)]
    slice x3 -> x0, local copies, waits for them, and re-layouts: 6.64 us -> none  [the longest x2 5.27 us: kernel_shards(): raw[1] * up_weight.astype(F32)]
where the time goes in v3:
time: 411 us; the launch traced here: 406 us
  Pallas kernels  386 us (94%)
  local copies, waits for them, and re-layouts  12.2 us (3%)
  other arithmetic  6.45 us (2%)
    pallas_call x1, Pallas kernels, forward_call(): pl.pallas_call(functools.partial(forward_kernel, n), out_shape=shapes, in...  148 us
    pallas_call x1, Pallas kernels, ffn_call(): pl.pallas_call(functools.partial(ffn_kernel, n), out_shape=[S((rows, widt...  127 us
    pallas_call x1, Pallas kernels, backward_call(): pl.pallas_call(functools.partial(backward_kernel, n), out_shape=[S((rows,...  112 us

profile of v3, /device:TPU:0, one launch (start us, length us, event | category | flops | bytes accessed | tf_op | source)
XLA Modules:
  0.0 406.0 jit_solution(13811157054594130027)
XLA Ops:
  0.6 0.7 fusion
  1.3 0.7 copy.26.g1_ref
  2.0 0.7 bitcast_convert_fusion
  2.7 0.7 copy.27.g2_ref.gain_ref
  4.0 2.1 pad.4.down
  6.1 147.8 %shard_map.203 = (bf16[2,1536,1152]{2,1,0:T(8,128)(2,1)}, bf16[1152,1536]{1,0:T(8,128)(2,1)}, bf16[8,128,1536]{2,1,0:T(8,128)(2,1)}, bf16[2,2,4,2,48,2176]{5,4,3...) custom-call(s32[1]{0:T(128)S(6)} %copy.33.length_ref, ...), custom_call_target="tpu_custom_call" | custom-call | tf_op jit(solution)/shard_map/pallas_call | solution.py:590
  153.9 126.5 %shard_map.204 = (f32[128,1536]{1,0:T(8,128)}, f32[128,1536]{1,0:T(8,128)}, bf16[2,384,1152]{2,1,0:T(8,128)(2,1)}, f32[288,1536]{1,0:T(8,128)}) custom-call(bf16[128,1536]{1,0:T(8,128)(2,1)} %get-tuple-element.33.n2_ref, bf16[2,1536,1152]{2,1,0:T(8,128)(2,1)} %get-tuple-element.34.gu_all, bf16[1152,1536]{1,0:T(8,128)(2,1)} %get-tuple-element.35.down_all, ...), custom_call_target="tpu_custom_call" | custom-call | tf_op jit(solution)/shard_map/pallas_call | solution.py:745
  280.4 0.0 copy-start.3
  280.4 111.6 %shard_map.205 = (bf16[128,1536]{1,0:T(8,128)(2,1)}, f32[128,1536]{1,0:T(8,128)}, f32[48,1536]{1,0:T(8,128)}, f32[48,2176]{1,0:T(8,128)}, f32[48,8960]{1,0:T(8,1...) custom-call(s32[1]{0:T(128)S(6)} %copy.33.length_ref, bf16[128,1536]{1,0:T(8,128)(2,1)} %bitcast.21, ...), custom_call_target="tpu_custom_call" | custom-call | tf_op jit(solution)/shard_map/pallas_call | solution.py:997
  392.0 0.0 copy-start.6
  392.0 0.0 copy-start.2
  392.0 2.6 slice_multiply_fusion
  394.6 1.9 convert_bitcast_fusion
  396.5 0.7 slice_bitcast_fusion
  397.3 0.6 dynamic_slice.8
  397.8 0.7 slice.18
  398.5 0.6 dynamic-slice_bitcast_fusion
  399.1 0.6 reduce
  399.7 1.3 slice.17
  401.1 0.7 copy.34
  401.8 0.7 copy.35
  402.5 1.2 copy.36
  403.7 0.9 copy-done
  404.6 1.2 copy.37
  (10 shorter events, 0.0 us)
Async XLA Ops:
  280.4 111.6 %copy-start.3 = (bf16[48,2048]{1,0:T(8,128)(2,1)S(1)}, bf16[48,2048]{1,0:T(8,128)(2,1)}, u32[]{:S(2)}) copy-start(bf16[48,2048]{1,0:T(8,128)(2,1)} %qw_ref.1) | copy-start | bytes 589828
  392.0 7.1 %copy-start.6 = (f32[48,1]{1,0:T(8,128)S(1)}, f32[48,1]{1,0:T(8,128)}, u32[]{:S(2)}) copy-start(f32[48,1]{1,0:T(8,128)} %get-tuple-element.49) | copy-start | bytes 580
  392.0 7.7 %copy-start.2 = (f32[288,1536]{1,0:T(8,128)S(1)}, f32[288,1536]{1,0:T(8,128)}, u32[]{:S(2)}) copy-start(f32[288,1536]{1,0:T(8,128)} %get-tuple-element.52) | copy-start | bytes 5308420
  396.5 4.5 %copy-start.4 = (bf16[128,1536]{1,0:T(8,128)(2,1)S(1)}, bf16[128,1536]{1,0:T(8,128)(2,1)}, u32[]{:S(2)}) copy-start(bf16[128,1536]{1,0:T(8,128)(2,1)} %get-tuple-element.45) | copy-start | bytes 1179652
  399.7 2.1 copy-start.5
  399.7 2.8 copy-start.1
  402.5 2.1 copy-start

commit v4 on v3

--- a/solution.py
+++ b/solution.py
@@ -365,26 +365,28 @@
         out[:, first : first + span] = jnp.where(here, block, out[:, first : first + span])
 
 def place_out(weight, gain, a, packs):
-    n, _, owned, chunk = packs.shape
+    n, _, _, chunk = packs.shape
+    owned = weight.shape[0]
     piece, padded = weight.shape[1] // (4 * n), chunk // 4
-    for part in range(n): packs[part, a] = jnp.zeros((owned, chunk), BF)
+    for part in range(n): packs[part, a, :owned] = jnp.zeros((owned, chunk), BF)
     for part, at, packed_at, first, span, packed_first, packed_span in windows(n, piece, padded):
         block = weight[:, first : first + span].astype(F32) * gain
         block = shift_lanes(block, packed_span, packed_at - at)[:, :packed_span]
         lane = lax.broadcasted_iota(jnp.int32, block.shape, 1)
         here = (lane >= packed_at) & (lane < packed_at + piece)
-        before = packs[part, a, :, packed_first : packed_first + packed_span].astype(F32)
-        packs[part, a, :, packed_first : packed_first + packed_span] = jnp.where(here, block, before).astype(BF)
+        before = packs[part, a, :owned, packed_first : packed_first + packed_span].astype(F32)
+        packs[part, a, :owned, packed_first : packed_first + packed_span] = jnp.where(here, block, before).astype(BF)
 
 
 def rope(values, table_c, table_s):
     return values * table_c + pltpu.roll(values, HEAD // 2, 1) * table_s
 
-def forward_kernel(n, length_ref, x_ref, og_ref, qw_ref, g1_ref, b_ref, gate_ref, up_ref, g2_ref, down, outw, tables,
-                   gu_all, down_all, cot_all, qkv_all, out_all, kv_all, q_out, att_out, mid_out, n2_out,
-                   w_kv, w_q0, w_q1, w_q2, w_o0, w_o1, xh_v, cot_v, kv_v, q_v, tab_v, pack_v,
-                   local, save, ss, rs, g_recv, g_send, g_far, g_sib, d_recv, d_far, d_sib, c_recv, c_send,
-                   kz_s, kz_r, kx_s, kx_r):
+def layer_kernel(n, length_ref, x_ref, og_ref, qw_ref, g1_ref, b_ref, gate_ref, up_ref, g2_ref, down, outw, tables,
+                 qkv_all, out_all, kv_all, q_out, half_sum, dsum, att_out, mid_out, u_own, o_own,
+                 gu_v, down_v, cot_v, n2_v, act_v, gg_v, gp_v, ut, uhh, uh, ot, ohh, oh, dgu_v, dd_v, r0g, r0d, r1d, w_o2,
+                 kv_v, q_v, tab_v,
+                 local, save, ss, rs, g_recv, g_send, g_own, g_far, g_sib, d_recv, d_far, d_sib, c_recv, c_send,
+                 kz_s, kz_r, kx_s, kx_r, n_recv, n_send, u_recv, u_send, o_recv_, o_send_, gs0, gr0, gsave, ds0, dr0, ds1, dr1, dsave):
     pc = Place(n)
     me, s, c = pc.me, pc.s, pc.c
     y, x, z, xp = s // 2, lax.rem(c, 2), c // 2, c + 1 - 2 * lax.rem(c, 2)
@@ -393,16 +395,29 @@
     length = length_ref[0]
     third, owners, deep = QDIM // 3, 4 * n, n // 2
 
-    def g_slot(i): return gu_all.at[:, pl.ds(pl.multiple_of(i * owned, owned), owned), :]
-    def d_slot(i): return down_all.at[pl.ds(pl.multiple_of(i * piece, piece), piece), :]
-
-    spreads = [Spread(pc, i % 2 == 0, w, ss, rs, i) for i, w in enumerate((w_kv, w_q0, w_q1, w_q2, w_o0, w_o1))]
-    kvs, q0, q1, q2, o0, o1 = spreads
-    cring = RingGather(pc, cot_all, c_send, c_recv)
-    ohalf = width // 2
+    def g_slot(i): return gu_v.at[:, pl.ds(pl.multiple_of(i * owned, owned), owned), :]
+    def pack(i): return act_v.at[i, :, pl.ds(0, owned), :]
+    def d_slot(i): return down_v.at[pl.ds(pl.multiple_of(i * piece, piece), piece), :]
+
+    kvw = 2 * KVDIM + HEAD
+    def cut(ref, first, w): return ref.at[:, :, :, :, :, pl.ds(first, w)]
+    w_kv = cut(dgu_v.at[0], 0, kvw)
+    wide = (w_kv, cut(dgu_v.at[0], kvw, third), cut(dgu_v.at[1], 0, third), cut(dgu_v.at[1], third, third),
+            cut(r0g, 0, width // 2), cut(r0g, width // 2, width // 4), w_o2)
+    spreads = [Spread(pc, i % 2 == 0, w, ss, rs, i) for i, w in enumerate(wide)]
+    kvs, q0, q1, q2, o0, o1, o2 = spreads
+    outs = ((o0, 0, width // 2), (o1, width // 2, width // 4), (o2, width // 4 * 3, width // 4))
+    pairs = n // 2
+    offsets = [o for j in range(1, pairs) for o in (-j, j)] + [pairs, 0]
+    index = {o: i for i, o in enumerate(offsets)}
+    index[-pairs] = index[pairs]
+    cring = RingGather(pc, cot_v, c_send, c_recv, index)
+    nring = RingGather(pc, n2_v, n_send, n_recv, index)
+    uring = RingSum(pc, ut, index, uhh, uh, u_send, u_recv, u_own)
+    oring = RingSum(pc, ot, index, ohh, oh, o_send_, o_recv_, o_own)
     lc = [pltpu.make_async_copy(a, b, local.at[i]) for i, (a, b) in enumerate((
-        (outw.at[:, pl.ds(0, ohalf)], w_o0.at[y, pc.core, z, x]), (outw.at[:, pl.ds(ohalf, ohalf)], w_o1.at[y, pc.core, z, x]),
-        (down, d_slot(s)), (tables.at[:, pl.ds(pl.multiple_of(c * rows, rows), rows), :], tab_v)))]
+        (outw.at[:, pl.ds(0, width // 2)], wide[4].at[y, pc.core, z, x]), (outw.at[:, pl.ds(width // 2, width // 4)], wide[5].at[y, pc.core, z, x]),
+        (outw.at[:, pl.ds(width // 4 * 3, width // 4)], w_o2.at[y, pc.core, z, x]), (down, d_slot(s)), (tables.at[:, pl.ds(pl.multiple_of(c * rows, rows), rows), :], tab_v)))]
     for copy in lc: copy.start()
     g1 = g1_ref[...]
     def scaled(first, w): return (qw_ref[:, first : first + w].astype(F32) * g1).astype(BF)
@@ -414,9 +429,9 @@
     row = jnp.where(odd, jnp.concatenate([rest, bias], 1), jnp.concatenate([bias, rest], 1))
     first_row = lax.broadcasted_iota(jnp.int32, (owned, HEAD), 0) == 0
     w_kv[y, pc.core, z, x, :, 2 * KVDIM :] = jnp.where(first_row, row, 0.0).astype(BF)
-    for i, w in enumerate((w_q0, w_q1, w_q2)): w[y, pc.core, z, x] = scaled(i * third, third)
+    for i, w in enumerate(wide[1:4]): w[y, pc.core, z, x] = scaled(i * third, third)
     slot_pos = c * rows + lax.broadcasted_iota(jnp.int32, (rows, width), 0)
-    cot_v[...] = jnp.where(slot_pos < length, og_ref[...].astype(F32), 0.0).astype(BF)
+    cot_v[index[0]] = jnp.where(slot_pos < length, og_ref[...].astype(F32), 0.0).astype(BF)
     enter(pc)
     def gu_turn(t):
         k = s * n + lax.rem(c + n - t, n)
@@ -426,40 +441,38 @@
     for p in (kvs, q0, q1, q2): p.begin()
     send(down, d_slot(s), d_far.at[0], d_recv.at[s], pc.far, c)
     send(down, d_slot(s), d_sib.at[s], d_recv.at[s], pc.sib, c)
-    own_cot = pltpu.make_async_copy(cot_v, cot_all.at[c], local.at[4])
-    own_cot.start()
     xf = x_ref[...].astype(F32)
-    xh_v[...] = (xf * inverse_rms(xf)).astype(BF)
+    att_out[...] = (xf * inverse_rms(xf)).astype(BF)
     g2 = g2_ref[...]
-    place_out(gate_ref, g2, 0, pack_v)
+    place_out(gate_ref, g2, 0, act_v)
     kvs.stage1()
     q0.stage1()
-    place_out(up_ref, g2, 1, pack_v)
+    place_out(up_ref, g2, 1, act_v)
     q1.stage1()
     kvs.stage2()
-    own_gu = pltpu.make_async_copy(pack_v.at[c], g_slot(me), local.at[5])
+    own_gu = pltpu.make_async_copy(pack(c), g_slot(me), local.at[5])
     own_gu.start()
     def feed(d, v):
         to = lax.rem(c + d, n)
-        send(pack_v.at[to], g_slot(me), g_send.at[to], g_recv.at[me], s, to)
+        send(pack(to), g_slot(me), g_send.at[to], g_recv.at[me], s, to)
         return v
     q2.stage1()
     lax.fori_loop(1, n, feed, 0)
     q0.stage2()
     kvs.stage3()
     q1.stage2()
-    lc[0].wait(); lc[1].wait()
-    o0.begin(); o1.begin()
+    for copy in lc[:3]: copy.wait()
+    o0.begin(); o1.begin(); o2.begin()
     q2.stage2()
     q0.stage3()
     q1.stage3()
     q2.stage3()
-    send(pack_v.at[c], g_slot(me), g_far.at[c], g_recv.at[me], pc.far, c)
-    send(pack_v.at[c], g_slot(me), g_sib.at[me], g_recv.at[me], pc.sib, c)
+    send(pack(c), g_slot(me), g_own.at[0], g_recv.at[me], pc.far, c)
+    send(pack(c), g_slot(me), g_own.at[1], g_recv.at[me], pc.sib, c)
     kvs.stage4()
-    lc[3].wait()
+    lc[4].wait()
     tc, ts = tab_v[0], tab_v[1]
-    xh = xh_v[...]
+    xh = att_out[...]
     def bias_of(tile):
         d = 2 * tile
         def part(i):
@@ -475,7 +488,7 @@
     for d in range(1, deep):
         send(own_kv, own_kv, kz_s.at[d], kz_r.at[d], s, 2 * lax.rem(z + d, deep) + x)
     send(own_kv, own_kv, kx_s.at[0], kx_r.at[0], s, xp)
-    o0.stage1(); o1.stage1()
+    o0.stage1(); o1.stage1(); o2.stage1()
     for i, p in enumerate((q0, q1, q2)):
         p.stage4()
         r = product(xh, p.w[...].reshape(owners * owned, third))
@@ -486,8 +499,8 @@
         block = kv_v.at[lax.rem(z + deep - d, deep), x]
         arrived(block, kz_r.at[d], pc)
         send(block, block, kx_s.at[d], kx_r.at[d], s, xp)
-    cring.hop(0, cot_v)
-    o0.stage2(); o1.stage2()
+    cring.hop(0)
+    o0.stage2(); o1.stage2(); o2.stage2()
     saves = [pltpu.make_async_copy(q_v, q_out, save.at[0])]
     for i, (p, first) in enumerate(((kvs, QDIM), (q0, 0), (q1, third), (q2, 2 * third))):
         saves.append(pltpu.make_async_copy(p.w, qkv_all.at[:, :, :, :, :, pl.ds(first, p.w.shape[5])], save.at[1 + i]))
@@ -511,34 +524,47 @@
             return v
         lax.fori_loop(first, first + count, head, 0)
     gu_turn(1); gu_turn(2)
-    o0.stage3(); o1.stage3()
+    o0.stage3(); o1.stage3(); o2.stage3()
     heads(0, GROUP)
     gu_turn(3); gu_turn(4)
     cring.turn(0)
     heads(GROUP, GROUP)
-    gu_turn(5); gu_turn(6); gu_turn(7)
-    o0.stage4(); o1.stage4()
+    gu_turn(5); gu_turn(6)
+    own_gu.wait()
+    for i in range(2): sent(pack(0), g_own.at[i], pc)
+    def fed(d, v):
+        sent(pack(0), g_send.at[lax.rem(c + d, n)], pc)
+        return v
+    lax.fori_loop(1, n, fed, 0)
+    gu_turn(7)
+    o0.stage4(); o1.stage4(); o2.stage4()
     saves2 = [pltpu.make_async_copy(kv_v, kv_all, save.at[5])]
-    for i, p in enumerate((o0, o1)):
-        saves2.append(pltpu.make_async_copy(p.w, out_all.at[:, :, :, :, :, pl.ds(i * ohalf, ohalf)], save.at[6 + i]))
+    for i, (p, first, w) in enumerate(outs):
+        saves2.append(pltpu.make_async_copy(p.w, out_all.at[:, :, :, :, :, pl.ds(first, w)], save.at[6 + i]))
     for copy in saves2: copy.start()
     cring.turn(1)
     att = att_out[...]
-    for i, p in enumerate((o0, o1)):
-        lanes = slice(i * ohalf, (i + 1) * ohalf)
-        mid_out[:, lanes] = x_ref[:, lanes].astype(F32) + product(att, p.w[...].reshape(owners * owned, ohalf))
+    for p, first, w in outs:
+        lanes = slice(first, first + w)
+        mid_out[:, lanes] = x_ref[:, lanes].astype(F32) + product(att, p.w[...].reshape(owners * owned, w))
     mid = mid_out[...]
-    n2_out[...] = (mid * inverse_rms(mid)).astype(BF)
+    n2_v[index[0]] = (mid * inverse_rms(mid)).astype(BF)
+    nring.hop(0)
     cring.turn(2)
     arrived(d_slot(pc.far), d_recv.at[pc.far], pc)
     send(d_slot(pc.far), d_slot(pc.far), d_sib.at[pc.far], d_recv.at[pc.far], pc.sib, c)
-    def across(t, v):
+    def across(t):
         k = pc.far * n + lax.rem(c + n - t, n)
         arrived(g_slot(k), g_recv.at[k], pc)
         send(g_slot(k), g_slot(k), g_sib.at[k], g_recv.at[k], pc.sib, c)
-        return v
-    lax.fori_loop(0, n, across, 0)
-    cring.turn(3)
+    for t in range(n):
+        if t == n - 1:
+            for copy in saves + saves2: copy.wait()
+            for p in spreads: p.finish()
+        across(t)
+        if t == 1: nring.turn(0)
+        if t == 3: cring.turn(3)
+        if t == 4: nring.turn(1)
     for plane in range(2):
         other = 2 * plane + 1 - pc.core
         arrived(d_slot(other), d_recv.at[other], pc)
@@ -547,79 +573,8 @@
             arrived(g_slot(i), g_recv.at[i], pc)
             return v
         lax.fori_loop(0, n, come, 0)
-    for copy in [lc[2], own_cot, own_gu] + saves + saves2: copy.wait()
-    for p in spreads: p.finish()
-    cring.finish()
-    for d in range(1, deep): sent(own_kv, kz_s.at[d], pc)
-    for d in range(deep): sent(own_kv, kx_s.at[d], pc)
-    sent(down, d_far.at[0], pc)
-    block = pack_v.at[0]
-    for plane in range(2):
-        own = 2 * plane + pc.core
-        sent(down, d_sib.at[own], pc)
-        def tail(t, v):
-            sent(block, g_sib.at[own * n + t], pc)
-            return v
-        lax.fori_loop(0, n, tail, 0)
-    def tail2(t, v):
-        src = lax.rem(c + t, n)
-        sent(block, g_far.at[src], pc)
-        @pl.when(t > 0)
-        def _():
-            sent(block, g_send.at[src], pc)
-        return v
-    lax.fori_loop(0, n, tail2, 0)
-
-def forward_call(n, length, x, og, qkv, gain_one, bias, gate, up, gain_two, outw, down, tables):
-    N, m = 4 * n, n // 2
-    rows, width = x.shape
-    owned, piece = qkv.shape[0], down.shape[0]
-    chunk = 4 * piece
-    S, V = jax.ShapeDtypeStruct, pltpu.VMEM
-    joint = QDIM + 2 * KVDIM + HEAD
-    shapes = [S((2, N * owned, chunk), BF), S((4 * piece, width), BF), S((n, rows, width), BF),
-              S((2, 2, m, 2, owned, joint), BF), S((2, 2, m, 2, owned, width), BF), S((m, 2, rows, 2 * KVDIM), BF),
-              S((HEADS, rows, HEAD), BF), S((rows, QDIM), BF), S((rows, width), F32), S((rows, width), BF)]
-    anys = pl.BlockSpec(memory_space=pl.ANY)
-    vmem = pl.BlockSpec(memory_space=pltpu.VMEM)
-    scratch = [V((2, 2, m, 2, owned, w), BF) for w in (2 * KVDIM + HEAD,) + (QDIM // 3,) * 3 + (width // 2,) * 2]
-    scratch += [V((rows, width), BF), V((rows, width), BF), V((m, 2, rows, 2 * KVDIM), BF), V((HEADS, rows, HEAD), BF),
-                V((2, rows, HEAD), F32), V((n, 2, owned, chunk), BF),
-                DMA((6,)), DMA((8,)), DMA((6, m + 5)), DMA((6, m + 5)), DMA((N,)), DMA((n,)), DMA((n,)), DMA((N,)),
-                DMA((4,)), DMA((1,)), DMA((4,)), DMA((2, m)), DMA((2, m)), DMA((m,)), DMA((m,)), DMA((m,)), DMA((m,))]
-    return pl.pallas_call(
-        functools.partial(forward_kernel, n),
-        out_shape=shapes,
-        in_specs=[pl.BlockSpec(memory_space=pltpu.SMEM)] + [vmem] * 9 + [anys] * 2,
-        out_specs=[anys] * 7 + [vmem] * 3,
-        scratch_shapes=scratch,
-        compiler_params=pltpu.CompilerParams(collective_id=0, has_side_effects=True, vmem_limit_bytes=56 * 2**20),
-    )(length, x, og, qkv, gain_one, bias, gate, up, gain_two, down, outw, tables)
-
-
-def ffn_kernel(n, n2_ref, gu_all, down_all, cot_all, u_own, o_own, gsum, ddown,
-               gu_v, down_v, cot_v, n2_v, act_v, gg_v, gp_v, ut, uhh, uh, ot, ohh, oh, dgu_v, dd_v, r0g, r1g, r0d, r1d,
-               load, rows_in, n_recv, n_send, u_recv, u_send, o_recv, o_send, gs0, gr0, gs1, gr1, save, ds0, dr0, ds1, dr1):
-    pc = Place(n)
-    s, c = pc.s, pc.c
-    _, rows, width = cot_all.shape
-    chunk = gu_all.shape[2]
-    pairs = n // 2
-    weights = [pltpu.make_async_copy(gu_all, gu_v, load.at[0]), pltpu.make_async_copy(down_all, down_v, load.at[1])]
-    offsets = [o for j in range(1, pairs) for o in (-j, j)] + [pairs, 0]
-    index = {o: i for i, o in enumerate(offsets)}
-    index[-pairs] = index[pairs]
-    fetch = [pltpu.make_async_copy(cot_all.at[pc.at(o)], cot_v.at[i], rows_in.at[i]) for i, o in enumerate(offsets)]
-    for w in weights: w.start()
-    for f in fetch: f.start()
-    n2_v[index[0]] = n2_ref[...]
-    nring = RingGather(pc, n2_v, n_send, n_recv, index)
-    uring = RingSum(pc, ut, index, uhh, uh, u_send, u_recv, u_own)
-    oring = RingSum(pc, ot, index, ohh, oh, o_send, o_recv, o_own)
-    enter(pc)
-    nring.hop(0)
-    for w in weights: w.wait()
-    tall = 2 * rows
+    lc[3].wait()
+    tall, chunk = 2 * rows, gu_v.shape[2]
     def forward(j):
         pair = slice(2 * j, 2 * j + 2)
         normed = n2_v[pair].reshape(tall, width)
@@ -628,7 +583,7 @@
         sig = jax.nn.sigmoid(gate)
         gs = gate * sig
         act = (gs * up).astype(BF)
-        act_v[pair] = act.reshape(2, rows, chunk)
+        act_v[pair] = act.reshape(2, 2, rows // 2, chunk)
         gp_v[pair] = gs.astype(BF).reshape(2, rows, chunk)
         gg_v[pair] = (up * (sig + gs * (1.0 - sig))).astype(BF).reshape(2, rows, chunk)
         ot[pair] = product(act, down_v[...]).astype(BF).reshape(2, rows, width)
@@ -642,9 +597,8 @@
         ut[pair] = (contract_cols(gg, gu_v[0]) + contract_cols(gp, gu_v[1])).astype(BF).reshape(2, rows, width)
 
     all_rows = n * rows
-    plane = gu_all.shape[1] // 4
-    piece = down_all.shape[0] // 4
-    core, y = pc.core, s // 2
+    plane = n * owned
+    core = pc.core
     tile = 384
     def cols_of(j): return pl.ds(j * tile, tile)
     wide_pieces = [(0, j, a) for j in range(chunk // tile) for a in range(2)]
@@ -654,8 +608,8 @@
         if kind == 0:
             lhs, rhs = n2_v[...].reshape(all_rows, width), (gg_v, gp_v)[a]
             grad = contract_rows(lhs, rhs[:, :, cols_of(j)].reshape(all_rows, tile))
-            dgu_v[a, :, :, :, cols_of(j)] = grad.astype(BF).reshape(2, 2, plane, tile)
-            send(dgu_v.at[a, :, 1 - core, :, cols_of(j)], r0g.at[a, :, :, cols_of(j)],
+            dgu_v[a, :, :, :, :, :, cols_of(j)] = grad.astype(BF).reshape(2, 2, deep, 2, owned, tile)
+            send(dgu_v.at[a, :, 1 - core, :, :, :, cols_of(j)], r0g.at[a, :, :, :, :, cols_of(j)],
                  gs0.at[a, j], gr0.at[a, j], pc.sib, c)
         else:
             grad = contract_rows(act_v[...].reshape(all_rows, chunk), cot_v[:, :, cols_of(j)].reshape(all_rows, tile))
@@ -665,32 +619,32 @@
         kind, j, a = p
         cols = cols_of(j)
         if kind == 0:
-            arrived(r0g.at[a, :, :, cols], gr0.at[a, j], pc)
+            arrived(r0g.at[a, :, :, :, :, cols], gr0.at[a, j], pc)
             for k in range(2):
-                r0g[a, k, :, cols] = add_low(r0g[a, k, :, cols], dgu_v[a, k, core, :, cols])
-            send(r0g.at[a, 1 - y, :, cols], r1g.at[a, :, cols], gs1.at[a, j], gr1.at[a, j], pc.far, c)
+                r0g[a, k, :, :, :, cols] = add_low(r0g[a, k, :, :, :, cols], dgu_v[a, k, core, :, :, :, cols])
+            copy = pltpu.make_async_copy(r0g.at[a, :, :, :, :, cols], half_sum.at[a, :, :, :, :, cols], gsave.at[a, j])
+            copy.start()
+            saves.append(copy)
         else:
             arrived(r0d.at[:, :, cols], dr0.at[j], pc)
             for k in range(2):
                 r0d[k, :, cols] = add_low(r0d[k, :, cols], dd_v[k, core, :, cols])
             send(r0d.at[1 - y, :, cols], r1d.at[:, cols], ds1.at[j], dr1.at[j], pc.far, c)
-    saves = []
     def add_far(p):
-        kind, j, a = p
+        _, j, _ = p
         cols = cols_of(j)
-        if kind == 0:
-            arrived(r1g.at[a, :, cols], gr1.at[a, j], pc)
-            r1g[a, :, cols] = add_low(r1g[a, :, cols], r0g[a, y, :, cols])
-            copy = pltpu.make_async_copy(r1g.at[a, :, cols], gsum.at[a, :, cols], save.at[a, j])
-            copy.start()
-            saves.append(copy)
-        else:
-            arrived(r1d.at[:, cols], dr1.at[j], pc)
-            ddown[:, cols] = r1d[:, cols].astype(F32) + r0d[y, :, cols].astype(F32)
-    for j in range(pairs):
-        nring.turn(j)
-        forward(j)
-    for f in fetch: f.wait()
+        arrived(r1d.at[:, cols], dr1.at[j], pc)
+        r1d[:, cols] = add_low(r1d[:, cols], r0d[y, :, cols])
+        copy = pltpu.make_async_copy(r1d.at[:, cols], dsum.at[:, cols], dsave.at[j])
+        copy.start()
+        saves.append(copy)
+    saves.clear()
+    forward(0)
+    nring.turn(2)
+    forward(1)
+    nring.turn(3)
+    forward(2)
+    forward(3)
     backward(3)
     uring.turn(0)
     oring.turn(0)
@@ -708,23 +662,20 @@
     backward(0)
     uring.turn(3)
     add_core(down_pieces[3])
-    oring.turn(1)
     for i, p in enumerate(wide_pieces):
         compute(p)
         if i: add_core(wide_pieces[i - 1])
+        if i == 0: oring.turn(1)
+        if i == 3: uring.turn(4)
+        if i == 4: oring.turn(2)
     add_core(wide_pieces[-1])
-    uring.turn(4)
-    oring.turn(2)
     for p in down_pieces: add_far(p)
-    for i, p in enumerate(wide_pieces):
-        add_far(p)
-        if i == 1: oring.turn(3)
+    oring.turn(3)
     oring.turn(4)
     for kind, j, a in wide_pieces + down_pieces:
         cols = cols_of(j)
         if kind == 0:
-            sent(r0g.at[a, :, :, cols], gs0.at[a, j], pc)
-            sent(r1g.at[a, :, cols], gs1.at[a, j], pc)
+            sent(r0g.at[a, :, :, :, :, cols], gs0.at[a, j], pc)
         else:
             sent(r0d.at[:, :, cols], ds0.at[j], pc)
             sent(r1d.at[:, cols], ds1.at[j], pc)
@@ -732,29 +683,55 @@
     nring.finish()
     uring.finish()
     oring.finish()
-
-def ffn_call(n, n2, gu_all, down_all, cot_all):
+    cring.finish()
+    for d in range(1, deep): sent(own_kv, kz_s.at[d], pc)
+    for d in range(deep): sent(own_kv, kx_s.at[d], pc)
+    sent(down, d_far.at[0], pc)
+    def left(t, v):
+        sent(g_slot(0), g_sib.at[pc.far * n + t], pc)
+        @pl.when(t > 0)
+        def _():
+            src = lax.rem(c + t, n)
+            sent(g_slot(0), g_far.at[src], pc)
+            sent(g_slot(0), g_sib.at[s * n + src], pc)
+        return v
+    lax.fori_loop(0, n, left, 0)
+    sent(down, d_sib.at[s], pc)
+    sent(down, d_sib.at[pc.far], pc)
+
+def layer_call(n, length, x, og, qkv, gain_one, bias, gate, up, gain_two, down, outw, tables):
+    N, m = 4 * n, n // 2
+    rows, width = x.shape
+    owned, piece = qkv.shape[0], down.shape[0]
+    chunk = 4 * piece
     S, V = jax.ShapeDtypeStruct, pltpu.VMEM
-    _, rows, width = cot_all.shape
-    chunk = gu_all.shape[2]
-    plane, piece = gu_all.shape[1] // 4, down_all.shape[0] // 4
-    a, b = chunk // 384, width // 384
+    joint = QDIM + 2 * KVDIM + HEAD
+    shapes = [S((2, 2, m, 2, owned, joint), BF), S((2, 2, m, 2, owned, width), BF), S((m, 2, rows, 2 * KVDIM), BF),
+              S((HEADS, rows, HEAD), BF), S((2, 2, m, 2, owned, chunk), BF), S((piece, width), BF),
+              S((rows, QDIM), BF), S((rows, width), F32), S((rows, width), F32), S((rows, width), F32)]
     anys = pl.BlockSpec(memory_space=pl.ANY)
     vmem = pl.BlockSpec(memory_space=pltpu.VMEM)
-    held = [V((2, rows, width // 2), BF), V((2, n // 2 - 1, rows, width), BF)]
+    all_rows = V((n, rows, width), BF)
+    hidden = V((n, rows, chunk), BF)
+    scratch = [V((2, N * owned, chunk), BF), V((4 * piece, width), BF), all_rows, all_rows, V((n, 2, rows // 2, chunk), BF), hidden, hidden,
+               all_rows, V((2, rows, width // 2), BF), V((2, n // 2 - 1, rows, width), BF),
+               all_rows, V((2, rows, width // 2), BF), V((2, n // 2 - 1, rows, width), BF),
+               V((2, 2, 2, m, 2, owned, chunk), BF), V((2, 2, piece, width), BF), V((2, 2, m, 2, owned, chunk), BF),
+               V((2, piece, width), BF), V((piece, width), BF),
+               V((2, 2, m, 2, owned, width // 4), BF),
+               V((m, 2, rows, 2 * KVDIM), BF), V((HEADS, rows, HEAD), BF), V((2, rows, HEAD), F32)]
+    a, b = chunk // 384, width // 384
+    scratch += [DMA((6,)), DMA((9,)), DMA((7, m + 5)), DMA((7, m + 5)), DMA((N,)), DMA((n,)), DMA((2,)), DMA((n,)), DMA((N,)),
+                DMA((4,)), DMA((1,)), DMA((4,)), DMA((2, m)), DMA((2, m)), DMA((m,)), DMA((m,)), DMA((m,)), DMA((m,))]
+    scratch += [DMA((2, m))] * 6 + [DMA((2, a))] * 3 + [DMA((b,))] * 5
     return pl.pallas_call(
-        functools.partial(ffn_kernel, n),
-        out_shape=[S((rows, width), F32), S((rows, width), F32), S((2, plane, chunk), BF), S((piece, width), F32)],
-        in_specs=[vmem] + [anys] * 3,
-        out_specs=[vmem, vmem, anys, vmem],
-        scratch_shapes=[V(gu_all.shape, BF), V(down_all.shape, BF), V(cot_all.shape, BF), V(cot_all.shape, BF)]
-        + [V((n, rows, chunk), BF)] * 3 + [V((n, rows, width), BF)] + held + [V((n, rows, width), BF)] + held
-        + [V((2, 2, 2, plane, chunk), BF), V((2, 2, piece, width), BF), V((2, 2, plane, chunk), BF), V((2, plane, chunk), BF),
-           V((2, piece, width), BF), V((piece, width), BF)]
-        + [DMA((2,)), DMA((n,))] + [DMA((2, n // 2))] * 6
-        + [DMA((2, a))] * 5 + [DMA((b,))] * 4,
-        compiler_params=pltpu.CompilerParams(collective_id=1, has_side_effects=True, vmem_limit_bytes=63 * 2**20),
-    )(n2, gu_all, down_all, cot_all)
+        functools.partial(layer_kernel, n),
+        out_shape=shapes,
+        in_specs=[pl.BlockSpec(memory_space=pltpu.SMEM)] + [vmem] * 9 + [anys] * 2,
+        out_specs=[anys] * 6 + [vmem] * 4,
+        scratch_shapes=scratch,
+        compiler_params=pltpu.CompilerParams(collective_id=0, has_side_effects=True, vmem_limit_bytes=63 * 2**20),
+    )(length, x, og, qkv, gain_one, bias, gate, up, gain_two, down, outw, tables)
 
 
 class Reduce:
@@ -809,11 +786,11 @@
         for d in range(1, self.pc.n // 2):
             sent(self.r2.at[0], self.ss.at[self.i, 2 + d], self.pc)
 
-def backward_kernel(n, length_ref, x_ref, og_ref, mid_ref, u_ref, o_ref, att_ref, q_ref, kv_ref, qkv_ref, out_ref, gate_ref, up_ref, gain_ref, tables, gsum,
+def backward_kernel(n, length_ref, x_ref, og_ref, mid_ref, u_ref, o_ref, att_ref, q_ref, kv_ref, qkv_ref, out_ref, gate_ref, up_ref, gain_ref, tables, half_sum,
                     y_out, dx_out, dout_out, dqkv_out, dgate_out, dup_out, dgain_out,
-                    tab_v, gm_v, gb_v, dm_v, gp_v, p_v, gs_v, dkv_v, kx, kz, raw_v, *rest):
+                    tab_v, gm_v, gb_v, dm_v, gp_v, p_v, gs_v, dkv_v, kx, kz, raw_v, r1_v, mine_v, *rest):
     pieces = 6
-    bufs, (local, kxs, kxr, kzs, kzr, gss, grs, ss, rs) = rest[: 5 * pieces], rest[5 * pieces :]
+    bufs, (local, kxs, kxr, kzs, kzr, gss, grs, fs, fr, ss, rs) = rest[: 5 * pieces], rest[5 * pieces :]
     pc = Place(n)
     s, c = pc.s, pc.c
     rows, width = x_ref.shape
@@ -824,15 +801,32 @@
     red = [Reduce(pc, i % 2 == 0, *bufs[5 * i : 5 * i + 5], ss, rs, i) for i in range(pieces)]
     tab = pltpu.make_async_copy(tables.at[:, pl.ds(pl.multiple_of(c * rows, rows), rows), :], tab_v, local.at[0])
     tab.start()
+    y = s // 2
+    mine = pltpu.make_async_copy(half_sum.at[:, y], mine_v, local.at[1])
+    mine.start()
     enter(pc)
     owned = out_ref.shape[1]
-    def g_rows(i): return gsum.at[:, pl.ds(pl.multiple_of(i * owned, owned), owned), :]
-    own_raw = pltpu.make_async_copy(g_rows(c), raw_v.at[c], local.at[1])
-    own_raw.start()
-    def feed(d, w):
-        to = lax.rem(c + d, n)
-        send(g_rows(to), raw_v.at[c], gss.at[to], grs.at[c], s, to)
-        return w
+    def cross(a):
+        send(half_sum.at[a, 1 - y], r1_v.at[a], fs.at[a], fr.at[a], pc.far, c)
+    def feed(a):
+        arrived(r1_v.at[a], fr.at[a], pc)
+        if a == 0:
+            cross(1)
+            mine.wait()
+        r1_v[a] = add_low(r1_v[a], mine_v[a])
+        def hand(d, w):
+            to = lax.rem(c + d, n)
+            send(r1_v.at[a, to // 2, lax.rem(to, 2)], raw_v.at[c, a], gss.at[a, to], grs.at[a, c], s, to)
+            return w
+        lax.fori_loop(1, n, hand, 0)
+        raw_v[c, a] = r1_v[a, c // 2, lax.rem(c, 2)]
+    def fed(a):
+        def come(d, w):
+            src = lax.rem(c + d, n)
+            arrived(raw_v.at[src, a], grs.at[a, src], pc)
+            return w
+        lax.fori_loop(1, n, come, 0)
+    cross(0)
     pos = c * rows + lax.broadcasted_iota(jnp.int32, (rows, width), 0)
     live = pos < length
     mid = mid_ref[...]
@@ -854,7 +848,6 @@
         grad = contract_rows(att_ref[...], gb[:, i * w : (i + 1) * w])
         red[i].p[...] = grad.astype(BF).reshape(red[i].p.shape)
         red[i].stage0()
-    lax.fori_loop(1, n, feed, 0)
     tab.wait()
     tc, ts = tab_v[0], tab_v[1]
 
@@ -912,6 +905,7 @@
         red[i].p[..., :w] = grad.reshape(shape)
     group(0)
     red[0].stage1(); red[1].stage1()
+    feed(0)
     group(1)
     kv_x(0)
     red[0].stage2(); red[1].stage2()
@@ -922,6 +916,7 @@
         if i == 0: kv_x(1)
     red[0].stage3(); red[1].stage3()
     red[2].stage1(); red[3].stage1(); red[4].stage1()
+    feed(1)
     kv_z(0); kv_z(1)
     joint(5, QDIM, 2 * KVDIM)
     sums = jnp.sum(gp_v[...].astype(F32), axis=0, keepdims=True)
@@ -948,17 +943,13 @@
     lax.fori_loop(0, owners // 8, back, 0)
     red[2].stage3(); red[3].stage3(); red[4].stage3()
     red[5].stage2()
-    own_raw.wait()
-    def fed(d, w):
-        src = lax.rem(c + d, n)
-        arrived(raw_v.at[src], grs.at[src], pc)
-        return w
-    lax.fori_loop(1, n, fed, 0)
+    fed(0)
     place_back(raw_v, 0, dgate_out)
     dx_out[...] = gm_v[...] + rms_back(x_ref[...].astype(F32), inverse, dx_out[...])
     for i in range(2):
         dout_out[:, i * (width // 2) : (i + 1) * (width // 2)] = red[i].stage4()
     red[5].stage3()
+    fed(1)
     place_back(raw_v, 1, dup_out)
     gain = gain_ref[...]
     dgain_out[...] = jnp.sum(
@@ -970,16 +961,18 @@
         dqkv_out[:, i * third : (i + 1) * third] = red[2 + i].stage4()
     dqkv_out[:, QDIM:] = red[5].stage4()
     for r in red: r.finish()
-    def fed_out(d, w):
-        sent(raw_v.at[0], gss.at[lax.rem(c + d, n)], pc)
-        return w
-    lax.fori_loop(1, n, fed_out, 0)
+    for a in range(2):
+        sent(r1_v.at[a], fs.at[a], pc)
+        def left(d, w):
+            sent(raw_v.at[0, a], gss.at[a, lax.rem(c + d, n)], pc)
+            return w
+        lax.fori_loop(1, n, left, 0)
     for g in range(2):
         lanes = slice(g * 2 * HEAD, g * 2 * HEAD + 2 * HEAD)
         sent(kx.at[:, :, lanes], kxs.at[g], pc)
         for d in range(1, n // 2): sent(kx.at[0, :, lanes], kzs.at[g, d], pc)
 
-def backward_call(n, length, x, og, mid, u, o, att, q, kv, qkv_all, out_all, gate, up, gain, tables, gsum):
+def backward_call(n, length, x, og, mid, u, o, att, q, kv, qkv_all, out_all, gate, up, gain, tables, half_sum):
     S, V = jax.ShapeDtypeStruct, pltpu.VMEM
     rows, width = x.shape
     owned = qkv_all.shape[1]
@@ -989,11 +982,11 @@
     scratch = [V((2, rows, HEAD), F32), V((rows, width), F32), V((rows, width), BF), V((HEADS, rows, HEAD), BF),
                V((rows, QDIM + 2 * KVDIM), BF), V((GROUP * rows, n * rows), BF), V((GROUP * rows, n * rows), BF),
                V((m, 2, rows, 2 * KVDIM), BF), V((m, rows, 2 * KVDIM), BF), V((m, rows, 2 * KVDIM), BF),
-               V((n, 2, owned, gsum.shape[2]), BF)]
+               V((n, 2, owned, half_sum.shape[-1]), BF), V((2,) + half_sum.shape[2:], BF), V((2,) + half_sum.shape[2:], BF)]
     for i, w in enumerate((width // 2, width // 2, QDIM // 3, QDIM // 3, QDIM // 3, 2 * KVDIM + HEAD)):
         one = (m, 2, owned, w) if i % 2 == 0 else (2, m, owned, w)
         scratch += [V((2, 2, m, 2, owned, w), BF), V((2, m, 2, owned, w), BF), V(one, BF), V((m, owned, w), BF), V((m, owned, w), BF)]
-    scratch += [DMA((2,)), DMA((2,)), DMA((2,)), DMA((2, m)), DMA((2, m)), DMA((n,)), DMA((n,)), DMA((6, 2 + m)), DMA((6, 2 + m))]
+    scratch += [DMA((2,)), DMA((2,)), DMA((2,)), DMA((2, m)), DMA((2, m)), DMA((2, n)), DMA((2, n)), DMA((2,)), DMA((2,)), DMA((6, 2 + m)), DMA((6, 2 + m))]
     return pl.pallas_call(
         functools.partial(backward_kernel, n),
         out_shape=[S((rows, width), BF), S((rows, width), F32), S((owned, width), F32), S((owned, qkv_all.shape[2]), F32),
@@ -1002,7 +995,7 @@
         out_specs=[vmem] * 7,
         scratch_shapes=scratch,
         compiler_params=pltpu.CompilerParams(collective_id=2, has_side_effects=True, vmem_limit_bytes=62 * 2**20),
-    )(length, x, og, mid, u, o, att, q, kv, qkv_all, out_all, gate, up, gain, tables, gsum)
+    )(length, x, og, mid, u, o, att, q, kv, qkv_all, out_all, gate, up, gain, tables, half_sum)
 
 
 def kernel_shards(
@@ -1034,16 +1027,15 @@
     tables = jnp.asarray(np.stack([np.concatenate([cosine, cosine], 1), np.concatenate([-sine, sine], 1)]), F32)
     down = jnp.pad(down_weight, ((0, padded - piece), (0, 0)))
     x, og = tokens[0], out_grad[0]
-    gu_all, down_all, cot_all, qkv_all, out_all, kv_all, q, att, mid, n2 = forward_call(
+    qkv_all, out_all, kv_all, q, half_sum, grad_down, att, mid, u, o = layer_call(
         parts, lengths, x, og, qkv_weight, gain_one, qkv_bias[None], gate_weight, up_weight, gain_two,
-        out_weight, down, tables,
+        down, out_weight, tables,
     )
-    u, o, gate_up_sum, grad_down = ffn_call(parts, n2, gu_all, down_all, cot_all)
     joint = qkv_all.shape[-1]
     output, grad_inputs, grad_out, raw_qkv, grad_gate, grad_up, grad_mlp_gain = backward_call(
         parts, lengths, x, og, mid, u, o, att, q, kv_all.reshape(parts, rows, 2 * KVDIM),
         qkv_all.reshape(owners, owned, joint), out_all.reshape(owners, owned, width),
-        gate_weight, up_weight, gain_two, tables, gate_up_sum,
+        gate_weight, up_weight, gain_two, tables, half_sum,
     )
     qk = QDIM + 2 * KVDIM
     bias_rows, raw_qkv = raw_qkv[:3, qk:], raw_qkv[:, :qk]
@@ -1061,7 +1053,7 @@
         grad_mlp_gain[:, 0],
         grad_gate,
         grad_up,
-        grad_down[:piece],
+        grad_down[:piece].astype(F32),
         grad_value_bias,
     )
 

time: 411 us -> 394 us (0.959)
  Pallas kernels: 386 us -> 369 us
    pallas_call x2 -> x1, Pallas kernels: 274 us -> 252 us  [layer_call(): pl.pallas_call(functools.partial(layer_kernel, n), out_shape=shapes, in_s...]
    pallas_call x1, Pallas kernels: 112 us -> 117 us  [backward_call(): pl.pallas_call(functools.partial(backward_kernel, n), out_shape=[S((rows,...]
where the time goes in v4:
time: 394 us; the launch traced here: 389 us
  Pallas kernels  369 us (94%)
  local copies, waits for them, and re-layouts  10.8 us (3%)
  other arithmetic  7.84 us (2%)
    pallas_call x1, Pallas kernels, layer_call(): pl.pallas_call(functools.partial(layer_kernel, n), out_shape=shapes, in_s...  252 us
    pallas_call x1, Pallas kernels, backward_call(): pl.pallas_call(functools.partial(backward_kernel, n), out_shape=[S((rows,...  117 us

profile of v4, /device:TPU:0, one launch (start us, length us, event | category | flops | bytes accessed | tf_op | source)
XLA Modules:
  0.0 389.0 jit_solution(13058682556193644758)
XLA Ops:
  0.6 0.7 fusion
  1.3 0.7 copy.26.g1_ref
  2.0 0.7 bitcast_convert_fusion
  2.7 0.7 copy.27.g2_ref.gain_ref
  4.0 2.1 pad.4.down
  6.1 251.9 %shard_map.203 = (bf16[2,2,4,2,48,2176]{5,4,3,2,1,0:T(8,128)(2,1)}, bf16[2,2,4,2,48,1536]{5,4,3,2,1,0:T(8,128)(2,1)}, bf16[4,2,128,512]{3,2,1,0:T(8,128)(2,1)}, ...) custom-call(s32[1]{0:T(128)S(6)} %copy.33.length_ref, ...), custom_call_target="tpu_custom_call" | custom-call | tf_op jit(solution)/shard_map/pallas_call | solution.py:727
  258.1 0.0 copy-start.3
  258.1 116.8 %shard_map.204 = (bf16[128,1536]{1,0:T(8,128)(2,1)}, f32[128,1536]{1,0:T(8,128)}, f32[48,1536]{1,0:T(8,128)}, f32[48,2176]{1,0:T(8,128)}, f32[48,8960]{1,0:T(8,1...) custom-call(s32[1]{0:T(128)S(6)} %copy.33.length_ref, bf16[128,1536]{1,0:T(8,128)(2,1)} %bitcast.21, ...), custom_call_target="tpu_custom_call" | custom-call | tf_op jit(solution)/shard_map/pallas_call | solution.py:990
  374.9 0.0 copy-start.6
  374.9 0.0 copy-start.2
  374.9 0.0 copy-done.3
  374.9 2.5 slice_multiply_fusion
  377.5 2.0 convert_bitcast_fusion
  379.4 0.7 slice_bitcast_fusion
  380.1 0.6 dynamic_slice.8
  380.7 0.7 slice.18
  381.4 0.6 dynamic-slice_bitcast_fusion
  382.0 0.6 reduce
  382.6 1.4 slice_convert_fusion
  384.0 0.7 copy.34
  384.8 0.7 copy.35
  385.5 1.2 copy.36
  386.7 0.9 copy-done
  387.6 1.2 copy.37
  (9 shorter events, 0.0 us)
Async XLA Ops:
  258.1 116.8 %copy-start.3 = (bf16[48,2048]{1,0:T(8,128)(2,1)S(1)}, bf16[48,2048]{1,0:T(8,128)(2,1)}, u32[]{:S(2)}) copy-start(bf16[48,2048]{1,0:T(8,128)(2,1)} %qw_ref.1) | copy-start | bytes 589828
  374.9 7.1 %copy-start.6 = (f32[48,1]{1,0:T(8,128)S(1)}, f32[48,1]{1,0:T(8,128)}, u32[]{:S(2)}) copy-start(f32[48,1]{1,0:T(8,128)} %get-tuple-element.41) | copy-start | bytes 580
  374.9 7.7 %copy-start.2 = (bf16[288,1536]{1,0:T(8,128)(2,1)S(1)}, bf16[288,1536]{1,0:T(8,128)(2,1)}, u32[]{:S(2)}) copy-start(bf16[288,1536]{1,0:T(8,128)(2,1)} %get-tuple-element.44) | copy-start | bytes 2654212
  377.5 6.5 %copy-start.4 = (bf16[128,1536]{1,0:T(8,128)(2,1)S(1)}, bf16[128,1536]{1,0:T(8,128)(2,1)}, u32[]{:S(2)}) copy-start(bf16[128,1536]{1,0:T(8,128)(2,1)} %get-tuple-element.37) | copy-start | bytes 1179652
  380.1 4.6 %copy-start.5 = (f32[48,1536]{1,0:T(8,128)S(1)}, f32[48,1536]{1,0:T(8,128)}, u32[]{:S(2)}) copy-start(f32[48,1536]{1,0:T(8,128)} %get-tuple-element.65) | copy-start | bytes 884740
  382.6 2.9 copy-start.1
  385.5 2.1 copy-start

commit v5 on v4

--- a/solution.py
+++ b/solution.py
@@ -236,6 +236,15 @@
 
 def add_low(left, right):
     return (left.astype(F32) + right.astype(F32)).astype(BF)
+
+def diagonal(n):
+    return lax.broadcasted_iota(jnp.int32, (n, n), 0) == lax.broadcasted_iota(jnp.int32, (n, n), 1)
+
+def column(row):
+    return jnp.sum(jnp.where(diagonal(row.shape[1]), row.astype(F32), 0.0), axis=1, keepdims=True)
+
+def as_row(values):
+    return jnp.sum(jnp.where(diagonal(values.shape[0]), values, 0.0), axis=0, keepdims=True)
 
 class RingGather:
     def __init__(self, pc, slots, ssem, rsem, index=None):
@@ -391,7 +400,7 @@
     me, s, c = pc.me, pc.s, pc.c
     y, x, z, xp = s // 2, lax.rem(c, 2), c // 2, c + 1 - 2 * lax.rem(c, 2)
     rows, width = x_ref.shape
-    owned, piece = qw_ref.shape[0], down.shape[0]
+    owned, piece = qw_ref.shape[0], down_v.shape[0] // 4
     length = length_ref[0]
     third, owners, deep = QDIM // 3, 4 * n, n // 2
 
@@ -417,9 +426,9 @@
     oring = RingSum(pc, ot, index, ohh, oh, o_send_, o_recv_, o_own)
     lc = [pltpu.make_async_copy(a, b, local.at[i]) for i, (a, b) in enumerate((
         (outw.at[:, pl.ds(0, width // 2)], wide[4].at[y, pc.core, z, x]), (outw.at[:, pl.ds(width // 2, width // 4)], wide[5].at[y, pc.core, z, x]),
-        (outw.at[:, pl.ds(width // 4 * 3, width // 4)], w_o2.at[y, pc.core, z, x]), (down, d_slot(s)), (tables.at[:, pl.ds(pl.multiple_of(c * rows, rows), rows), :], tab_v)))]
+        (outw.at[:, pl.ds(width // 4 * 3, width // 4)], w_o2.at[y, pc.core, z, x]), (tables.at[:, pl.ds(pl.multiple_of(c * rows, rows), rows), :], tab_v)))]
     for copy in lc: copy.start()
-    g1 = g1_ref[...]
+    g1 = column(g1_ref[...])
     def scaled(first, w): return (qw_ref[:, first : first + w].astype(F32) * g1).astype(BF)
     w_kv[y, pc.core, z, x, :, : 2 * KVDIM] = scaled(QDIM, 2 * KVDIM)
     share = b_ref.shape[1]
@@ -432,6 +441,12 @@
     for i, w in enumerate(wide[1:4]): w[y, pc.core, z, x] = scaled(i * third, third)
     slot_pos = c * rows + lax.broadcasted_iota(jnp.int32, (rows, width), 0)
     cot_v[index[0]] = jnp.where(slot_pos < length, og_ref[...].astype(F32), 0.0).astype(BF)
+    g2 = column(g2_ref[...])
+    place_out(gate_ref, g2, 0, act_v)
+    place_out(up_ref, g2, 1, act_v)
+    short = down[...].astype(F32)
+    padding = jnp.zeros((piece - short.shape[0], width), F32)
+    down_v[pl.ds(pl.multiple_of(s * piece, piece), piece), :] = jnp.concatenate([short, padding], 0).astype(BF)
     enter(pc)
     def gu_turn(t):
         k = s * n + lax.rem(c + n - t, n)
@@ -439,25 +454,22 @@
         send(g_slot(k), g_slot(k), g_far.at[lax.rem(c + n - t, n)], g_recv.at[k], pc.far, c)
         send(g_slot(k), g_slot(k), g_sib.at[k], g_recv.at[k], pc.sib, c)
     for p in (kvs, q0, q1, q2): p.begin()
-    send(down, d_slot(s), d_far.at[0], d_recv.at[s], pc.far, c)
-    send(down, d_slot(s), d_sib.at[s], d_recv.at[s], pc.sib, c)
-    xf = x_ref[...].astype(F32)
-    att_out[...] = (xf * inverse_rms(xf)).astype(BF)
-    g2 = g2_ref[...]
-    place_out(gate_ref, g2, 0, act_v)
-    kvs.stage1()
-    q0.stage1()
-    place_out(up_ref, g2, 1, act_v)
-    q1.stage1()
-    kvs.stage2()
     own_gu = pltpu.make_async_copy(pack(c), g_slot(me), local.at[5])
     own_gu.start()
     def feed(d, v):
         to = lax.rem(c + d, n)
         send(pack(to), g_slot(me), g_send.at[to], g_recv.at[me], s, to)
         return v
+    lax.fori_loop(1, n, feed, 0)
+    send(d_slot(s), d_slot(s), d_far.at[0], d_recv.at[s], pc.far, c)
+    send(d_slot(s), d_slot(s), d_sib.at[s], d_recv.at[s], pc.sib, c)
+    xf = x_ref[...].astype(F32)
+    att_out[...] = (xf * inverse_rms(xf)).astype(BF)
+    kvs.stage1()
+    q0.stage1()
+    q1.stage1()
+    kvs.stage2()
     q2.stage1()
-    lax.fori_loop(1, n, feed, 0)
     q0.stage2()
     kvs.stage3()
     q1.stage2()
@@ -470,7 +482,7 @@
     send(pack(c), g_slot(me), g_own.at[0], g_recv.at[me], pc.far, c)
     send(pack(c), g_slot(me), g_own.at[1], g_recv.at[me], pc.sib, c)
     kvs.stage4()
-    lc[4].wait()
+    lc[3].wait()
     tc, ts = tab_v[0], tab_v[1]
     xh = att_out[...]
     def bias_of(tile):
@@ -573,7 +585,6 @@
             arrived(g_slot(i), g_recv.at[i], pc)
             return v
         lax.fori_loop(0, n, come, 0)
-    lc[3].wait()
     tall, chunk = 2 * rows, gu_v.shape[2]
     def forward(j):
         pair = slice(2 * j, 2 * j + 2)
@@ -686,7 +697,7 @@
     cring.finish()
     for d in range(1, deep): sent(own_kv, kz_s.at[d], pc)
     for d in range(deep): sent(own_kv, kx_s.at[d], pc)
-    sent(down, d_far.at[0], pc)
+    sent(d_slot(0), d_far.at[0], pc)
     def left(t, v):
         sent(g_slot(0), g_sib.at[pc.far * n + t], pc)
         @pl.when(t > 0)
@@ -696,13 +707,13 @@
             sent(g_slot(0), g_sib.at[s * n + src], pc)
         return v
     lax.fori_loop(0, n, left, 0)
-    sent(down, d_sib.at[s], pc)
-    sent(down, d_sib.at[pc.far], pc)
+    sent(d_slot(0), d_sib.at[s], pc)
+    sent(d_slot(0), d_sib.at[pc.far], pc)
 
 def layer_call(n, length, x, og, qkv, gain_one, bias, gate, up, gain_two, down, outw, tables):
     N, m = 4 * n, n // 2
     rows, width = x.shape
-    owned, piece = qkv.shape[0], down.shape[0]
+    owned, piece = qkv.shape[0], -(-down.shape[0] // 32) * 32
     chunk = 4 * piece
     S, V = jax.ShapeDtypeStruct, pltpu.VMEM
     joint = QDIM + 2 * KVDIM + HEAD
@@ -786,9 +797,9 @@
         for d in range(1, self.pc.n // 2):
             sent(self.r2.at[0], self.ss.at[self.i, 2 + d], self.pc)
 
-def backward_kernel(n, length_ref, x_ref, og_ref, mid_ref, u_ref, o_ref, att_ref, q_ref, kv_ref, qkv_ref, out_ref, gate_ref, up_ref, gain_ref, tables, half_sum,
-                    y_out, dx_out, dout_out, dqkv_out, dgate_out, dup_out, dgain_out,
-                    tab_v, gm_v, gb_v, dm_v, gp_v, p_v, gs_v, dkv_v, kx, kz, raw_v, r1_v, mine_v, *rest):
+def backward_kernel(n, length_ref, x_ref, og_ref, mid_ref, u_ref, o_ref, att_ref, q_ref, kv_ref, out_ref, gate_ref, up_ref, qw_ref, gain_ref, gain_one_ref, qkv_all, tables, half_sum,
+                    y_out, dx_out, dout_out, dqkv_out, dbias_out, dgate_out, dup_out, dgain_out, dgain_one_out,
+                    tab_v, gm_v, gb_v, dm_v, gp_v, p_v, gs_v, dkv_v, kx, kz, raw_v, r1_v, mine_v, dx_v, qkv_v, *rest):
     pieces = 6
     bufs, (local, kxs, kxr, kzs, kzr, gss, grs, fs, fr, ss, rs) = rest[: 5 * pieces], rest[5 * pieces :]
     pc = Place(n)
@@ -804,6 +815,8 @@
     y = s // 2
     mine = pltpu.make_async_copy(half_sum.at[:, y], mine_v, local.at[1])
     mine.start()
+    weights = pltpu.make_async_copy(qkv_all, qkv_v, local.at[2])
+    weights.start()
     enter(pc)
     owned = out_ref.shape[1]
     def cross(a):
@@ -935,31 +948,42 @@
     red[5].stage1()
     qk = QDIM + 2 * KVDIM
     gp = gp_v[...]
+    weights.wait()
     def back(j, w):
-        weight = qkv_ref[pl.ds(j * 8, 8), :, :qk].reshape(8 * owned, qk)
+        weight = qkv_v[pl.ds(j * 8, 8), :, :qk].reshape(8 * owned, qk)
         cols = pl.ds(pl.multiple_of(j * 8 * owned, 8 * owned), 8 * owned)
-        dx_out[:, cols] = contract_cols(gp, weight)
+        dx_v[:, cols] = contract_cols(gp, weight)
         return w
     lax.fori_loop(0, owners // 8, back, 0)
     red[2].stage3(); red[3].stage3(); red[4].stage3()
     red[5].stage2()
     fed(0)
     place_back(raw_v, 0, dgate_out)
-    dx_out[...] = gm_v[...] + rms_back(x_ref[...].astype(F32), inverse, dx_out[...])
+    dx_out[...] = (gm_v[...] + rms_back(x_ref[...].astype(F32), inverse, dx_v[...])).astype(BF)
     for i in range(2):
         dout_out[:, i * (width // 2) : (i + 1) * (width // 2)] = red[i].stage4()
     red[5].stage3()
     fed(1)
     place_back(raw_v, 1, dup_out)
-    gain = gain_ref[...]
-    dgain_out[...] = jnp.sum(
+    gain = column(gain_ref[...])
+    dgain_out[...] = as_row(jnp.sum(
         dgate_out[...] * gate_ref[...].astype(F32) + dup_out[...] * up_ref[...].astype(F32), axis=1, keepdims=True
-    )
+    ))
     dgate_out[...] = dgate_out[...] * gain
     dup_out[...] = dup_out[...] * gain
+    gain_one = column(gain_one_ref[...])
+    rows_sum = jnp.zeros((owned, 1), F32)
     for i in range(3):
-        dqkv_out[:, i * third : (i + 1) * third] = red[2 + i].stage4()
-    dqkv_out[:, QDIM:] = red[5].stage4()
+        cols = slice(i * third, (i + 1) * third)
+        raw = red[2 + i].stage4()
+        rows_sum = rows_sum + jnp.sum(raw * qw_ref[:, cols].astype(F32), axis=1, keepdims=True)
+        dqkv_out[:, cols] = raw * gain_one
+    raw = red[5].stage4()
+    dbias_out[...] = raw[:8, 2 * KVDIM :]
+    raw = raw[:, : 2 * KVDIM]
+    rows_sum = rows_sum + jnp.sum(raw * qw_ref[:, QDIM:].astype(F32), axis=1, keepdims=True)
+    dqkv_out[:, QDIM:] = raw * gain_one
+    dgain_one_out[...] = as_row(rows_sum)
     for r in red: r.finish()
     for a in range(2):
         sent(r1_v.at[a], fs.at[a], pc)
@@ -972,7 +996,7 @@
         sent(kx.at[:, :, lanes], kxs.at[g], pc)
         for d in range(1, n // 2): sent(kx.at[0, :, lanes], kzs.at[g, d], pc)
 
-def backward_call(n, length, x, og, mid, u, o, att, q, kv, qkv_all, out_all, gate, up, gain, tables, half_sum):
+def backward_call(n, length, x, og, mid, u, o, att, q, kv, out_all, gate, up, qkv, gain, gain_one, qkv_all, tables, half_sum):
     S, V = jax.ShapeDtypeStruct, pltpu.VMEM
     rows, width = x.shape
     owned = qkv_all.shape[1]
@@ -982,20 +1006,21 @@
     scratch = [V((2, rows, HEAD), F32), V((rows, width), F32), V((rows, width), BF), V((HEADS, rows, HEAD), BF),
                V((rows, QDIM + 2 * KVDIM), BF), V((GROUP * rows, n * rows), BF), V((GROUP * rows, n * rows), BF),
                V((m, 2, rows, 2 * KVDIM), BF), V((m, rows, 2 * KVDIM), BF), V((m, rows, 2 * KVDIM), BF),
-               V((n, 2, owned, half_sum.shape[-1]), BF), V((2,) + half_sum.shape[2:], BF), V((2,) + half_sum.shape[2:], BF)]
+               V((n, 2, owned, half_sum.shape[-1]), BF), V((2,) + half_sum.shape[2:], BF), V((2,) + half_sum.shape[2:], BF),
+               V((rows, width), F32), V(qkv_all.shape, BF)]
     for i, w in enumerate((width // 2, width // 2, QDIM // 3, QDIM // 3, QDIM // 3, 2 * KVDIM + HEAD)):
         one = (m, 2, owned, w) if i % 2 == 0 else (2, m, owned, w)
         scratch += [V((2, 2, m, 2, owned, w), BF), V((2, m, 2, owned, w), BF), V(one, BF), V((m, owned, w), BF), V((m, owned, w), BF)]
-    scratch += [DMA((2,)), DMA((2,)), DMA((2,)), DMA((2, m)), DMA((2, m)), DMA((2, n)), DMA((2, n)), DMA((2,)), DMA((2,)), DMA((6, 2 + m)), DMA((6, 2 + m))]
+    scratch += [DMA((3,)), DMA((2,)), DMA((2,)), DMA((2, m)), DMA((2, m)), DMA((2, n)), DMA((2, n)), DMA((2,)), DMA((2,)), DMA((6, 2 + m)), DMA((6, 2 + m))]
     return pl.pallas_call(
         functools.partial(backward_kernel, n),
-        out_shape=[S((rows, width), BF), S((rows, width), F32), S((owned, width), F32), S((owned, qkv_all.shape[2]), F32),
-                   S(gate.shape, F32), S(gate.shape, F32), S((owned, 1), F32)],
-        in_specs=[pl.BlockSpec(memory_space=pltpu.SMEM)] + [vmem] * 13 + [anys] * 2,
-        out_specs=[vmem] * 7,
+        out_shape=[S((rows, width), BF), S((rows, width), BF), S((owned, width), F32), S(qkv.shape, F32), S((8, HEAD), F32),
+                   S(gate.shape, F32), S(gate.shape, F32), S((1, owned), F32), S((1, owned), F32)],
+        in_specs=[pl.BlockSpec(memory_space=pltpu.SMEM)] + [vmem] * 14 + [anys] * 3,
+        out_specs=[vmem] * 9,
         scratch_shapes=scratch,
         compiler_params=pltpu.CompilerParams(collective_id=2, has_side_effects=True, vmem_limit_bytes=62 * 2**20),
-    )(length, x, og, mid, u, o, att, q, kv, qkv_all, out_all, gate, up, gain, tables, half_sum)
+    )(length, x, og, mid, u, o, att, q, kv, out_all, gate, up, qkv, gain, gain_one, qkv_all, tables, half_sum)
 
 
 def kernel_shards(
@@ -1015,42 +1040,36 @@
     rows, width = tokens.shape[1:]
     owned = gate_weight.shape[0]
     piece = down_weight.shape[0]
-    padded = -(-piece // 32) * 32
     owners = seqs * parts
     me = lax.axis_index("seq") * parts + lax.axis_index("ctx")
-    gain_one = attn_gain.astype(F32)[:, None]
-    gain_two = mlp_gain.astype(F32)[:, None]
+    gain_one, gain_two = attn_gain[None], mlp_gain[None]
     half = HEAD // 2
     frequency = np.float32(ROPE_BASE) ** (-np.arange(half, dtype=np.float32) * np.float32(2.0 / HEAD))
     angles = np.arange(rows * parts, dtype=np.float32)[:, None] * frequency.astype(np.float32)[None, :]
     cosine, sine = np.cos(angles), np.sin(angles)
     tables = jnp.asarray(np.stack([np.concatenate([cosine, cosine], 1), np.concatenate([-sine, sine], 1)]), F32)
-    down = jnp.pad(down_weight, ((0, padded - piece), (0, 0)))
     x, og = tokens[0], out_grad[0]
     qkv_all, out_all, kv_all, q, half_sum, grad_down, att, mid, u, o = layer_call(
         parts, lengths, x, og, qkv_weight, gain_one, qkv_bias[None], gate_weight, up_weight, gain_two,
-        down, out_weight, tables,
+        down_weight, out_weight, tables,
     )
     joint = qkv_all.shape[-1]
-    output, grad_inputs, grad_out, raw_qkv, grad_gate, grad_up, grad_mlp_gain = backward_call(
+    output, grad_inputs, grad_out, grad_qkv, bias_rows, grad_gate, grad_up, grad_mlp_gain, grad_attn_gain = backward_call(
         parts, lengths, x, og, mid, u, o, att, q, kv_all.reshape(parts, rows, 2 * KVDIM),
-        qkv_all.reshape(owners, owned, joint), out_all.reshape(owners, owned, width),
-        gate_weight, up_weight, gain_two, tables, half_sum,
+        out_all.reshape(owners, owned, width), gate_weight, up_weight, qkv_weight, gain_two, gain_one,
+        qkv_all.reshape(owners, owned, joint), tables, half_sum,
     )
-    qk = QDIM + 2 * KVDIM
-    bias_rows, raw_qkv = raw_qkv[:3, qk:], raw_qkv[:, :qk]
-    grad_attn_gain = jnp.sum(raw_qkv * qkv_weight.astype(F32), axis=1)
     per, per_value = (QDIM + KVDIM) // owners, KVDIM // owners
     grad_qk_bias = lax.dynamic_slice_in_dim(bias_rows[:2].reshape(2 * HEAD), lax.rem(per * me, HEAD), per)
     grad_value_bias = lax.dynamic_slice_in_dim(bias_rows[2], lax.rem(per_value * me, HEAD), per_value)
     return (
         output[None],
-        grad_inputs.astype(BF)[None],
-        grad_attn_gain,
-        raw_qkv * gain_one,
+        grad_inputs[None],
+        grad_attn_gain[0],
+        grad_qkv,
         grad_qk_bias,
         grad_out,
-        grad_mlp_gain[:, 0],
+        grad_mlp_gain[0],
         grad_gate,
         grad_up,
         grad_down[:piece].astype(F32),

time: 394 us -> 383 us (0.972)
  other arithmetic: 7.84 us -> 1.4 us
  Pallas kernels: 369 us -> 365 us
where the time goes in v5:
time: 383 us; the launch traced here: 378 us
  Pallas kernels  365 us (95%)
  local copies, waits for them, and re-layouts  9.89 us (3%)
    pallas_call x1, Pallas kernels, layer_call(): pl.pallas_call(functools.partial(layer_kernel, n), out_shape=shapes, in_s...  250 us
    pallas_call x1, Pallas kernels, backward_call(): pl.pallas_call(functools.partial(backward_kernel, n), out_shape=[S((rows,...  115 us

profile of v5, /device:TPU:0, one launch (start us, length us, event | category | flops | bytes accessed | tf_op | source)
XLA Modules:
  0.0 378.2 jit_solution(10616757026442690032)
XLA Ops:
  1.3 250.5 %shard_map.203 = (bf16[2,2,4,2,48,2176]{5,4,3,2,1,0:T(8,128)(2,1)}, bf16[2,2,4,2,48,1536]{5,4,3,2,1,0:T(8,128)(2,1)}, bf16[4,2,128,512]{3,2,1,0:T(8,128)(2,1)}, ...) custom-call(s32[1]{0:T(128)S(6)} %copy.31.length_ref, ...), custom_call_target="tpu_custom_call" | custom-call | tf_op jit(solution)/shard_map/pallas_call | solution.py:738
  251.8 0.0 copy-start.2
  251.8 114.9 %shard_map.204 = (bf16[128,1536]{1,0:T(8,128)(2,1)}, bf16[128,1536]{1,0:T(8,128)(2,1)}, f32[48,1536]{1,0:T(8,128)}, f32[48,2048]{1,0:T(8,128)}, f32[8,128]{1,0:T...) custom-call(s32[1]{0:T(128)S(6)} %copy.31.length_ref, ...), custom_call_target="tpu_custom_call" | custom-call | tf_op jit(solution)/shard_map/pallas_call | solution.py:1015
  366.7 0.0 copy-start.5
  366.7 0.0 copy-start.4
  366.7 0.8 slice_bitcast_fusion
  367.5 0.6 dynamic_slice.8
  368.1 0.7 slice.11
  368.8 0.6 dynamic-slice_bitcast_fusion
  369.3 0.0 copy-done.2
  369.3 1.4 slice_convert_fusion
  370.7 0.0 copy-done.5
  370.8 0.7 copy.32
  371.5 0.0 copy-done.4
  371.5 0.7 copy.33
  372.3 0.0 copy-done.8
  372.3 0.5 copy.34
  372.8 0.0 copy-done.3
  372.8 0.7 copy.35
  373.5 0.7 copy.36
  374.2 0.5 copy.37
  374.8 1.2 copy.38
  375.9 0.9 copy-done
  376.8 1.2 copy.39
  (9 shorter events, 0.0 us)
Async XLA Ops:
  251.8 117.6 %copy-start.2 = (bf16[288,1536]{1,0:T(8,128)(2,1)S(1)}, bf16[288,1536]{1,0:T(8,128)(2,1)}, u32[]{:S(2)}) copy-start(bf16[288,1536]{1,0:T(8,128)(2,1)} %get-tuple-element.48) | copy-start | bytes 2654212
  366.7 4.0 %copy-start.5 = (bf16[128,1536]{1,0:T(8,128)(2,1)S(1)}, bf16[128,1536]{1,0:T(8,128)(2,1)}, u32[]{:S(2)}) copy-start(bf16[128,1536]{1,0:T(8,128)(2,1)} %get-tuple-element.39) | copy-start | bytes 1179652
  366.7 4.8 %copy-start.4 = (bf16[128,1536]{1,0:T(8,128)(2,1)S(1)}, bf16[128,1536]{1,0:T(8,128)(2,1)}, u32[]{:S(2)}) copy-start(bf16[128,1536]{1,0:T(8,128)(2,1)} %get-tuple-element.40) | copy-start | bytes 1179652
  369.3 2.9 copy-start.8
  369.3 3.4 copy-start.3
  370.7 2.8 copy-start.6
  370.7 3.5 copy-start.7
  370.7 4.0 %copy-start.1 = (f32[48,8960]{1,0:T(8,128)S(1)}, f32[48,8960]{1,0:T(8,128)}, u32[]{:S(2)}) copy-start(f32[48,8960]{1,0:T(8,128)} %get-tuple-element.67) | copy-start | bytes 5160964
  374.8 2.1 copy-start

commit v6 on v5

--- a/solution.py
+++ b/solution.py
@@ -461,6 +461,8 @@
         send(pack(to), g_slot(me), g_send.at[to], g_recv.at[me], s, to)
         return v
     lax.fori_loop(1, n, feed, 0)
+    send(pack(c), g_slot(me), g_own.at[0], g_recv.at[me], pc.far, c)
+    send(pack(c), g_slot(me), g_own.at[1], g_recv.at[me], pc.sib, c)
     send(d_slot(s), d_slot(s), d_far.at[0], d_recv.at[s], pc.far, c)
     send(d_slot(s), d_slot(s), d_sib.at[s], d_recv.at[s], pc.sib, c)
     xf = x_ref[...].astype(F32)
@@ -479,8 +481,7 @@
     q0.stage3()
     q1.stage3()
     q2.stage3()
-    send(pack(c), g_slot(me), g_own.at[0], g_recv.at[me], pc.far, c)
-    send(pack(c), g_slot(me), g_own.at[1], g_recv.at[me], pc.sib, c)
+    gu_turn(1); gu_turn(2)
     kvs.stage4()
     lc[3].wait()
     tc, ts = tab_v[0], tab_v[1]
@@ -531,11 +532,10 @@
             val = kv_v[:, :, :, pl.ds(pl.multiple_of(KVDIM + col, HEAD), HEAD)].reshape(total, HEAD)
             scores = jnp.where(allowed, contract_cols(q_v[h], key) * SCALE, MASKED)
             e = jnp.exp(scores - jnp.max(scores, axis=1, keepdims=True))
-            probs = (e / jnp.sum(e, axis=1, keepdims=True)).astype(BF)
+            probs = (e * (1.0 / jnp.sum(e, axis=1, keepdims=True))).astype(BF)
             att_out[:, pl.ds(pl.multiple_of(h * HEAD, HEAD), HEAD)] = product(probs, val).astype(BF)
             return v
         lax.fori_loop(first, first + count, head, 0)
-    gu_turn(1); gu_turn(2)
     o0.stage3(); o1.stage3(); o2.stage3()
     heads(0, GROUP)
     gu_turn(3); gu_turn(4)
@@ -668,6 +668,7 @@
     compute(down_pieces[2])
     backward(1)
     uring.turn(2)
+    oring.turn(1)
     add_core(down_pieces[2])
     compute(down_pieces[3])
     backward(0)
@@ -676,12 +677,11 @@
     for i, p in enumerate(wide_pieces):
         compute(p)
         if i: add_core(wide_pieces[i - 1])
-        if i == 0: oring.turn(1)
         if i == 3: uring.turn(4)
-        if i == 4: oring.turn(2)
+        if i == 1: oring.turn(2)
+        if i == 5: oring.turn(3)
     add_core(wide_pieces[-1])
     for p in down_pieces: add_far(p)
-    oring.turn(3)
     oring.turn(4)
     for kind, j, a in wide_pieces + down_pieces:
         cols = cols_of(j)
@@ -800,7 +800,7 @@
 def backward_kernel(n, length_ref, x_ref, og_ref, mid_ref, u_ref, o_ref, att_ref, q_ref, kv_ref, out_ref, gate_ref, up_ref, qw_ref, gain_ref, gain_one_ref, qkv_all, tables, half_sum,
                     y_out, dx_out, dout_out, dqkv_out, dbias_out, dgate_out, dup_out, dgain_out, dgain_one_out,
                     tab_v, gm_v, gb_v, dm_v, gp_v, p_v, gs_v, dkv_v, kx, kz, raw_v, r1_v, mine_v, dx_v, qkv_v, *rest):
-    pieces = 6
+    pieces = 7
     bufs, (local, kxs, kxr, kzs, kzr, gss, grs, fs, fr, ss, rs) = rest[: 5 * pieces], rest[5 * pieces :]
     pc = Place(n)
     s, c = pc.s, pc.c
@@ -875,7 +875,7 @@
             part = pl.ds(pl.multiple_of(i * rows, rows), rows)
             scores = jnp.where(allowed, contract_cols(q_ref[h], key) * SCALE, MASKED)
             e = jnp.exp(scores - jnp.max(scores, axis=1, keepdims=True))
-            probs = e / jnp.sum(e, axis=1, keepdims=True)
+            probs = e * (1.0 / jnp.sum(e, axis=1, keepdims=True))
             gprobs = contract_cols(dm_v[h], val)
             inner = jnp.sum(probs * gprobs, axis=1, keepdims=True)
             gs = (probs * (gprobs - inner)).astype(BF)
@@ -931,7 +931,9 @@
     red[2].stage1(); red[3].stage1(); red[4].stage1()
     feed(1)
     kv_z(0); kv_z(1)
-    joint(5, QDIM, 2 * KVDIM)
+    joint(5, QDIM, KVDIM)
+    joint(6, QDIM + KVDIM, KVDIM)
+    red[6].stage0()
     sums = jnp.sum(gp_v[...].astype(F32), axis=0, keepdims=True)
     p5 = red[5].p
     qk_width = QDIM + KVDIM
@@ -942,10 +944,10 @@
         for k, t in enumerate(tiles):
             part = jnp.where(at == k, sums[:, t * HEAD : t * HEAD + HEAD], part)
         plane = d // n
-        p5[plane // 2, plane % 2, d % n // 2, d % 2, :, 2 * KVDIM :] = part.astype(BF)
+        p5[plane // 2, plane % 2, d % n // 2, d % 2, :, KVDIM:] = part.astype(BF)
     red[5].stage0()
     red[2].stage2(); red[3].stage2(); red[4].stage2()
-    red[5].stage1()
+    red[6].stage1(); red[5].stage1()
     qk = QDIM + 2 * KVDIM
     gp = gp_v[...]
     weights.wait()
@@ -956,13 +958,13 @@
         return w
     lax.fori_loop(0, owners // 8, back, 0)
     red[2].stage3(); red[3].stage3(); red[4].stage3()
-    red[5].stage2()
+    red[6].stage2(); red[5].stage2()
     fed(0)
     place_back(raw_v, 0, dgate_out)
     dx_out[...] = (gm_v[...] + rms_back(x_ref[...].astype(F32), inverse, dx_v[...])).astype(BF)
     for i in range(2):
         dout_out[:, i * (width // 2) : (i + 1) * (width // 2)] = red[i].stage4()
-    red[5].stage3()
+    red[6].stage3(); red[5].stage3()
     fed(1)
     place_back(raw_v, 1, dup_out)
     gain = column(gain_ref[...])
@@ -978,11 +980,13 @@
         raw = red[2 + i].stage4()
         rows_sum = rows_sum + jnp.sum(raw * qw_ref[:, cols].astype(F32), axis=1, keepdims=True)
         dqkv_out[:, cols] = raw * gain_one
-    raw = red[5].stage4()
-    dbias_out[...] = raw[:8, 2 * KVDIM :]
-    raw = raw[:, : 2 * KVDIM]
-    rows_sum = rows_sum + jnp.sum(raw * qw_ref[:, QDIM:].astype(F32), axis=1, keepdims=True)
-    dqkv_out[:, QDIM:] = raw * gain_one
+    for i, first in ((6, QDIM + KVDIM), (5, QDIM)):
+        cols = slice(first, first + KVDIM)
+        whole = red[i].stage4()
+        raw = whole[:, :KVDIM]
+        rows_sum = rows_sum + jnp.sum(raw * qw_ref[:, cols].astype(F32), axis=1, keepdims=True)
+        dqkv_out[:, cols] = raw * gain_one
+    dbias_out[...] = whole[:8, KVDIM:]
     dgain_one_out[...] = as_row(rows_sum)
     for r in red: r.finish()
     for a in range(2):
@@ -1008,10 +1012,10 @@
                V((m, 2, rows, 2 * KVDIM), BF), V((m, rows, 2 * KVDIM), BF), V((m, rows, 2 * KVDIM), BF),
                V((n, 2, owned, half_sum.shape[-1]), BF), V((2,) + half_sum.shape[2:], BF), V((2,) + half_sum.shape[2:], BF),
                V((rows, width), F32), V(qkv_all.shape, BF)]
-    for i, w in enumerate((width // 2, width // 2, QDIM // 3, QDIM // 3, QDIM // 3, 2 * KVDIM + HEAD)):
+    for i, w in enumerate((width // 2, width // 2, QDIM // 3, QDIM // 3, QDIM // 3, KVDIM + HEAD, KVDIM)):
         one = (m, 2, owned, w) if i % 2 == 0 else (2, m, owned, w)
         scratch += [V((2, 2, m, 2, owned, w), BF), V((2, m, 2, owned, w), BF), V(one, BF), V((m, owned, w), BF), V((m, owned, w), BF)]
-    scratch += [DMA((3,)), DMA((2,)), DMA((2,)), DMA((2, m)), DMA((2, m)), DMA((2, n)), DMA((2, n)), DMA((2,)), DMA((2,)), DMA((6, 2 + m)), DMA((6, 2 + m))]
+    scratch += [DMA((3,)), DMA((2,)), DMA((2,)), DMA((2, m)), DMA((2, m)), DMA((2, n)), DMA((2, n)), DMA((2,)), DMA((2,)), DMA((7, 2 + m)), DMA((7, 2 + m))]
     return pl.pallas_call(
         functools.partial(backward_kernel, n),
         out_shape=[S((rows, width), BF), S((rows, width), BF), S((owned, width), F32), S(qkv.shape, F32), S((8, HEAD), F32),

time: 383 us -> 379 us (0.990)
  Pallas kernels: 365 us -> 361 us
where the time goes in v6:
time: 379 us; the launch traced here: 374 us
  Pallas kernels  361 us (95%)
  local copies, waits for them, and re-layouts  9.89 us (3%)
    pallas_call x1, Pallas kernels, layer_call(): pl.pallas_call(functools.partial(layer_kernel, n), out_shape=shapes, in_s...  249 us
    pallas_call x1, Pallas kernels, backward_call(): pl.pallas_call(functools.partial(backward_kernel, n), out_shape=[S((rows,...  112 us

profile of v6, /device:TPU:0, one launch (start us, length us, event | category | flops | bytes accessed | tf_op | source)
XLA Modules:
  0.0 373.9 jit_solution(362083475339515253)
XLA Ops:
  1.3 249.0 %shard_map.203 = (bf16[2,2,4,2,48,2176]{5,4,3,2,1,0:T(8,128)(2,1)}, bf16[2,2,4,2,48,1536]{5,4,3,2,1,0:T(8,128)(2,1)}, bf16[4,2,128,512]{3,2,1,0:T(8,128)(2,1)}, ...) custom-call(s32[1]{0:T(128)S(6)} %copy.31.length_ref, ...), custom_call_target="tpu_custom_call" | custom-call | tf_op jit(solution)/shard_map/pallas_call | solution.py:738
  250.3 0.0 copy-start.2
  250.3 112.1 %shard_map.204 = (bf16[128,1536]{1,0:T(8,128)(2,1)}, bf16[128,1536]{1,0:T(8,128)(2,1)}, f32[48,1536]{1,0:T(8,128)}, f32[48,2048]{1,0:T(8,128)}, f32[8,128]{1,0:T...) custom-call(s32[1]{0:T(128)S(6)} %copy.31.length_ref, ...), custom_call_target="tpu_custom_call" | custom-call | tf_op jit(solution)/shard_map/pallas_call | solution.py:1019
  362.4 0.0 copy-start.5
  362.4 0.0 copy-start.4
  362.4 0.8 slice_bitcast_fusion
  363.1 0.6 dynamic_slice.8
  363.7 0.7 slice.11
  364.4 0.6 dynamic-slice_bitcast_fusion
  365.0 0.0 copy-done.2
  365.0 1.4 slice_convert_fusion
  366.4 0.0 copy-done.5
  366.4 0.7 copy.32
  367.2 0.0 copy-done.4
  367.2 0.7 copy.33
  367.9 0.0 copy-done.8
  367.9 0.5 copy.34
  368.4 0.0 copy-done.3
  368.4 0.7 copy.35
  369.2 0.7 copy.36
  369.9 0.5 copy.37
  370.4 1.2 copy.38
  371.6 0.9 copy-done
  372.5 1.2 copy.39
  (9 shorter events, 0.0 us)
Async XLA Ops:
  250.3 114.7 %copy-start.2 = (bf16[288,1536]{1,0:T(8,128)(2,1)S(1)}, bf16[288,1536]{1,0:T(8,128)(2,1)}, u32[]{:S(2)}) copy-start(bf16[288,1536]{1,0:T(8,128)(2,1)} %get-tuple-element.48) | copy-start | bytes 2654212
  362.4 4.0 %copy-start.5 = (bf16[128,1536]{1,0:T(8,128)(2,1)S(1)}, bf16[128,1536]{1,0:T(8,128)(2,1)}, u32[]{:S(2)}) copy-start(bf16[128,1536]{1,0:T(8,128)(2,1)} %get-tuple-element.39) | copy-start | bytes 1179652
  362.4 4.8 %copy-start.4 = (bf16[128,1536]{1,0:T(8,128)(2,1)S(1)}, bf16[128,1536]{1,0:T(8,128)(2,1)}, u32[]{:S(2)}) copy-start(bf16[128,1536]{1,0:T(8,128)(2,1)} %get-tuple-element.40) | copy-start | bytes 1179652
  365.0 2.9 copy-start.8
  365.0 3.4 copy-start.3
  366.4 2.8 copy-start.6
  366.4 3.5 copy-start.7
  366.4 4.0 %copy-start.1 = (f32[48,8960]{1,0:T(8,128)S(1)}, f32[48,8960]{1,0:T(8,128)}, u32[]{:S(2)}) copy-start(f32[48,8960]{1,0:T(8,128)} %get-tuple-element.67) | copy-start | bytes 5160964
  370.4 2.1 copy-start

commit v7 on v6

--- a/solution.py
+++ b/solution.py
@@ -223,7 +223,7 @@
 def sent(src, ssem, place):
     pltpu.make_async_remote_copy(src, src, ssem, ssem, device_id=(place.s, place.c), device_id_type=MESH).wait_send()
 
-def enter(place, whole_group=True):
+def greet_all(place):
     barrier = pltpu.get_barrier_semaphore()
     def greet(d, z):
         pl.semaphore_signal(barrier, inc=1, device_id=(place.s, lax.rem(place.c + d, place.n)), device_id_type=MESH)
@@ -231,7 +231,10 @@
     lax.fori_loop(1, place.n, greet, 0)
     pl.semaphore_signal(barrier, inc=1, device_id=(place.sib, place.c), device_id_type=MESH)
     pl.semaphore_signal(barrier, inc=1, device_id=(place.far, place.c), device_id_type=MESH)
-    pl.semaphore_wait(barrier, place.n + 1)
+
+def enter(place):
+    greet_all(place)
+    pl.semaphore_wait(pltpu.get_barrier_semaphore(), place.n + 1)
 
 
 def add_low(left, right):
@@ -397,6 +400,7 @@
                  local, save, ss, rs, g_recv, g_send, g_own, g_far, g_sib, d_recv, d_far, d_sib, c_recv, c_send,
                  kz_s, kz_r, kx_s, kx_r, n_recv, n_send, u_recv, u_send, o_recv_, o_send_, gs0, gr0, gsave, ds0, dr0, ds1, dr1, dsave):
     pc = Place(n)
+    greet_all(pc)
     me, s, c = pc.me, pc.s, pc.c
     y, x, z, xp = s // 2, lax.rem(c, 2), c // 2, c + 1 - 2 * lax.rem(c, 2)
     rows, width = x_ref.shape
@@ -447,7 +451,7 @@
     short = down[...].astype(F32)
     padding = jnp.zeros((piece - short.shape[0], width), F32)
     down_v[pl.ds(pl.multiple_of(s * piece, piece), piece), :] = jnp.concatenate([short, padding], 0).astype(BF)
-    enter(pc)
+    pl.semaphore_wait(pltpu.get_barrier_semaphore(), n + 1)
     def gu_turn(t):
         k = s * n + lax.rem(c + n - t, n)
         arrived(g_slot(k), g_recv.at[k], pc)
@@ -849,12 +853,12 @@
     y_out[...] = jnp.where(live, mid + o_ref[...], 0.0).astype(BF)
     owners = 4 * n
     def mix(j, w):
-        weight = out_ref[pl.ds(j * 8, 8)].reshape(8 * owned, width)
+        weight = out_ref[pl.ds(j * 16, 16)].reshape(16 * owned, width)
         r = contract_cols(gb_v[...], weight).astype(BF)
-        for k in range(8 * owned // HEAD):
-            dm_v[j * (8 * owned // HEAD) + k] = r[:, k * HEAD : (k + 1) * HEAD]
+        for k in range(16 * owned // HEAD):
+            dm_v[j * (16 * owned // HEAD) + k] = r[:, k * HEAD : (k + 1) * HEAD]
         return w
-    lax.fori_loop(0, owners // 8, mix, 0)
+    lax.fori_loop(0, owners // 16, mix, 0)
     gb = gb_v[...]
     for i in range(2):
         w = width // 2
@@ -952,11 +956,11 @@
     gp = gp_v[...]
     weights.wait()
     def back(j, w):
-        weight = qkv_v[pl.ds(j * 8, 8), :, :qk].reshape(8 * owned, qk)
-        cols = pl.ds(pl.multiple_of(j * 8 * owned, 8 * owned), 8 * owned)
+        weight = qkv_v[pl.ds(j * 16, 16), :, :qk].reshape(16 * owned, qk)
+        cols = pl.ds(pl.multiple_of(j * 16 * owned, 16 * owned), 16 * owned)
         dx_v[:, cols] = contract_cols(gp, weight)
         return w
-    lax.fori_loop(0, owners // 8, back, 0)
+    lax.fori_loop(0, owners // 16, back, 0)
     red[2].stage3(); red[3].stage3(); red[4].stage3()
     red[6].stage2(); red[5].stage2()
     fed(0)

time: 379 us -> 377 us (level)
  no operation moved by 1% of the time
where the time goes in v7:
time: 377 us; the launch traced here: 373 us
  Pallas kernels  360 us (95%)
  local copies, waits for them, and re-layouts  9.89 us (3%)
    pallas_call x1, Pallas kernels, layer_call(): pl.pallas_call(functools.partial(layer_kernel, n), out_shape=shapes, in_s...  248 us
    pallas_call x1, Pallas kernels, backward_call(): pl.pallas_call(functools.partial(backward_kernel, n), out_shape=[S((rows,...  112 us

profile of v7, /device:TPU:0, one launch (start us, length us, event | category | flops | bytes accessed | tf_op | source)
XLA Modules:
  0.0 373.0 jit_solution(3525364079711826335)
XLA Ops:
  1.3 247.7 %shard_map.203 = (bf16[2,2,4,2,48,2176]{5,4,3,2,1,0:T(8,128)(2,1)}, bf16[2,2,4,2,48,1536]{5,4,3,2,1,0:T(8,128)(2,1)}, bf16[4,2,128,512]{3,2,1,0:T(8,128)(2,1)}, ...) custom-call(s32[1]{0:T(128)S(6)} %copy.31.length_ref, ...), custom_call_target="tpu_custom_call" | custom-call | tf_op jit(solution)/shard_map/pallas_call | solution.py:742
  249.0 0.0 copy-start.2
  249.0 112.5 %shard_map.204 = (bf16[128,1536]{1,0:T(8,128)(2,1)}, bf16[128,1536]{1,0:T(8,128)(2,1)}, f32[48,1536]{1,0:T(8,128)}, f32[48,2048]{1,0:T(8,128)}, f32[8,128]{1,0:T...) custom-call(s32[1]{0:T(128)S(6)} %copy.31.length_ref, ...), custom_call_target="tpu_custom_call" | custom-call | tf_op jit(solution)/shard_map/pallas_call | solution.py:1023
  361.5 0.0 copy-start.5
  361.5 0.0 copy-start.4
  361.5 0.8 slice_bitcast_fusion
  362.2 0.6 dynamic_slice.8
  362.8 0.7 slice.11
  363.5 0.6 dynamic-slice_bitcast_fusion
  364.1 0.0 copy-done.2
  364.1 1.4 slice_convert_fusion
  365.5 0.0 copy-done.5
  365.5 0.7 copy.32
  366.3 0.0 copy-done.4
  366.3 0.7 copy.33
  367.0 0.0 copy-done.8
  367.0 0.5 copy.34
  367.5 0.0 copy-done.3
  367.5 0.7 copy.35
  368.3 0.7 copy.36
  369.0 0.5 copy.37
  369.5 1.2 copy.38
  370.7 0.9 copy-done
  371.6 1.2 copy.39
  (9 shorter events, 0.0 us)
Async XLA Ops:
  249.0 115.1 %copy-start.2 = (bf16[288,1536]{1,0:T(8,128)(2,1)S(1)}, bf16[288,1536]{1,0:T(8,128)(2,1)}, u32[]{:S(2)}) copy-start(bf16[288,1536]{1,0:T(8,128)(2,1)} %get-tuple-element.48) | copy-start | bytes 2654212
  361.5 4.0 %copy-start.5 = (bf16[128,1536]{1,0:T(8,128)(2,1)S(1)}, bf16[128,1536]{1,0:T(8,128)(2,1)}, u32[]{:S(2)}) copy-start(bf16[128,1536]{1,0:T(8,128)(2,1)} %get-tuple-element.39) | copy-start | bytes 1179652
  361.5 4.8 %copy-start.4 = (bf16[128,1536]{1,0:T(8,128)(2,1)S(1)}, bf16[128,1536]{1,0:T(8,128)(2,1)}, u32[]{:S(2)}) copy-start(bf16[128,1536]{1,0:T(8,128)(2,1)} %get-tuple-element.40) | copy-start | bytes 1179652
  364.1 2.9 copy-start.8
  364.1 3.4 copy-start.3
  365.5 2.8 copy-start.6
  365.5 3.5 copy-start.7
  365.5 4.0 %copy-start.1 = (f32[48,8960]{1,0:T(8,128)S(1)}, f32[48,8960]{1,0:T(8,128)}, u32[]{:S(2)}) copy-start(f32[48,8960]{1,0:T(8,128)} %get-tuple-element.67) | copy-start | bytes 5160964
  369.5 2.1 copy-start
